TPU v7x, 256 devices: a whole 4x4x8 slice. The times are simulated.
256 devices in a mesh: dp: 16 (over y, x), shard: 16 (over z, core).
Axes of the slice: x: 4, y: 4, z: 8, core: 2. Of those that a mesh axis runs over, the one named last changes fastest.
Arguments:
- grad_parts: bfloat16 [16, 16, 1792, 1792], P('dp', None, 'shard'), may hold values from -5 to 5
- moment: bfloat16 [16, 1792, 1792], P('dp', 'shard'), may hold values from -6 to 6
- second: float32 [16, 1792, 1792], P('dp', 'shard'), may hold values from 0.1 to 10
- left_basis: bfloat16 [16, 1792, 1792], P('dp', 'shard'), may hold values from -0.125 to 0.125
- right_basis: bfloat16 [16, 1792, 1792], P('dp', 'shard'), may hold values from -0.125 to 0.125
- block_steps: int32 [16], P('dp'), may hold values from 1 to 40
Outputs:
- moment_new: bfloat16 [16, 1792, 1792], P('dp', 'shard')
- second_new: float32 [16, 1792, 1792], P('dp', 'shard')
- update: bfloat16 [16, 1792, 1792], P('dp', 'shard')
All inputs are finite; a program needn't handle non-finite values.
Results may differ from a plain program's by a relative error of at most 0.017.
Values may be sent and summed in bfloat16 or wider, within the bound.
No kernel may reach another device: no remote copies, remote signals or barrier semaphores. Data moves between devices by JAX's collectives and lax.ppermute only.
A program may use at most 128 MiB of HBM per device.

v0:
```python
import jax
import jax.numpy as jnp
from jax import lax
from jax.sharding import PartitionSpec as P

beta_one = 0.8
beta_two = 0.95
epsilon = 1e-08


def local(grad_parts, moment, second, left_basis, right_basis, block_steps):
    left_full, right_full = (
        lax.all_gather(left_basis[0], "shard", axis=0, tiled=True),
        lax.all_gather(right_basis[0], "shard", axis=0, tiled=True),
    )
    summed = lax.psum_scatter(grad_parts[0], "dp", scatter_dimension=0, tiled=True).astype(
        jnp.float32
    )
    gradient = summed[0].astype(jnp.bfloat16)
    moment_new = (
        beta_one * moment[0].astype(jnp.float32) + (1.0 - beta_one) * gradient.astype(jnp.float32)
    ).astype(jnp.bfloat16)
    grad_cols, mom_cols = (
        lax.all_to_all(gradient, "shard", split_axis=1, concat_axis=0, tiled=True),
        lax.all_to_all(moment_new, "shard", split_axis=1, concat_axis=0, tiled=True),
    )
    left_grad = jnp.einsum(
        "ki,kc->ic", left_full, grad_cols, preferred_element_type=jnp.float32
    ).astype(jnp.bfloat16)
    left_mom = jnp.einsum(
        "ki,kc->ic", left_full, mom_cols, preferred_element_type=jnp.float32
    ).astype(jnp.bfloat16)
    grad_rows, mom_rows = (
        lax.all_to_all(left_grad, "shard", split_axis=0, concat_axis=1, tiled=True),
        lax.all_to_all(left_mom, "shard", split_axis=0, concat_axis=1, tiled=True),
    )
    left_pair = jnp.stack([grad_rows, mom_rows])
    rotated = jnp.einsum("nrk,kc->nrc", left_pair, right_full, preferred_element_type=jnp.float32)
    rot_grad = rotated[0]
    rot_mom = rotated[1]
    second_new = beta_two * second[0] + (1.0 - beta_two) * rot_grad * rot_grad
    steps_float = block_steps[0].astype(jnp.float32)
    first_fix = 1.0 - jnp.power(jnp.float32(beta_one), steps_float)
    second_fix = 1.0 - jnp.power(jnp.float32(beta_two), steps_float)
    direction = (rot_mom / first_fix / (jnp.sqrt(second_new / second_fix) + epsilon)).astype(
        jnp.bfloat16
    )
    back = jnp.einsum(
        "rc,kc->rk", direction, right_full, preferred_element_type=jnp.float32
    ).astype(jnp.bfloat16)
    back_cols = lax.all_to_all(back, "shard", split_axis=1, concat_axis=0, tiled=True)
    update_cols = jnp.dot(left_full, back_cols, preferred_element_type=jnp.float32).astype(
        jnp.bfloat16
    )
    update = lax.all_to_all(update_cols, "shard", split_axis=0, concat_axis=1, tiled=True)
    return (moment_new[None], second_new[None], update[None])


def solution(mesh):
    return jax.shard_map(
        local,
        mesh=mesh,
        in_specs=(
            P("dp", None, "shard", None),
            P("dp", "shard", None),
            P("dp", "shard", None),
            P("dp", "shard", None),
            P("dp", "shard", None),
            P("dp"),
        ),
        out_specs=(P("dp", "shard", None), P("dp", "shard", None), P("dp", "shard", None)),
        check_vma=False,
    )
```

profile of v0, /device:TPU:1, one launch (start us, length us, event | category | flops | bytes accessed | tf_op | source)
XLA Modules:
  0.0 249.9 jit_solution(12319372799956456485)
XLA Ops:
  9.9 92.2 %reduce-scatter.4.cloned.1.call-done = bf16[1,112,1792]{2,1,0:T(8,128)(2,1)} async-done(((bf16[16,112,1792]{2,1,0:T(8,128)(2,1)}), bf16[1,112,1792]{2,1,0:T(8,128)(2,1)}) %reduce-scatter.4.cloned.1.call-update) | async-done | bytes 401424
  102.1 1.9 convert_multiply_fusion
  104.3 2.0 copy.36
  106.3 1.2 add_convert_fusion
  107.5 24.5 %all_to_all.99 = bf16[112,16,112]{0,2,1:T(8,128)(2,1)S(1)} all-to-all(bf16[112,16,112]{0,2,1:T(8,128)(2,1)S(1)} %add_convert_fusion), channel_id=1, replica_groups=mesh['dp'=16,'shard'=16] {'shard'}, dimensions={1} | all-to-all | bytes 802816 | tf_op jit(solution)/shard_map/all_to_all | solution.py:25
  132.0 3.5 %all-to-all-start = ((bf16[112,16,112]{0,2,1:T(8,128)(2,1)}), bf16[112,16,112]{0,2,1:T(8,128)(2,1)S(1)}, u32[]{:S(2)}, u32[]{:S(2)}) async-start(bf16[112,16,112]{0,2,1:T(8,128)(2,1)} %bitcast.23), calls=%async_computation | async-start | bytes 917504 | tf_op jit(solution)/shard_map/all_to_all | solution.py:24
  136.2 3.9 %fusion.25 = bf16[1792,112]{0,1:T(8,128)(2,1)S(1)} fusion(bf16[1792,112]{0,1:T(8,128)(2,1)S(1)} %all_to_all.82, bf16[1,1792,1792]{2,1,0:T(8,128)(2,1)} %all-gather.5.cloned.1.call-done), kind=kOutput, calls=%fused_computation.15 | convolution fusion | flops 719523840 | bytes 7225344 | tf_op jit(solution)/shard_map/ki,kc->ic/dot_general | solution.py:30
  140.8 0.9 copy.26
  141.8 9.1 %all-to-all-done = bf16[112,16,112]{0,2,1:T(8,128)(2,1)S(1)} async-done(((bf16[112,16,112]{0,2,1:T(8,128)(2,1)}), bf16[112,16,112]{0,2,1:T(8,128)(2,1)S(1)}, u32[]{:S(2)}, u32[]{:S(2)}) %all-to-all-start) | async-done | bytes 401440 | tf_op jit(solution)/shard_map/all_to_all | solution.py:24
  150.8 3.5 %all-to-all-start.3 = ((bf16[16,112,112]{1,2,0:T(8,128)(2,1)}), bf16[16,112,112]{1,2,0:T(8,128)(2,1)S(1)}, u32[]{:S(2)}, u32[]{:S(2)}) async-start(bf16[16,112,112]{1,2,0:T(8,128)(2,1)} %copy.26), calls=%async_computation.3 | async-start | bytes 917504 | tf_op jit(solution)/shard_map/all_to_all | solution.py:35
  154.9 3.9 %fusion.10 = bf16[1792,112]{0,1:T(8,128)(2,1)S(1)} fusion(bf16[1792,112]{0,1:T(8,128)(2,1)S(1)} %all_to_all.76, bf16[1,1792,1792]{2,1,0:T(8,128)(2,1)} %all-gather.5.cloned.1.call-done), kind=kOutput, calls=%fused_computation.10 | convolution fusion | flops 719523840 | bytes 7225344 | tf_op jit(solution)/shard_map/ki,kc->ic/dot_general | solution.py:27
  159.6 0.9 copy.21
  160.5 9.1 %all-to-all-done.3 = bf16[16,112,112]{1,2,0:T(8,128)(2,1)S(1)} async-done(((bf16[16,112,112]{1,2,0:T(8,128)(2,1)}), bf16[16,112,112]{1,2,0:T(8,128)(2,1)S(1)}, u32[]{:S(2)}, u32[]{:S(2)}) %all-to-all-start.3) | async-done | bytes 401440 | tf_op jit(solution)/shard_map/all_to_all | solution.py:35
  169.6 3.5 %all-to-all-start.1 = ((bf16[16,112,112]{1,2,0:T(8,128)(2,1)}), bf16[16,112,112]{1,2,0:T(8,128)(2,1)S(1)}, u32[]{:S(2)}, u32[]{:S(2)}) async-start(bf16[16,112,112]{1,2,0:T(8,128)(2,1)} %copy.21), calls=%async_computation.1 | async-start | bytes 917504 | tf_op jit(solution)/shard_map/all_to_all | solution.py:34
  174.1 14.4 %all-to-all-done.1 = bf16[16,112,112]{1,2,0:T(8,128)(2,1)S(1)} async-done(((bf16[16,112,112]{1,2,0:T(8,128)(2,1)}), bf16[16,112,112]{1,2,0:T(8,128)(2,1)S(1)}, u32[]{:S(2)}, u32[]{:S(2)}) %all-to-all-start.1) | async-done | bytes 401440 | tf_op jit(solution)/shard_map/all_to_all | solution.py:34
  188.7 4.6 %fusion = f32[2,112,1792]{2,1,0:T(8,128)S(1)} fusion(bf16[1,1792,1792]{2,1,0:T(8,128)(2,1)} %all-gather.7.cloned.1.call-done, bf16[1,112,1792]{2,1,0:T(8,128)(2,1)S(1)} %copy.34, bf16[1,112,1792]{2,1,0:T(8,128)(2,1)S(1)} %copy.32), kind=kOutput, calls=%fused_computation | convolution fusion | flops 1439047680 | bytes 8830976 | tf_op jit(solution)/shard_map/nrk,kc->nrc/dot_general | solution.py:38
  193.3 1.1 copy-done.1
  194.5 2.0 fusion.19
  196.8 18.7 %all_to_all.100 = bf16[112,16,112]{0,2,1:T(8,128)(2,1)S(1)} all-to-all(bf16[112,16,112]{0,2,1:T(8,128)(2,1)S(1)} %bitcast.88), channel_id=1, replica_groups=mesh['dp'=16,'shard'=16] {'shard'}, dimensions={1} | all-to-all | bytes 802816 | tf_op jit(solution)/shard_map/all_to_all | solution.py:51
  216.1 4.9 %fusion.22 = bf16[1792,112]{0,1:T(8,128)(2,1)S(1)} fusion(bf16[1792,112]{0,1:T(8,128)(2,1)S(1)} %all_to_all.89, bf16[1,1792,1792]{2,1,0:T(8,128)(2,1)} %all-gather.5.cloned.1.call-done), kind=kOutput, calls=%fused_computation.14 | convolution fusion | flops 719523840 | bytes 7225344 | tf_op jit(solution)/shard_map/dot_general | solution.py:52
  222.7 3.5 %all-to-all-start.5 = ((bf16[16,112,112]{1,2,0:T(8,128)(2,1)}), bf16[16,112,112]{1,2,0:T(8,128)(2,1)S(1)}, u32[]{:S(2)}, u32[]{:S(2)}) async-start(bf16[16,112,112]{1,2,0:T(8,128)(2,1)} %copy.30), calls=%async_computation.5 | async-start | bytes 917504 | tf_op jit(solution)/shard_map/all_to_all | solution.py:55
  226.1 2.1 fusion.28
  228.3 13.2 %all-to-all-done.5 = bf16[16,112,112]{1,2,0:T(8,128)(2,1)S(1)} async-done(((bf16[16,112,112]{1,2,0:T(8,128)(2,1)}), bf16[16,112,112]{1,2,0:T(8,128)(2,1)S(1)}, u32[]{:S(2)}, u32[]{:S(2)}) %all-to-all-start.5) | async-done | bytes 401440 | tf_op jit(solution)/shard_map/all_to_all | solution.py:55
  241.5 1.0 copy.31
  (29 shorter events, 8.0 us)
Async XLA Ops:
  8.0 94.1 %copy-start.2 = (bf16[1,112,1792]{2,1,0:T(8,128)(2,1)S(1)}, bf16[1,112,1792]{2,1,0:T(8,128)(2,1)}, u32[]{:S(2)}) copy-start(bf16[1,112,1792]{2,1,0:T(8,128)(2,1)} %param.7) | copy-start | bytes 1204228
  8.0 94.1 %reduce-scatter.4.cloned.1.call-start = ((), (), s32[]{:S(2)}) async-start(), calls=%async_computation.9 | async-start | bytes 6823936
  8.7 127.4 %all-gather.5.cloned.1.call-start = ((), (), s32[]{:S(2)}) async-start(), calls=%async_computation.7 | async-start | bytes 6823936 | tf_op jit(solution)/shard_map/all_gather | solution.py:13
  9.3 179.4 %all-gather.7.cloned.1.call-start = ((), (), s32[]{:S(2)}) async-start(), calls=%async_computation.8 | async-start | bytes 6823936 | tf_op jit(solution)/shard_map/all_gather | solution.py:14
  132.0 18.8 %all-to-all-start = ((bf16[112,16,112]{0,2,1:T(8,128)(2,1)}), bf16[112,16,112]{0,2,1:T(8,128)(2,1)S(1)}, u32[]{:S(2)}, u32[]{:S(2)}) async-start(bf16[112,16,112]{0,2,1:T(8,128)(2,1)} %bitcast.23), calls=%async_computation | async-start | bytes 917504 | tf_op jit(solution)/shard_map/all_to_all | solution.py:24
  150.8 18.8 %all-to-all-start.3 = ((bf16[16,112,112]{1,2,0:T(8,128)(2,1)}), bf16[16,112,112]{1,2,0:T(8,128)(2,1)S(1)}, u32[]{:S(2)}, u32[]{:S(2)}) async-start(bf16[16,112,112]{1,2,0:T(8,128)(2,1)} %copy.26), calls=%async_computation.3 | async-start | bytes 917504 | tf_op jit(solution)/shard_map/all_to_all | solution.py:35
  169.6 18.8 %all-to-all-start.1 = ((bf16[16,112,112]{1,2,0:T(8,128)(2,1)}), bf16[16,112,112]{1,2,0:T(8,128)(2,1)S(1)}, u32[]{:S(2)}, u32[]{:S(2)}) async-start(bf16[16,112,112]{1,2,0:T(8,128)(2,1)} %copy.21), calls=%async_computation.1 | async-start | bytes 917504 | tf_op jit(solution)/shard_map/all_to_all | solution.py:34
  188.6 5.8 %copy-start = (f32[1,112,1792]{2,1,0:T(8,128)S(1)}, f32[1,112,1792]{2,1,0:T(8,128)}, u32[]{:S(2)}) copy-start(f32[1,112,1792]{2,1,0:T(8,128)} %param.8) | copy-start | bytes 2408452
  188.7 5.8 %copy-start.3 = (bf16[1,1792,1792]{2,1,0:T(8,128)(2,1)S(1)}, bf16[1,1792,1792]{2,1,0:T(8,128)(2,1)}, u32[]{:S(2)}) copy-start(bf16[1,1792,1792]{2,1,0:T(8,128)(2,1)} %all-gather.7.cloned.1.call-done) | copy-start | bytes 19267588
  193.3 1.1 copy-start.1
  222.7 18.8 %all-to-all-start.5 = ((bf16[16,112,112]{1,2,0:T(8,128)(2,1)}), bf16[16,112,112]{1,2,0:T(8,128)(2,1)S(1)}, u32[]{:S(2)}, u32[]{:S(2)}) async-start(bf16[16,112,112]{1,2,0:T(8,128)(2,1)} %copy.30), calls=%async_computation.5 | async-start | bytes 917504 | tf_op jit(solution)/shard_map/all_to_all | solution.py:55
Sparse Core Ops, SparseCore 0:
  12.6 89.5 reduce-scatter.3
Sparse Core Ops, SparseCore 1:
  11.2 50.8 all-gather.4
  63.9 45.2 all-gather.6
where the time goes:
time: 251 us; the launch traced here: 250 us
  waiting for transfers between devices  140 us (56%)
  blocking collectives  43.2 us (17%)
  matrix products  19.3 us (8%)
  between operations  16.4 us (7%)
  starting transfers between devices  14 us (6%)
  local copies, waits for them, and re-layouts  12 us (5%)
  other arithmetic  5.21 us (2%)
    unnamed x4, waiting for transfers between devices  94 us
    all_to_all x1, blocking collectives, local(): lax.all_to_all(moment_new, 'shard', split_axis=1, concat_axis=0, tiled=True)  24.5 us
    all_to_all x1, blocking collectives, local(): lax.all_to_all(back, 'shard', split_axis=1, concat_axis=0, tiled=True)  18.7 us
    all_to_all x1, waiting for transfers between devices, local(): lax.all_to_all(left_grad, 'shard', split_axis=0, concat_axis=1, tiled=True)  14.4 us
    all_to_all x1, waiting for transfers between devices, local(): lax.all_to_all(update_cols, 'shard', split_axis=0, concat_axis=1, tiled=T...  13.2 us
    all_to_all x1, waiting for transfers between devices, local(): lax.all_to_all(left_mom, 'shard', split_axis=0, concat_axis=1, tiled=True)  9.11 us
    all_to_all x1, waiting for transfers between devices, local(): lax.all_to_all(gradient, 'shard', split_axis=1, concat_axis=0, tiled=True)  9.07 us
  transfers between devices with their start and end apart: 7, of which 5 were waited for; matrix products, arithmetic and copies ran while one was open for 7% of the time, Pallas kernels for 0%

commit v1 on v0

v1 whole, which is shorter than its diff:
```python
import jax
import jax.numpy as jnp
from jax import lax
from jax.sharding import PartitionSpec as P

beta_one = 0.8
beta_two = 0.95
epsilon = 1e-08
f32, bf16 = jnp.float32, jnp.bfloat16
SIDE = 4
TOGETHER = 56


def swaps(axis, mask):
    if axis:
        return [(y * SIDE + x, y * SIDE + (x ^ mask)) for y in range(SIDE) for x in range(SIDE)]
    return [(y * SIDE + x, (y ^ mask) * SIDE + x) for y in range(SIDE) for x in range(SIDE)]


def halving(values, at, order):
    spot = list(at)
    for axis in order:

        def own(mask, axis=axis, values=values):
            return lax.dynamic_index_in_dim(values, spot[axis] ^ mask, axis=axis, keepdims=True).astype(f32)

        away = jnp.concatenate([own(1), own(2)], axis=axis).astype(bf16)
        got = lax.ppermute(away, "dp", swaps(axis, 1)).astype(f32)
        first, second = jnp.split(got, 2, axis=axis)
        across = lax.ppermute((own(3) + second).astype(bf16), "dp", swaps(axis, 3))
        values = own(0) + first + across.astype(f32)
        spot[axis] = 0
    return values[0, 0]


def reduce_blocks(parts):
    rows, columns = parts.shape[1:]
    me = lax.axis_index("dp")
    at = (me // SIDE, me % SIDE)
    upper = lax.psum_scatter(parts[:, :TOGETHER], "dp", scatter_dimension=0, tiled=True)[0]
    grid = parts.reshape(SIDE, SIDE, rows, columns)[:, :, TOGETHER:]
    left = halving(grid[..., : columns // 2], at, (1, 0))
    right = halving(grid[..., columns // 2 :], at, (0, 1))
    lower = jnp.concatenate([left, right], axis=1).astype(bf16)
    return jnp.concatenate([upper, lower], axis=0)


def to_cols(rows):
    return lax.all_to_all(rows, "shard", split_axis=rows.ndim - 1, concat_axis=rows.ndim - 2, tiled=True)


def to_rows(cols):
    return lax.all_to_all(cols, "shard", split_axis=cols.ndim - 2, concat_axis=cols.ndim - 1, tiled=True)


def local(grad_parts, moment, second, left_basis, right_basis, block_steps):
    right_full = lax.all_gather(right_basis[0], "shard", axis=0, tiled=True)
    left_full = lax.all_gather(left_basis[0], "shard", axis=0, tiled=True)
    gradient = reduce_blocks(grad_parts[0])
    second_cols = to_cols(second[0].astype(bf16))
    gradient, second_cols = lax.optimization_barrier((gradient, second_cols))
    moment_new = (beta_one * moment[0].astype(f32) + (1.0 - beta_one) * gradient.astype(f32)).astype(bf16)

    pair = jnp.stack([gradient, moment_new])
    pair_right = jnp.einsum("nrk,kc->nrc", pair, right_full, preferred_element_type=f32).astype(bf16)
    pair_cols = to_cols(pair_right)
    rot_grad, rot_mom = jnp.einsum("ki,nkc->nic", left_full, pair_cols, preferred_element_type=f32)

    second_new_cols = beta_two * second_cols.astype(f32) + (1.0 - beta_two) * rot_grad * rot_grad
    steps_float = block_steps[0].astype(f32)
    first_fix = 1.0 - jnp.power(f32(beta_one), steps_float)
    second_fix = 1.0 - jnp.power(f32(beta_two), steps_float)
    direction = (rot_mom / first_fix / (jnp.sqrt(second_new_cols / second_fix) + epsilon)).astype(bf16)
    left_dir = jnp.dot(left_full, direction, preferred_element_type=f32).astype(bf16)

    rot_grad_rows, left_dir_rows = to_rows(jnp.stack([rot_grad.astype(bf16), left_dir]))
    rot_grad_rows = rot_grad_rows.astype(f32)
    second_new = beta_two * second[0] + (1.0 - beta_two) * rot_grad_rows * rot_grad_rows
    update = jnp.einsum("rc,kc->rk", left_dir_rows, right_full, preferred_element_type=f32).astype(bf16)
    return (moment_new[None], second_new[None], update[None])


def solution(mesh):
    return jax.shard_map(
        local,
        mesh=mesh,
        in_specs=(
            P("dp", None, "shard", None),
            P("dp", "shard", None),
            P("dp", "shard", None),
            P("dp", "shard", None),
            P("dp", "shard", None),
            P("dp"),
        ),
        out_specs=(P("dp", "shard", None), P("dp", "shard", None), P("dp", "shard", None)),
        check_vma=False,
    )
```

time: 251 us -> 199 us (0.79)
  waiting for transfers between devices: 140 us -> 72.9 us
  starting transfers between devices: 14 us -> 32.9 us
  blocking collectives: 43.2 us -> 28.9 us
  local copies, waits for them, and re-layouts: 12 us -> 20.3 us
  other arithmetic: 5.21 us -> 10.2 us
    unnamed x4, waiting for transfers between devices: 94 us -> 16.9 us
    ppermute x0 -> x8, waiting for transfers between devices: none -> 22.4 us  [the longest x4 14.3 us: halving(): across = lax.ppermute((own(3) + second).astype(bf16), 'dp', swaps(axis, 3))]
    all_to_all x2 -> x1, blocking collectives: 43.2 us -> 28.9 us  [to_rows(): lax.all_to_all(cols, 'shard', split_axis=cols.ndim - 2, concat_axis=cols....]
    ppermute x0 -> x8, starting transfers between devices: none -> 14.1 us  [the longest x4 9.94 us: halving(): across = lax.ppermute((own(3) + second).astype(bf16), 'dp', swaps(axis, 3))]
    all_to_all x4 -> x2, waiting for transfers between devices: 45.7 us -> 33.5 us  [to_cols(): lax.all_to_all(rows, 'shard', split_axis=rows.ndim - 1, concat_axis=rows....]
    slice x0 -> x2, local copies, waits for them, and re-layouts: none -> 5.96 us  [the longest x1 3.77 us: reduce_blocks(): parts[:, :TOGETHER]]
    all_to_all x4 -> x2, starting transfers between devices: 13.8 us -> 18.7 us  [to_cols(): lax.all_to_all(rows, 'shard', split_axis=rows.ndim - 1, concat_axis=rows....]
    convert_element_type x1 -> x9, other arithmetic: 1.16 us -> 4.54 us  [the longest x4 2.77 us: halving(): got = lax.ppermute(away, 'dp', swaps(axis, 1)).astype(f32)]
  transfers between devices with their start and end apart: 7 -> 13, of which waited for: 5 -> 7; matrix products, arithmetic and copies ran while one was open for 7% -> 11% of each run, Pallas kernels for 0% -> 0%
where the time goes in v1:
time: 199 us
  waiting for transfers between devices  72.9 us (37%)
  starting transfers between devices  32.9 us (17%)
  blocking collectives  28.9 us (15%)
  local copies, waits for them, and re-layouts  20.3 us (10%)
  matrix products  17 us (9%)
  between operations  16.5 us (8%)
  other arithmetic  10.2 us (5%)
    all_to_all x2, waiting for transfers between devices, to_cols(): lax.all_to_all(rows, 'shard', split_axis=rows.ndim - 1, concat_axis=rows....  33.5 us
    all_to_all x1, blocking collectives, to_rows(): lax.all_to_all(cols, 'shard', split_axis=cols.ndim - 2, concat_axis=cols....  28.9 us
    all_to_all x2, starting transfers between devices, to_cols(): lax.all_to_all(rows, 'shard', split_axis=rows.ndim - 1, concat_axis=rows....  18.7 us
    unnamed x4, waiting for transfers between devices  16.9 us
    ppermute x4, waiting for transfers between devices, halving(): across = lax.ppermute((own(3) + second).astype(bf16), 'dp', swaps(axis, 3))  14.3 us
    ppermute x4, starting transfers between devices, halving(): across = lax.ppermute((own(3) + second).astype(bf16), 'dp', swaps(axis, 3))  9.94 us
    ppermute x4, waiting for transfers between devices, halving(): got = lax.ppermute(away, 'dp', swaps(axis, 1)).astype(f32)  8.09 us
    dot_general x1, matrix products, local(): jnp.einsum('rc,kc->rk', left_dir_rows, right_full, preferred_element_type...  5.67 us
  transfers between devices with their start and end apart: 13, of which 7 were waited for; matrix products, arithmetic and copies ran while one was open for 11% of the time, Pallas kernels for 0%

profile of v1, /device:TPU:1, one launch (start us, length us, event | category | flops | bytes accessed | tf_op | source)
XLA Modules:
  0.0 198.6 jit_solution(12540229361720293355)
XLA Ops:
  8.0 3.8 %slice.17 = bf16[16,56,1792]{2,1,0:T(8,128)(2,1)} slice(bf16[16,112,1792]{2,1,0:T(8,128)(2,1)} %bitcast.85), slice={[0:16], [0:56], [0:1792]} | slice | bytes 6422528 | tf_op jit(solution)/shard_map/slice | solution.py:40
  13.0 2.2 %fusion.61 = (bf16[4,4,56,896]{3,2,1,0:T(8,128)(2,1)S(1)}, bf16[4,4,56,896]{3,2,1,0:T(8,128)(2,1)S(1)}) fusion(bf16[4,4,112,1792]{3,2,1,0:T(8,128)(2,1)} %bitcast.86), kind=kLoop, calls=%fused_computation.78 | loop fusion | bytes 6422528 | tf_op jit(solution)/shard_map/slice | solution.py:42
  16.3 2.1 %collective-permute-start.4 = (bf16[2,4,56,896]{3,2,1,0:T(8,128)(2,1)}, bf16[2,4,56,896]{3,2,1,0:T(8,128)(2,1)}, u32[]{:S(2)}, u32[]{:S(2)}) collective-permute-start(bf16[2,4,56,896]{3,2,1,0:T(8,128)(2,1)} %pad_maximum_fusion.1), channel_id=1, source_target_pairs={{0,64},{16,80},{32,96},{48,112},{64,0},{80,16},{96,32},{112,48},{1... | collective-permute-start | bytes 2408456 | tf_op jit(solution)/shard_map/ppermute | solution.py:28
  21.5 2.0 copy.15
  23.5 9.7 %all-to-all-start = ((bf16[112,16,112]{0,2,1:T(8,128)(2,1)}), bf16[112,16,112]{0,2,1:T(8,128)(2,1)}, u32[]{:S(2)}, u32[]{:S(2)}) async-start(bf16[112,16,112]{0,2,1:T(8,128)(2,1)} %bitcast.91), calls=%async_computation | async-start | bytes 917504 | tf_op jit(solution)/shard_map/all_to_all | solution.py:49
  33.2 4.3 %collective-permute-done.4 = bf16[2,4,56,896]{3,2,1,0:T(8,128)(2,1)} collective-permute-done((bf16[2,4,56,896]{3,2,1,0:T(8,128)(2,1)}, bf16[2,4,56,896]{3,2,1,0:T(8,128)(2,1)}, u32[]{:S(2)}, u32[]{:S(2)}) %collective-permute-start.4) | collective-permute-done | bytes 802848 | tf_op jit(solution)/shard_map/ppermute | solution.py:28
  40.8 3.9 %collective-permute-start.5 = (bf16[1,4,56,896]{3,2,1,0:T(8,128)(2,1)}, bf16[1,4,56,896]{3,2,1,0:T(8,128)(2,1)}, u32[]{:S(2)}, u32[]{:S(2)}) collective-permute-start(bf16[1,4,56,896]{3,2,1,0:T(8,128)(2,1)} %fusion.33), channel_id=1, source_target_pairs={{0,192},{16,208},{32,224},{48,240},{64,128},{80,144},{96,160},{112... | collective-permute-start | bytes 1204232 | tf_op jit(solution)/shard_map/ppermute | solution.py:30
  44.7 9.0 %all-to-all-done = bf16[112,16,112]{0,2,1:T(8,128)(2,1)} async-done(((bf16[112,16,112]{0,2,1:T(8,128)(2,1)}), bf16[112,16,112]{0,2,1:T(8,128)(2,1)}, u32[]{:S(2)}, u32[]{:S(2)}) %all-to-all-start) | async-done | bytes 401440 | tf_op jit(solution)/shard_map/all_to_all | solution.py:49
  53.7 1.9 copy.16
  55.6 2.3 %all_to_all.38 = bf16[1792,112]{0,1:T(8,128)(2,1)} reshape(bf16[16,112,112]{1,0,2:T(8,128)(2,1)} %copy.16) | data formatting | bytes 802816 | tf_op jit(solution)/shard_map/all_to_all | solution.py:49
  62.8 11.8 %collective-permute-done.1 = bf16[4,1,56,896]{3,2,1,0:T(8,128)(2,1)S(1)} collective-permute-done((bf16[4,1,56,896]{3,2,1,0:T(8,128)(2,1)S(1)}, bf16[4,1,56,896]{3,2,1,0:T(8,128)(2,1)S(1)}, u32[]{:S(2)}, u32[]{:S(2)}) %collective-permute-start.1) | collective-permute-done | bytes 401440 | tf_op jit(solution)/shard_map/ppermute | solution.py:30
  75.3 2.0 %collective-permute-start.7 = (bf16[1,1,56,896]{3,2,1,0:T(8,128)(2,1)S(1)}, bf16[1,1,56,896]{3,2,1,0:T(8,128)(2,1)S(1)}, u32[]{:S(2)}, u32[]{:S(2)}) collective-permute-start(bf16[1,1,56,896]{3,2,1,0:T(8,128)(2,1)S(1)} %fusion.49), channel_id=1, source_target_pairs={{0,48},{16,32},{32,16},{48,0},{64,112},{80,96},{96,80},{112,64},{1... | collective-permute-start | bytes 301064 | tf_op jit(solution)/shard_map/ppermute | solution.py:30
  77.3 3.8 %collective-permute-done.2 = bf16[2,1,56,896]{3,2,1,0:T(8,128)(2,1)S(1)} collective-permute-done((bf16[2,1,56,896]{3,2,1,0:T(8,128)(2,1)S(1)}, bf16[2,1,56,896]{3,2,1,0:T(8,128)(2,1)S(1)}, u32[]{:S(2)}, u32[]{:S(2)}) %collective-permute-start.2) | collective-permute-done | bytes 200736 | tf_op jit(solution)/shard_map/ppermute | solution.py:28
  81.2 2.2 %collective-permute-start.3 = (bf16[1,1,56,896]{3,2,1,0:T(8,128)(2,1)S(1)}, bf16[1,1,56,896]{3,2,1,0:T(8,128)(2,1)S(1)}, u32[]{:S(2)}, u32[]{:S(2)}) collective-permute-start(bf16[1,1,56,896]{3,2,1,0:T(8,128)(2,1)S(1)} %fusion.52), channel_id=1, source_target_pairs={{0,192},{16,208},{32,224},{48,240},{64,128},{80,144},{96,160},{112... | collective-permute-start | bytes 301064 | tf_op jit(solution)/shard_map/ppermute | solution.py:30
  83.5 2.5 %collective-permute-done.3 = bf16[1,1,56,896]{3,2,1,0:T(8,128)(2,1)S(1)} collective-permute-done((bf16[1,1,56,896]{3,2,1,0:T(8,128)(2,1)S(1)}, bf16[1,1,56,896]{3,2,1,0:T(8,128)(2,1)S(1)}, u32[]{:S(2)}, u32[]{:S(2)}) %collective-permute-start.3) | collective-permute-done | bytes 100384 | tf_op jit(solution)/shard_map/ppermute | solution.py:30
  86.0 15.8 %reduce-scatter.4.cloned.1.call-done = bf16[1,56,1792]{2,1,0:T(8,128)(2,1)} async-done(((bf16[16,56,1792]{2,1,0:T(8,128)(2,1)}), bf16[1,56,1792]{2,1,0:T(8,128)(2,1)}) %reduce-scatter.4.cloned.1.call-update) | async-done | bytes 200720
  103.0 4.7 %fusion.11 = bf16[2,112,1792]{2,1,0:T(8,128)(2,1)S(1)} fusion(bf16[1,1792,1792]{2,1,0:T(8,128)(2,1)} %all-gather.5.cloned.1.call-done, bf16[1,112,1792]{2,1,0:T(8,128)(2,1)S(1)} %fusion.43, bf16[1,112,1792]{2,1,0:T(8,128)(2,1)S(1)} %bitcast.92), kind=kOutput, calls=%fused_computation.9 | convolution fusion | flops 1439449088 | bytes 8028160 | tf_op jit(solution)/shard_map/nrk,kc->nrc/dot_general | solution.py:65
  107.7 2.1 %copy.17 = bf16[2,112,1792]{1,0,2:T(2,128)(2,1)} copy(bf16[2,112,1792]{2,1,0:T(8,128)(2,1)S(1)} %fusion.11) | data formatting | bytes 1605632 | tf_op jit(solution)/shard_map/convert_element_type | solution.py:65
  109.8 9.0 %all-to-all-start.1 = ((bf16[2,112,1792]{1,0,2:T(2,128)(2,1)}), bf16[2,112,1792]{1,0,2:T(2,128)(2,1)S(1)}, u32[]{:S(2)}, u32[]{:S(2)}) async-start(bf16[2,112,1792]{1,0,2:T(2,128)(2,1)} %copy.17), calls=%async_computation.1 | async-start | bytes 1835008 | tf_op jit(solution)/shard_map/all_to_all | solution.py:49
  119.5 24.6 %all-to-all-done.1 = bf16[2,112,1792]{1,0,2:T(2,128)(2,1)S(1)} async-done(((bf16[2,112,1792]{1,0,2:T(2,128)(2,1)}), bf16[2,112,1792]{1,0,2:T(2,128)(2,1)S(1)}, u32[]{:S(2)}, u32[]{:S(2)}) %all-to-all-start.1) | async-done | bytes 802848 | tf_op jit(solution)/shard_map/all_to_all | solution.py:49
  145.5 4.6 %fusion.8 = f32[2,1792,112]{1,2,0:T(8,128)S(1)} fusion(bf16[2,1792,112]{1,2,0:T(8,128)(2,1)S(1)} %all_to_all.42, bf16[1,1792,1792]{2,1,0:T(8,128)(2,1)} %all-gather.7.cloned.1.call-done), kind=kOutput, calls=%fused_computation.8 | convolution fusion | flops 1438646272 | bytes 8830976 | tf_op jit(solution)/shard_map/ki,nkc->nic/dot_general | solution.py:67
  150.3 2.0 %fusion.20 = bf16[1,1792,112]{1,2,0:T(8,128)(2,1)S(1)} fusion(bf16[1,1792,1792]{2,1,0:T(8,128)(2,1)S(1)} %copy-done.7, bf16[1792,112]{0,1:T(8,128)(2,1)S(1)} %copy-done.6, f32[2,1792,112]{1,2,0:T(8,128)S(1)} %fusion.8, f32[]{:T(128)} %bitcast.20, f32[]{:T(128)} %bitcast.18), kind=kOutput, calls=%fused_computation.12 | convolution fusion | flops 721530880 | bytes 8830984 | tf_op jit(solution)/shard_map/dot_general | solution.py:74
  153.6 28.9 %all_to_all.49 = bf16[2,1792,112]{2,0,1:T(2,128)(2,1)S(1)} all-to-all(bf16[2,1792,112]{2,0,1:T(2,128)(2,1)S(1)} %copy.19), channel_id=1, replica_groups=mesh['dp'=16,'shard'=16] {'shard'}, dimensions={1} | all-to-all | bytes 1605632 | tf_op jit(solution)/shard_map/all_to_all | solution.py:53
  185.5 5.7 %fusion.23 = bf16[1,112,1792]{2,1,0:T(8,128)(2,1)} fusion(bf16[112,1792]{1,0:T(8,128)(2,1)S(1)} %unstack.28, bf16[1,1792,1792]{2,1,0:T(8,128)(2,1)} %all-gather.5.cloned.1.call-done), kind=kOutput, calls=%fused_computation.13 | convolution fusion | flops 719523840 | bytes 7225344 | tf_op jit(solution)/shard_map/rc,kc->rk/dot_general | solution.py:79
  (65 shorter events, 21.4 us)
Async XLA Ops:
  8.0 93.8 %reduce-scatter.4.cloned.1.call-start = ((), (), s32[]{:S(2)}) async-start(), calls=%async_computation.6 | async-start | bytes 3411968
  11.8 91.2 %all-gather.5.cloned.1.call-start = ((), (), s32[]{:S(2)}) async-start(), calls=%async_computation.4 | async-start | bytes 6823936 | tf_op jit(solution)/shard_map/all_gather | solution.py:57
  12.4 133.1 %all-gather.7.cloned.1.call-start = ((), (), s32[]{:S(2)}) async-start(), calls=%async_computation.5 | async-start | bytes 6823936 | tf_op jit(solution)/shard_map/all_gather | solution.py:58
  16.3 21.2 %collective-permute-start.4 = (bf16[2,4,56,896]{3,2,1,0:T(8,128)(2,1)}, bf16[2,4,56,896]{3,2,1,0:T(8,128)(2,1)}, u32[]{:S(2)}, u32[]{:S(2)}) collective-permute-start(bf16[2,4,56,896]{3,2,1,0:T(8,128)(2,1)} %pad_maximum_fusion.1), channel_id=1, source_target_pairs={{0,64},{16,80},{32,96},{48,112},{64,0},{80,16},{96,32},{112,48},{1... | collective-permute-start | bytes 2408456 | tf_op jit(solution)/shard_map/ppermute | solution.py:28
  18.4 2.3 %copy-start.2 = (f32[1,112,1792]{2,1,0:T(8,128)S(1)}, f32[1,112,1792]{2,1,0:T(8,128)}, u32[]{:S(2)}) copy-start(f32[1,112,1792]{2,1,0:T(8,128)} %param.8) | copy-start | bytes 2408452
  19.5 38.4 %collective-permute-start = (bf16[4,2,56,896]{3,2,1,0:T(8,128)(2,1)}, bf16[4,2,56,896]{3,2,1,0:T(8,128)(2,1)}, u32[]{:S(2)}, u32[]{:S(2)}) collective-permute-start(bf16[4,2,56,896]{3,2,1,0:T(8,128)(2,1)} %pad_maximum_fusion), channel_id=1, source_target_pairs={{0,16},{16,0},{32,48},{48,32},{64,80},{80,64},{96,112},{112,96},{1... | collective-permute-start | bytes 2408456 | tf_op jit(solution)/shard_map/ppermute | solution.py:28
  23.5 30.1 %all-to-all-start = ((bf16[112,16,112]{0,2,1:T(8,128)(2,1)}), bf16[112,16,112]{0,2,1:T(8,128)(2,1)}, u32[]{:S(2)}, u32[]{:S(2)}) async-start(bf16[112,16,112]{0,2,1:T(8,128)(2,1)} %bitcast.91), calls=%async_computation | async-start | bytes 917504 | tf_op jit(solution)/shard_map/all_to_all | solution.py:49
  38.8 1.2 copy-start
  40.8 20.4 %collective-permute-start.5 = (bf16[1,4,56,896]{3,2,1,0:T(8,128)(2,1)}, bf16[1,4,56,896]{3,2,1,0:T(8,128)(2,1)}, u32[]{:S(2)}, u32[]{:S(2)}) collective-permute-start(bf16[1,4,56,896]{3,2,1,0:T(8,128)(2,1)} %fusion.33), channel_id=1, source_target_pairs={{0,192},{16,208},{32,224},{48,240},{64,128},{80,144},{96,160},{112... | collective-permute-start | bytes 1204232 | tf_op jit(solution)/shard_map/ppermute | solution.py:30
  57.9 3.3 %copy-start.1 = (f32[2,4,56,896]{3,2,1,0:T(8,128)S(1)}, f32[2,4,56,896]{3,2,1,0:T(8,128)}, u32[]{:S(2)}) copy-start(f32[2,4,56,896]{3,2,1,0:T(8,128)} %copy-done) | copy-start | bytes 4816900
  59.4 15.2 %collective-permute-start.1 = (bf16[4,1,56,896]{3,2,1,0:T(8,128)(2,1)S(1)}, bf16[4,1,56,896]{3,2,1,0:T(8,128)(2,1)S(1)}, u32[]{:S(2)}, u32[]{:S(2)}) collective-permute-start(bf16[4,1,56,896]{3,2,1,0:T(8,128)(2,1)S(1)} %fusion.35), channel_id=1, source_target_pairs={{0,48},{16,32},{32,16},{48,0},{64,112},{80,96},{96,80},{112,64},{1... | collective-permute-start | bytes 1204232 | tf_op jit(solution)/shard_map/ppermute | solution.py:30
  62.5 12.8 %collective-permute-start.6 = (bf16[1,2,56,896]{3,2,1,0:T(8,128)(2,1)S(1)}, bf16[1,2,56,896]{3,2,1,0:T(8,128)(2,1)S(1)}, u32[]{:S(2)}, u32[]{:S(2)}) collective-permute-start(bf16[1,2,56,896]{3,2,1,0:T(8,128)(2,1)S(1)} %pad_maximum_fusion.4), channel_id=1, source_target_pairs={{0,16},{16,0},{32,48},{48,32},{64,80},{80,64},{96,112},{112,96},{1... | collective-permute-start | bytes 602120 | tf_op jit(solution)/shard_map/ppermute | solution.py:28
  74.8 6.3 %collective-permute-start.2 = (bf16[2,1,56,896]{3,2,1,0:T(8,128)(2,1)S(1)}, bf16[2,1,56,896]{3,2,1,0:T(8,128)(2,1)S(1)}, u32[]{:S(2)}, u32[]{:S(2)}) collective-permute-start(bf16[2,1,56,896]{3,2,1,0:T(8,128)(2,1)S(1)} %pad_maximum_fusion.3), channel_id=1, source_target_pairs={{0,64},{16,80},{32,96},{48,112},{64,0},{80,16},{96,32},{112,48},{1... | collective-permute-start | bytes 602120 | tf_op jit(solution)/shard_map/ppermute | solution.py:28
  75.3 27.5 %copy-start.4 = (bf16[1,112,1792]{2,1,0:T(8,128)(2,1)S(1)}, bf16[1,112,1792]{2,1,0:T(8,128)(2,1)}, u32[]{:S(2)}) copy-start(bf16[1,112,1792]{2,1,0:T(8,128)(2,1)} %param.7) | copy-start | bytes 1204228
  75.3 8.1 %collective-permute-start.7 = (bf16[1,1,56,896]{3,2,1,0:T(8,128)(2,1)S(1)}, bf16[1,1,56,896]{3,2,1,0:T(8,128)(2,1)S(1)}, u32[]{:S(2)}, u32[]{:S(2)}) collective-permute-start(bf16[1,1,56,896]{3,2,1,0:T(8,128)(2,1)S(1)} %fusion.49), channel_id=1, source_target_pairs={{0,48},{16,32},{32,16},{48,0},{64,112},{80,96},{96,80},{112,64},{1... | collective-permute-start | bytes 301064 | tf_op jit(solution)/shard_map/ppermute | solution.py:30
  81.2 4.8 %collective-permute-start.3 = (bf16[1,1,56,896]{3,2,1,0:T(8,128)(2,1)S(1)}, bf16[1,1,56,896]{3,2,1,0:T(8,128)(2,1)S(1)}, u32[]{:S(2)}, u32[]{:S(2)}) collective-permute-start(bf16[1,1,56,896]{3,2,1,0:T(8,128)(2,1)S(1)} %fusion.52), channel_id=1, source_target_pairs={{0,192},{16,208},{32,224},{48,240},{64,128},{80,144},{96,160},{112... | collective-permute-start | bytes 301064 | tf_op jit(solution)/shard_map/ppermute | solution.py:30
  103.0 4.8 %copy-start.5 = (bf16[1,112,1792]{2,1,0:T(8,128)(2,1)}, bf16[1,112,1792]{2,1,0:T(8,128)(2,1)S(1)}, u32[]{:S(2)}) copy-start(bf16[1,112,1792]{2,1,0:T(8,128)(2,1)S(1)} %fusion.43) | copy-start | bytes 1204228
  109.8 34.3 %all-to-all-start.1 = ((bf16[2,112,1792]{1,0,2:T(2,128)(2,1)}), bf16[2,112,1792]{1,0,2:T(2,128)(2,1)S(1)}, u32[]{:S(2)}, u32[]{:S(2)}) async-start(bf16[2,112,1792]{1,0,2:T(2,128)(2,1)} %copy.17), calls=%async_computation.1 | async-start | bytes 1835008 | tf_op jit(solution)/shard_map/all_to_all | solution.py:49
  145.5 4.7 %copy-start.6 = (bf16[1792,112]{0,1:T(8,128)(2,1)S(1)}, bf16[1792,112]{0,1:T(8,128)(2,1)}, u32[]{:S(2)}) copy-start(bf16[1792,112]{0,1:T(8,128)(2,1)} %all_to_all.38) | copy-start | bytes 1204228
  145.5 4.8 %copy-start.7 = (bf16[1,1792,1792]{2,1,0:T(8,128)(2,1)S(1)}, bf16[1,1792,1792]{2,1,0:T(8,128)(2,1)}, u32[]{:S(2)}) copy-start(bf16[1,1792,1792]{2,1,0:T(8,128)(2,1)} %all-gather.7.cloned.1.call-done) | copy-start | bytes 19267588
  182.9 1.1 copy-start.3
Sparse Core Ops, SparseCore 0:
  12.6 89.2 reduce-scatter.3
Sparse Core Ops, SparseCore 1:
  14.1 60.6 all-gather.4
  76.5 45.2 all-gather.6

commit v2 on v1

--- a/solution.py
+++ b/solution.py
@@ -8,7 +8,6 @@
 epsilon = 1e-08
 f32, bf16 = jnp.float32, jnp.bfloat16
 SIDE = 4
-TOGETHER = 56
 
 
 def swaps(axis, mask):
@@ -17,32 +16,41 @@
     return [(y * SIDE + x, (y ^ mask) * SIDE + x) for y in range(SIDE) for x in range(SIDE)]
 
 
-def halving(values, at, order):
+def halving(grid, corner, extent, at, order, mask):
+    other = mask ^ 2
     spot = list(at)
     for axis in order:
 
-        def own(mask, axis=axis, values=values):
-            return lax.dynamic_index_in_dim(values, spot[axis] ^ mask, axis=axis, keepdims=True).astype(f32)
+        def own(flip, axis=axis, grid=grid, corner=corner):
+            start = [0, 0, *corner]
+            start[axis] = spot[axis] ^ flip
+            sizes = [*grid.shape[:2], *extent]
+            sizes[axis] = 1
+            return lax.dynamic_slice(grid, start, sizes)
 
-        away = jnp.concatenate([own(1), own(2)], axis=axis).astype(bf16)
-        got = lax.ppermute(away, "dp", swaps(axis, 1)).astype(f32)
-        first, second = jnp.split(got, 2, axis=axis)
-        across = lax.ppermute((own(3) + second).astype(bf16), "dp", swaps(axis, 3))
-        values = own(0) + first + across.astype(f32)
-        spot[axis] = 0
-    return values[0, 0]
+        away = jnp.concatenate([own(mask), own(2)], axis=axis).astype(bf16)
+        got = lax.ppermute(away, "dp", swaps(axis, mask))
+        first = lax.slice_in_dim(got, 0, 1, axis=axis).astype(f32)
+        second = lax.slice_in_dim(got, 1, 2, axis=axis).astype(f32)
+        across = (own(other).astype(f32) + second).astype(bf16)
+        across = lax.ppermute(across, "dp", swaps(axis, other))
+        grid = own(0).astype(f32) + first + across.astype(f32)
+        spot[axis], corner = 0, (0, 0)
+    return grid[0, 0]
 
 
 def reduce_blocks(parts):
     rows, columns = parts.shape[1:]
     me = lax.axis_index("dp")
     at = (me // SIDE, me % SIDE)
-    upper = lax.psum_scatter(parts[:, :TOGETHER], "dp", scatter_dimension=0, tiled=True)[0]
-    grid = parts.reshape(SIDE, SIDE, rows, columns)[:, :, TOGETHER:]
-    left = halving(grid[..., : columns // 2], at, (1, 0))
-    right = halving(grid[..., columns // 2 :], at, (0, 1))
-    lower = jnp.concatenate([left, right], axis=1).astype(bf16)
-    return jnp.concatenate([upper, lower], axis=0)
+    grid = parts.reshape(SIDE, SIDE, rows, columns)
+    extent = (rows // 2, columns // 2)
+    streams = [((1, 0), 1), ((0, 1), 1), ((1, 0), 3), ((0, 1), 3)]
+    quarters = [
+        halving(grid, (r * extent[0], c * extent[1]), extent, at, *streams[2 * r + c]) for r in range(2) for c in range(2)
+    ]
+    upper, lower = jnp.concatenate(quarters[:2], axis=1), jnp.concatenate(quarters[2:], axis=1)
+    return jnp.concatenate([upper, lower], axis=0).astype(bf16)
 
 
 def to_cols(rows):

time: 199 us -> 195 us (0.980)
  local copies, waits for them, and re-layouts: 20.3 us -> 11.6 us
  starting transfers between devices: 32.9 us -> 38.6 us
  other arithmetic: 10.2 us -> 13.1 us
  waiting for transfers between devices: 72.9 us -> 70.5 us
    unnamed x4 -> x2, waiting for transfers between devices: 16.9 us -> 1.38 us
    ppermute x8 -> x16, waiting for transfers between devices: 22.4 us -> 32.1 us  [the longest x8 17.3 us: halving(): got = lax.ppermute(away, 'dp', swaps(axis, mask))]
    slice x2 -> x0, local copies, waits for them, and re-layouts: 5.96 us -> none  [the longest x1 3.77 us: reduce_blocks(): parts[:, :TOGETHER]]
    add x2 -> x4, other arithmetic: 1.28 us -> 5.8 us  [halving(): grid = own(0).astype(f32) + first + across.astype(f32)]
    all_to_all x2, waiting for transfers between devices: 33.5 us -> 37 us  [to_cols(): lax.all_to_all(rows, 'shard', split_axis=rows.ndim - 1, concat_axis=rows....]
    ppermute x8 -> x16, starting transfers between devices: 14.1 us -> 17 us  [the longest x8 10.8 us: halving(): got = lax.ppermute(away, 'dp', swaps(axis, mask))]
    all_to_all x4, local copies, waits for them, and re-layouts: 5.66 us -> 2.79 us  [to_cols(): lax.all_to_all(rows, 'shard', split_axis=rows.ndim - 1, concat_axis=rows....]
    all_to_all x2, starting transfers between devices: 18.7 us -> 21.5 us  [to_cols(): lax.all_to_all(rows, 'shard', split_axis=rows.ndim - 1, concat_axis=rows....]
  transfers between devices with their start and end apart: 13 -> 20, of which waited for: 7 -> 10; matrix products, arithmetic and copies ran while one was open for 11% -> 12% of each run, Pallas kernels for 0% -> 0%
where the time goes in v2:
time: 195 us
  waiting for transfers between devices  70.5 us (36%)
  starting transfers between devices  38.6 us (20%)
  blocking collectives  28.9 us (15%)
  matrix products  17 us (9%)
  between operations  15.1 us (8%)
  other arithmetic  13.1 us (7%)
  local copies, waits for them, and re-layouts  11.6 us (6%)
    all_to_all x2, waiting for transfers between devices, to_cols(): lax.all_to_all(rows, 'shard', split_axis=rows.ndim - 1, concat_axis=rows....  37 us
    all_to_all x1, blocking collectives, to_rows(): lax.all_to_all(cols, 'shard', split_axis=cols.ndim - 2, concat_axis=cols....  28.9 us
    all_to_all x2, starting transfers between devices, to_cols(): lax.all_to_all(rows, 'shard', split_axis=rows.ndim - 1, concat_axis=rows....  21.5 us
    ppermute x8, waiting for transfers between devices, halving(): got = lax.ppermute(away, 'dp', swaps(axis, mask))  17.3 us
    ppermute x8, waiting for transfers between devices, halving(): across = lax.ppermute(across, 'dp', swaps(axis, other))  14.8 us
    ppermute x8, starting transfers between devices, halving(): got = lax.ppermute(away, 'dp', swaps(axis, mask))  10.8 us
    ppermute x8, starting transfers between devices, halving(): across = lax.ppermute(across, 'dp', swaps(axis, other))  6.22 us
    add x4, other arithmetic, halving(): grid = own(0).astype(f32) + first + across.astype(f32)  5.8 us
  transfers between devices with their start and end apart: 20, of which 10 were waited for; matrix products, arithmetic and copies ran while one was open for 12% of the time, Pallas kernels for 0%

profile of v2, /device:TPU:1, one launch (start us, length us, event | category | flops | bytes accessed | tf_op | source)
XLA Modules:
  0.0 194.7 jit_solution(855725620316547066)
XLA Ops:
  10.3 2.2 %collective-permute-start.4 = (bf16[2,4,56,896]{3,2,1,0:T(8,128)(2,1)S(1)}, bf16[2,4,56,896]{3,2,1,0:T(8,128)(2,1)}, u32[]{:S(2)}, u32[]{:S(2)}) collective-permute-start(bf16[2,4,56,896]{3,2,1,0:T(8,128)(2,1)S(1)} %pad_maximum_fusion.1), channel_id=1, source_target_pairs={{0,64},{16,80},{32,96},{48,112},{64,0},{80,16},{96,32},{112,48},{1... | collective-permute-start | bytes 2408456 | tf_op jit(solution)/shard_map/ppermute | solution.py:32
  17.2 1.9 collective-permute-start.12
  20.1 10.0 %all-to-all-start = ((bf16[112,16,112]{0,2,1:T(8,128)(2,1)}), bf16[112,16,112]{0,2,1:T(8,128)(2,1)S(1)}, u32[]{:S(2)}, u32[]{:S(2)}) async-start(bf16[112,16,112]{0,2,1:T(8,128)(2,1)} %bitcast.6), calls=%async_computation | async-start | bytes 917504 | tf_op jit(solution)/shard_map/all_to_all | solution.py:57
  31.1 1.8 collective-permute-start.8
  36.3 1.6 collective-permute-start.1
  37.9 12.5 %all-to-all-done = bf16[112,16,112]{0,2,1:T(8,128)(2,1)S(1)} async-done(((bf16[112,16,112]{0,2,1:T(8,128)(2,1)}), bf16[112,16,112]{0,2,1:T(8,128)(2,1)S(1)}, u32[]{:S(2)}, u32[]{:S(2)}) %all-to-all-start) | async-done | bytes 401440 | tf_op jit(solution)/shard_map/all_to_all | solution.py:57
  51.8 1.8 convert_add_fusion.2
  54.0 6.7 %collective-permute-done.1 = bf16[4,1,56,896]{3,2,1,0:T(8,128)(2,1)} collective-permute-done((bf16[4,1,56,896]{3,2,1,0:T(8,128)(2,1)S(1)}, bf16[4,1,56,896]{3,2,1,0:T(8,128)(2,1)}, u32[]{:S(2)}, u32[]{:S(2)}) %collective-permute-start.1) | collective-permute-done | bytes 401440 | tf_op jit(solution)/shard_map/ppermute | solution.py:36
  64.6 12.0 %collective-permute-done.6 = bf16[1,2,56,896]{3,2,1,0:T(8,128)(2,1)S(1)} collective-permute-done((bf16[1,2,56,896]{3,2,1,0:T(8,128)(2,1)S(1)}, bf16[1,2,56,896]{3,2,1,0:T(8,128)(2,1)S(1)}, u32[]{:S(2)}, u32[]{:S(2)}) %collective-permute-start.6) | collective-permute-done | bytes 200736 | tf_op jit(solution)/shard_map/ppermute | solution.py:32
  76.7 1.9 collective-permute-start.7
  79.5 2.0 %collective-permute-done.7 = bf16[1,1,56,896]{3,2,1,0:T(8,128)(2,1)S(1)} collective-permute-done((bf16[1,1,56,896]{3,2,1,0:T(8,128)(2,1)S(1)}, bf16[1,1,56,896]{3,2,1,0:T(8,128)(2,1)S(1)}, u32[]{:S(2)}, u32[]{:S(2)}) %collective-permute-start.7) | collective-permute-done | bytes 100384 | tf_op jit(solution)/shard_map/ppermute | solution.py:36
  81.5 2.2 %collective-permute-done.3 = bf16[1,1,56,896]{3,2,1,0:T(8,128)(2,1)S(1)} collective-permute-done((bf16[1,1,56,896]{3,2,1,0:T(8,128)(2,1)S(1)}, bf16[1,1,56,896]{3,2,1,0:T(8,128)(2,1)S(1)}, u32[]{:S(2)}, u32[]{:S(2)}) %collective-permute-start.3) | collective-permute-done | bytes 100384 | tf_op jit(solution)/shard_map/ppermute | solution.py:36
  87.9 3.5 %collective-permute-done.14 = bf16[1,2,56,896]{3,2,1,0:T(8,128)(2,1)S(1)} collective-permute-done((bf16[1,2,56,896]{3,2,1,0:T(8,128)(2,1)S(1)}, bf16[1,2,56,896]{3,2,1,0:T(8,128)(2,1)S(1)}, u32[]{:S(2)}, u32[]{:S(2)}) %collective-permute-start.14) | collective-permute-done | bytes 200736 | tf_op jit(solution)/shard_map/ppermute | solution.py:32
  91.5 1.8 collective-permute-done.10
  93.6 1.8 collective-permute-done.15
  95.5 2.0 %collective-permute-done.11 = bf16[1,1,56,896]{3,2,1,0:T(8,128)(2,1)S(1)} collective-permute-done((bf16[1,1,56,896]{3,2,1,0:T(8,128)(2,1)S(1)}, bf16[1,1,56,896]{3,2,1,0:T(8,128)(2,1)S(1)}, u32[]{:S(2)}, u32[]{:S(2)}) %collective-permute-start.11) | collective-permute-done | bytes 100384 | tf_op jit(solution)/shard_map/ppermute | solution.py:36
  97.8 4.7 %fusion.11 = bf16[2,112,1792]{2,1,0:T(8,128)(2,1)S(1)} fusion(bf16[1,1792,1792]{2,1,0:T(8,128)(2,1)} %all-gather.5.cloned.1.call-done, bf16[1,112,1792]{2,1,0:T(8,128)(2,1)S(1)} %fusion.39, bf16[1,112,1792]{2,1,0:T(8,128)(2,1)S(1)} %bitcast.99), kind=kOutput, calls=%fused_computation.9 | convolution fusion | flops 1439449088 | bytes 8028160 | tf_op jit(solution)/shard_map/nrk,kc->nrc/dot_general | solution.py:73
  102.4 2.0 %copy.17 = bf16[2,112,1792]{1,0,2:T(2,128)(2,1)} copy(bf16[2,112,1792]{2,1,0:T(8,128)(2,1)S(1)} %fusion.11) | data formatting | bytes 1605632 | tf_op jit(solution)/shard_map/convert_element_type | solution.py:73
  104.5 11.5 %all-to-all-start.1 = ((bf16[2,112,1792]{1,0,2:T(2,128)(2,1)}), bf16[2,112,1792]{1,0,2:T(2,128)(2,1)S(1)}, u32[]{:S(2)}, u32[]{:S(2)}) async-start(bf16[2,112,1792]{1,0,2:T(2,128)(2,1)} %copy.17), calls=%async_computation.1 | async-start | bytes 1835008 | tf_op jit(solution)/shard_map/all_to_all | solution.py:57
  116.8 24.6 %all-to-all-done.1 = bf16[2,112,1792]{1,0,2:T(2,128)(2,1)S(1)} async-done(((bf16[2,112,1792]{1,0,2:T(2,128)(2,1)}), bf16[2,112,1792]{1,0,2:T(2,128)(2,1)S(1)}, u32[]{:S(2)}, u32[]{:S(2)}) %all-to-all-start.1) | async-done | bytes 802848 | tf_op jit(solution)/shard_map/all_to_all | solution.py:57
  142.8 4.6 %fusion.8 = f32[2,1792,112]{1,2,0:T(8,128)S(1)} fusion(bf16[2,1792,112]{1,2,0:T(8,128)(2,1)S(1)} %all_to_all.42, bf16[1,1792,1792]{2,1,0:T(8,128)(2,1)} %all-gather.7.cloned.1.call-done), kind=kOutput, calls=%fused_computation.8 | convolution fusion | flops 1438646272 | bytes 8830976 | tf_op jit(solution)/shard_map/ki,nkc->nic/dot_general | solution.py:75
  147.6 2.0 %fusion.20 = bf16[1,1792,112]{1,2,0:T(8,128)(2,1)S(1)} fusion(bf16[1,1792,1792]{2,1,0:T(8,128)(2,1)S(1)} %copy-done.4, bf16[1792,112]{0,1:T(8,128)(2,1)S(1)} %copy-done.3, f32[2,1792,112]{1,2,0:T(8,128)S(1)} %fusion.8, f32[]{:T(128)} %bitcast.20, f32[]{:T(128)} %bitcast.18), kind=kOutput, calls=%fused_computation.12 | convolution fusion | flops 721530880 | bytes 8830984 | tf_op jit(solution)/shard_map/dot_general | solution.py:82
  150.9 28.9 %all_to_all.49 = bf16[2,1792,112]{2,0,1:T(2,128)(2,1)S(1)} all-to-all(bf16[2,1792,112]{2,0,1:T(2,128)(2,1)S(1)} %copy.19), channel_id=1, replica_groups=mesh['dp'=16,'shard'=16] {'shard'}, dimensions={1} | all-to-all | bytes 1605632 | tf_op jit(solution)/shard_map/all_to_all | solution.py:61
  182.2 5.7 %fusion.23 = bf16[1,112,1792]{2,1,0:T(8,128)(2,1)} fusion(bf16[112,1792]{1,0:T(8,128)(2,1)S(1)} %unstack.28, bf16[1,1792,1792]{2,1,0:T(8,128)(2,1)} %all-gather.5.cloned.1.call-done), kind=kOutput, calls=%fused_computation.13 | convolution fusion | flops 719523840 | bytes 7225344 | tf_op jit(solution)/shard_map/rc,kc->rk/dot_general | solution.py:87
  (78 shorter events, 29.8 us)
Async XLA Ops:
  7.2 11.9 %copy-start = (f32[1,112,1792]{2,1,0:T(8,128)S(1)}, f32[1,112,1792]{2,1,0:T(8,128)}, u32[]{:S(2)}) copy-start(f32[1,112,1792]{2,1,0:T(8,128)} %param.8) | copy-start | bytes 2408452
  7.2 90.6 %all-gather.5.cloned.1.call-start = ((), (), s32[]{:S(2)}) async-start(), calls=%async_computation.3 | async-start | bytes 6823936 | tf_op jit(solution)/shard_map/all_gather | solution.py:65
  7.9 134.9 %all-gather.7.cloned.1.call-start = ((), (), s32[]{:S(2)}) async-start(), calls=%async_computation.4 | async-start | bytes 6823936 | tf_op jit(solution)/shard_map/all_gather | solution.py:66
  10.3 22.7 %collective-permute-start.4 = (bf16[2,4,56,896]{3,2,1,0:T(8,128)(2,1)S(1)}, bf16[2,4,56,896]{3,2,1,0:T(8,128)(2,1)}, u32[]{:S(2)}, u32[]{:S(2)}) collective-permute-start(bf16[2,4,56,896]{3,2,1,0:T(8,128)(2,1)S(1)} %pad_maximum_fusion.1), channel_id=1, source_target_pairs={{0,64},{16,80},{32,96},{48,112},{64,0},{80,16},{96,32},{112,48},{1... | collective-permute-start | bytes 2408456 | tf_op jit(solution)/shard_map/ppermute | solution.py:32
  15.0 20.1 %collective-permute-start = (bf16[4,2,56,896]{3,2,1,0:T(8,128)(2,1)}, bf16[4,2,56,896]{3,2,1,0:T(8,128)(2,1)}, u32[]{:S(2)}, u32[]{:S(2)}) collective-permute-start(bf16[4,2,56,896]{3,2,1,0:T(8,128)(2,1)} %pad_maximum_fusion), channel_id=1, source_target_pairs={{0,16},{16,0},{32,48},{48,32},{64,80},{80,64},{96,112},{112,96},{1... | collective-permute-start | bytes 2408456 | tf_op jit(solution)/shard_map/ppermute | solution.py:32
  17.2 34.6 %collective-permute-start.12 = (bf16[2,4,56,896]{3,2,1,0:T(8,128)(2,1)}, bf16[2,4,56,896]{3,2,1,0:T(8,128)(2,1)}, u32[]{:S(2)}, u32[]{:S(2)}) collective-permute-start(bf16[2,4,56,896]{3,2,1,0:T(8,128)(2,1)} %pad_maximum_fusion.3), channel_id=1, source_target_pairs={{0,192},{16,208},{32,224},{48,240},{64,128},{80,144},{96,160},{112... | collective-permute-start | bytes 2408456 | tf_op jit(solution)/shard_map/ppermute | solution.py:32
  20.1 30.3 %all-to-all-start = ((bf16[112,16,112]{0,2,1:T(8,128)(2,1)}), bf16[112,16,112]{0,2,1:T(8,128)(2,1)S(1)}, u32[]{:S(2)}, u32[]{:S(2)}) async-start(bf16[112,16,112]{0,2,1:T(8,128)(2,1)} %bitcast.6), calls=%async_computation | async-start | bytes 917504 | tf_op jit(solution)/shard_map/all_to_all | solution.py:57
  31.1 22.9 %collective-permute-start.8 = (bf16[4,2,56,896]{3,2,1,0:T(8,128)(2,1)}, bf16[4,2,56,896]{3,2,1,0:T(8,128)(2,1)S(1)}, u32[]{:S(2)}, u32[]{:S(2)}) collective-permute-start(bf16[4,2,56,896]{3,2,1,0:T(8,128)(2,1)} %pad_maximum_fusion.2), channel_id=1, source_target_pairs={{0,48},{16,32},{32,16},{48,0},{64,112},{80,96},{96,80},{112,64},{1... | collective-permute-start | bytes 2408456 | tf_op jit(solution)/shard_map/ppermute | solution.py:32
  34.2 17.6 %collective-permute-start.5 = (bf16[1,4,56,896]{3,2,1,0:T(8,128)(2,1)S(1)}, bf16[1,4,56,896]{3,2,1,0:T(8,128)(2,1)}, u32[]{:S(2)}, u32[]{:S(2)}) collective-permute-start(bf16[1,4,56,896]{3,2,1,0:T(8,128)(2,1)S(1)} %add_convert_fusion.2), channel_id=1, source_target_pairs={{0,192},{16,208},{32,224},{48,240},{64,128},{80,144},{96,160},{112... | collective-permute-start | bytes 1204232 | tf_op jit(solution)/shard_map/ppermute | solution.py:36
  36.3 24.4 %collective-permute-start.1 = (bf16[4,1,56,896]{3,2,1,0:T(8,128)(2,1)S(1)}, bf16[4,1,56,896]{3,2,1,0:T(8,128)(2,1)}, u32[]{:S(2)}, u32[]{:S(2)}) collective-permute-start(bf16[4,1,56,896]{3,2,1,0:T(8,128)(2,1)S(1)} %add_convert_fusion.3), channel_id=1, source_target_pairs={{0,48},{16,32},{32,16},{48,0},{64,112},{80,96},{96,80},{112,64},{1... | collective-permute-start | bytes 1204232 | tf_op jit(solution)/shard_map/ppermute | solution.py:36
  53.5 30.2 %collective-permute-start.13 = (bf16[1,4,56,896]{3,2,1,0:T(8,128)(2,1)S(1)}, bf16[1,4,56,896]{3,2,1,0:T(8,128)(2,1)S(1)}, u32[]{:S(2)}, u32[]{:S(2)}) collective-permute-start(bf16[1,4,56,896]{3,2,1,0:T(8,128)(2,1)S(1)} %get-tuple-element.14), channel_id=1, source_target_pairs={{0,64},{16,80},{32,96},{48,112},{64,0},{80,16},{96,32},{112,48},{1... | collective-permute-start | bytes 1204232 | tf_op jit(solution)/shard_map/ppermute | solution.py:36
  62.3 35.2 %copy-start.1 = (bf16[1,112,1792]{2,1,0:T(8,128)(2,1)S(1)}, bf16[1,112,1792]{2,1,0:T(8,128)(2,1)}, u32[]{:S(2)}) copy-start(bf16[1,112,1792]{2,1,0:T(8,128)(2,1)} %param.7) | copy-start | bytes 1204228
  62.3 23.5 %collective-permute-start.9 = (bf16[4,1,56,896]{3,2,1,0:T(8,128)(2,1)S(1)}, bf16[4,1,56,896]{3,2,1,0:T(8,128)(2,1)S(1)}, u32[]{:S(2)}, u32[]{:S(2)}) collective-permute-start(bf16[4,1,56,896]{3,2,1,0:T(8,128)(2,1)S(1)} %get-tuple-element.8), channel_id=1, source_target_pairs={{0,16},{16,0},{32,48},{48,32},{64,80},{80,64},{96,112},{112,96},{1... | collective-permute-start | bytes 1204232 | tf_op jit(solution)/shard_map/ppermute | solution.py:36
  62.5 14.1 %collective-permute-start.6 = (bf16[1,2,56,896]{3,2,1,0:T(8,128)(2,1)S(1)}, bf16[1,2,56,896]{3,2,1,0:T(8,128)(2,1)S(1)}, u32[]{:S(2)}, u32[]{:S(2)}) collective-permute-start(bf16[1,2,56,896]{3,2,1,0:T(8,128)(2,1)S(1)} %pad_maximum_fusion.6), channel_id=1, source_target_pairs={{0,16},{16,0},{32,48},{48,32},{64,80},{80,64},{96,112},{112,96},{1... | collective-permute-start | bytes 602120 | tf_op jit(solution)/shard_map/ppermute | solution.py:32
  64.1 14.5 %collective-permute-start.2 = (bf16[2,1,56,896]{3,2,1,0:T(8,128)(2,1)S(1)}, bf16[2,1,56,896]{3,2,1,0:T(8,128)(2,1)S(1)}, u32[]{:S(2)}, u32[]{:S(2)}) collective-permute-start(bf16[2,1,56,896]{3,2,1,0:T(8,128)(2,1)S(1)} %pad_maximum_fusion.5), channel_id=1, source_target_pairs={{0,64},{16,80},{32,96},{48,112},{64,0},{80,16},{96,32},{112,48},{1... | collective-permute-start | bytes 602120 | tf_op jit(solution)/shard_map/ppermute | solution.py:32
  76.7 4.8 %collective-permute-start.7 = (bf16[1,1,56,896]{3,2,1,0:T(8,128)(2,1)S(1)}, bf16[1,1,56,896]{3,2,1,0:T(8,128)(2,1)S(1)}, u32[]{:S(2)}, u32[]{:S(2)}) collective-permute-start(bf16[1,1,56,896]{3,2,1,0:T(8,128)(2,1)S(1)} %add_convert_fusion.9), channel_id=1, source_target_pairs={{0,48},{16,32},{32,16},{48,0},{64,112},{80,96},{96,80},{112,64},{1... | collective-permute-start | bytes 301064 | tf_op jit(solution)/shard_map/ppermute | solution.py:36
  78.6 5.1 %collective-permute-start.3 = (bf16[1,1,56,896]{3,2,1,0:T(8,128)(2,1)S(1)}, bf16[1,1,56,896]{3,2,1,0:T(8,128)(2,1)S(1)}, u32[]{:S(2)}, u32[]{:S(2)}) collective-permute-start(bf16[1,1,56,896]{3,2,1,0:T(8,128)(2,1)S(1)} %add_convert_fusion.11), channel_id=1, source_target_pairs={{0,192},{16,208},{32,224},{48,240},{64,128},{80,144},{96,160},{112... | collective-permute-start | bytes 301064 | tf_op jit(solution)/shard_map/ppermute | solution.py:36
  85.1 6.3 %collective-permute-start.14 = (bf16[1,2,56,896]{3,2,1,0:T(8,128)(2,1)S(1)}, bf16[1,2,56,896]{3,2,1,0:T(8,128)(2,1)S(1)}, u32[]{:S(2)}, u32[]{:S(2)}) collective-permute-start(bf16[1,2,56,896]{3,2,1,0:T(8,128)(2,1)S(1)} %pad_maximum_fusion.8), channel_id=1, source_target_pairs={{0,48},{16,32},{32,16},{48,0},{64,112},{80,96},{96,80},{112,64},{1... | collective-permute-start | bytes 602120 | tf_op jit(solution)/shard_map/ppermute | solution.py:32
  87.0 6.3 %collective-permute-start.10 = (bf16[2,1,56,896]{3,2,1,0:T(8,128)(2,1)S(1)}, bf16[2,1,56,896]{3,2,1,0:T(8,128)(2,1)S(1)}, u32[]{:S(2)}, u32[]{:S(2)}) collective-permute-start(bf16[2,1,56,896]{3,2,1,0:T(8,128)(2,1)S(1)} %pad_maximum_fusion.7), channel_id=1, source_target_pairs={{0,192},{16,208},{32,224},{48,240},{64,128},{80,144},{96,160},{112... | collective-permute-start | bytes 602120 | tf_op jit(solution)/shard_map/ppermute | solution.py:32
  91.4 4.0 %collective-permute-start.15 = (bf16[1,1,56,896]{3,2,1,0:T(8,128)(2,1)S(1)}, bf16[1,1,56,896]{3,2,1,0:T(8,128)(2,1)S(1)}, u32[]{:S(2)}, u32[]{:S(2)}) collective-permute-start(bf16[1,1,56,896]{3,2,1,0:T(8,128)(2,1)S(1)} %add_convert_fusion.5), channel_id=1, source_target_pairs={{0,16},{16,0},{32,48},{48,32},{64,80},{80,64},{96,112},{112,96},{1... | collective-permute-start | bytes 301064 | tf_op jit(solution)/shard_map/ppermute | solution.py:36
  93.3 4.2 %collective-permute-start.11 = (bf16[1,1,56,896]{3,2,1,0:T(8,128)(2,1)S(1)}, bf16[1,1,56,896]{3,2,1,0:T(8,128)(2,1)S(1)}, u32[]{:S(2)}, u32[]{:S(2)}) collective-permute-start(bf16[1,1,56,896]{3,2,1,0:T(8,128)(2,1)S(1)} %add_convert_fusion.7), channel_id=1, source_target_pairs={{0,64},{16,80},{32,96},{48,112},{64,0},{80,16},{96,32},{112,48},{1... | collective-permute-start | bytes 301064 | tf_op jit(solution)/shard_map/ppermute | solution.py:36
  97.7 6.8 %copy-start.2 = (bf16[1,112,1792]{2,1,0:T(8,128)(2,1)}, bf16[1,112,1792]{2,1,0:T(8,128)(2,1)S(1)}, u32[]{:S(2)}) copy-start(bf16[1,112,1792]{2,1,0:T(8,128)(2,1)S(1)} %fusion.39) | copy-start | bytes 1204228
  104.5 36.8 %all-to-all-start.1 = ((bf16[2,112,1792]{1,0,2:T(2,128)(2,1)}), bf16[2,112,1792]{1,0,2:T(2,128)(2,1)S(1)}, u32[]{:S(2)}, u32[]{:S(2)}) async-start(bf16[2,112,1792]{1,0,2:T(2,128)(2,1)} %copy.17), calls=%async_computation.1 | async-start | bytes 1835008 | tf_op jit(solution)/shard_map/all_to_all | solution.py:57
  142.8 4.8 %copy-start.4 = (bf16[1,1792,1792]{2,1,0:T(8,128)(2,1)S(1)}, bf16[1,1792,1792]{2,1,0:T(8,128)(2,1)}, u32[]{:S(2)}) copy-start(bf16[1,1792,1792]{2,1,0:T(8,128)(2,1)} %all-gather.7.cloned.1.call-done) | copy-start | bytes 19267588
  (1 other events, 4.7 us)
Sparse Core Ops, SparseCore 0:
  9.8 60.6 all-gather.4
  72.4 45.2 all-gather.6

commit v3 on v1

--- a/solution.py
+++ b/solution.py
@@ -7,42 +7,6 @@
 beta_two = 0.95
 epsilon = 1e-08
 f32, bf16 = jnp.float32, jnp.bfloat16
-SIDE = 4
-TOGETHER = 56
-
-
-def swaps(axis, mask):
-    if axis:
-        return [(y * SIDE + x, y * SIDE + (x ^ mask)) for y in range(SIDE) for x in range(SIDE)]
-    return [(y * SIDE + x, (y ^ mask) * SIDE + x) for y in range(SIDE) for x in range(SIDE)]
-
-
-def halving(values, at, order):
-    spot = list(at)
-    for axis in order:
-
-        def own(mask, axis=axis, values=values):
-            return lax.dynamic_index_in_dim(values, spot[axis] ^ mask, axis=axis, keepdims=True).astype(f32)
-
-        away = jnp.concatenate([own(1), own(2)], axis=axis).astype(bf16)
-        got = lax.ppermute(away, "dp", swaps(axis, 1)).astype(f32)
-        first, second = jnp.split(got, 2, axis=axis)
-        across = lax.ppermute((own(3) + second).astype(bf16), "dp", swaps(axis, 3))
-        values = own(0) + first + across.astype(f32)
-        spot[axis] = 0
-    return values[0, 0]
-
-
-def reduce_blocks(parts):
-    rows, columns = parts.shape[1:]
-    me = lax.axis_index("dp")
-    at = (me // SIDE, me % SIDE)
-    upper = lax.psum_scatter(parts[:, :TOGETHER], "dp", scatter_dimension=0, tiled=True)[0]
-    grid = parts.reshape(SIDE, SIDE, rows, columns)[:, :, TOGETHER:]
-    left = halving(grid[..., : columns // 2], at, (1, 0))
-    right = halving(grid[..., columns // 2 :], at, (0, 1))
-    lower = jnp.concatenate([left, right], axis=1).astype(bf16)
-    return jnp.concatenate([upper, lower], axis=0)
 
 
 def to_cols(rows):
@@ -54,13 +18,13 @@
 
 
 def local(grad_parts, moment, second, left_basis, right_basis, block_steps):
-    right_full = lax.all_gather(right_basis[0], "shard", axis=0, tiled=True)
-    left_full = lax.all_gather(left_basis[0], "shard", axis=0, tiled=True)
-    gradient = reduce_blocks(grad_parts[0])
+    gradient = lax.psum_scatter(grad_parts[0], "dp", scatter_dimension=0, tiled=True)[0]
+    bases = jnp.concatenate([right_basis, left_basis], axis=0)
+    right_full, left_full = lax.all_gather(bases, "shard", axis=1, tiled=True)
     second_cols = to_cols(second[0].astype(bf16))
     gradient, second_cols = lax.optimization_barrier((gradient, second_cols))
+
     moment_new = (beta_one * moment[0].astype(f32) + (1.0 - beta_one) * gradient.astype(f32)).astype(bf16)
-
     pair = jnp.stack([gradient, moment_new])
     pair_right = jnp.einsum("nrk,kc->nrc", pair, right_full, preferred_element_type=f32).astype(bf16)
     pair_cols = to_cols(pair_right)

time: 199 us -> 200 us (level)
  blocking collectives: 28.9 us -> 56.2 us
  starting transfers between devices: 32.9 us -> 8.89 us
  waiting for transfers between devices: 72.9 us -> 89.3 us
  local copies, waits for them, and re-layouts: 20.3 us -> 9.05 us
  other arithmetic: 10.2 us -> 3.35 us
    unnamed x4 -> x3, waiting for transfers between devices: 16.9 us -> 64.7 us
    all_to_all x0 -> x1, blocking collectives: none -> 27.3 us  [to_cols(): lax.all_to_all(rows, 'shard', split_axis=rows.ndim - 1, concat_axis=rows....]
    ppermute x8 -> x0, waiting for transfers between devices: 22.4 us -> none  [the longest x4 14.3 us: halving(): across = lax.ppermute((own(3) + second).astype(bf16), 'dp', swaps(axis, 3))]
    ppermute x8 -> x0, starting transfers between devices: 14.1 us -> none  [the longest x4 9.94 us: halving(): across = lax.ppermute((own(3) + second).astype(bf16), 'dp', swaps(axis, 3))]
    all_to_all x2 -> x1, starting transfers between devices: 18.7 us -> 8.81 us  [to_cols(): lax.all_to_all(rows, 'shard', split_axis=rows.ndim - 1, concat_axis=rows....]
    all_to_all x2 -> x1, waiting for transfers between devices: 33.5 us -> 24.6 us  [to_cols(): lax.all_to_all(rows, 'shard', split_axis=rows.ndim - 1, concat_axis=rows....]
    slice x2 -> x0, local copies, waits for them, and re-layouts: 5.96 us -> none  [the longest x1 3.77 us: reduce_blocks(): parts[:, :TOGETHER]]
    convert_element_type x8 -> x0, other arithmetic: 3.75 us -> none  [the longest x4 2.77 us: halving(): got = lax.ppermute(away, 'dp', swaps(axis, 1)).astype(f32)]
  transfers between devices with their start and end apart: 13 -> 3, of which waited for: 7 -> 2; matrix products, arithmetic and copies ran while one was open for 11% -> 1% of each run, Pallas kernels for 0% -> 0%
where the time goes in v3:
time: 200 us
  waiting for transfers between devices  89.3 us (45%)
  blocking collectives  56.2 us (28%)
  matrix products  17 us (8%)
  between operations  16.4 us (8%)
  local copies, waits for them, and re-layouts  9.05 us (5%)
  starting transfers between devices  8.89 us (4%)
  other arithmetic  3.35 us (2%)
    unnamed x3, waiting for transfers between devices  64.7 us
    all_to_all x1, blocking collectives, to_rows(): lax.all_to_all(cols, 'shard', split_axis=cols.ndim - 2, concat_axis=cols....  28.9 us
    all_to_all x1, blocking collectives, to_cols(): lax.all_to_all(rows, 'shard', split_axis=rows.ndim - 1, concat_axis=rows....  27.3 us
    all_to_all x1, waiting for transfers between devices, to_cols(): lax.all_to_all(rows, 'shard', split_axis=rows.ndim - 1, concat_axis=rows....  24.6 us
    all_to_all x1, starting transfers between devices, to_cols(): lax.all_to_all(rows, 'shard', split_axis=rows.ndim - 1, concat_axis=rows....  8.81 us
    dot_general x1, matrix products, local(): jnp.einsum('rc,kc->rk', left_dir_rows, right_full, preferred_element_type...  5.68 us
    dot_general x1, matrix products, local(): jnp.einsum('nrk,kc->nrc', pair, right_full, preferred_element_type=f32)  4.69 us
    dot_general x1, matrix products, local(): jnp.einsum('ki,nkc->nic', left_full, pair_cols, preferred_element_type=f32)  4.59 us
  transfers between devices with their start and end apart: 3, of which 2 were waited for; matrix products, arithmetic and copies ran while one was open for 1% of the time, Pallas kernels for 0%

profile of v3, /device:TPU:1, one launch (start us, length us, event | category | flops | bytes accessed | tf_op | source)
XLA Modules:
  0.0 200.1 jit_solution(16272576186391541933)
XLA Ops:
  8.1 0.7 reduce-scatter.4.cloned.1.call-update
  8.8 0.2 copy-done.1
  9.1 1.0 pad_maximum_fusion
  10.2 0.3 copy.15
  10.4 27.3 %all_to_all.49 = bf16[112,16,112]{0,2,1:T(8,128)(2,1)S(1)} all-to-all(bf16[112,16,112]{0,2,1:T(8,128)(2,1)S(1)} %bitcast.84), channel_id=1, replica_groups=mesh['dp'=16,'shard'=16] {'shard'}, dimensions={1} | all-to-all | bytes 802816 | tf_op jit(solution)/shard_map/all_to_all | solution.py:13
  37.8 0.5 all_to_all.38
  38.3 64.0 %reduce-scatter.4.cloned.1.call-done = bf16[1,112,1792]{2,1,0:T(8,128)(2,1)} async-done(((bf16[16,112,1792]{2,1,0:T(8,128)(2,1)}), bf16[1,112,1792]{2,1,0:T(8,128)(2,1)}) %reduce-scatter.4.cloned.1.call-update) | async-done | bytes 401424
  102.3 1.1 fusion.43
  103.5 4.7 %fusion.15 = bf16[2,112,1792]{2,1,0:T(8,128)(2,1)S(1)} fusion(bf16[2,1792,1792]{2,1,0:T(8,128)(2,1)} %all-gather.2.cloned.1.call-done, bf16[1,112,1792]{2,1,0:T(8,128)(2,1)S(1)} %fusion.43, bf16[1,112,1792]{2,1,0:T(8,128)(2,1)} %reduce-scatter.4.cloned.1.call-done), kind=kOutput, calls=%fused_computation.13 | convolution fusion | flops 1439449088 | bytes 8028160 | tf_op jit(solution)/shard_map/nrk,kc->nrc/dot_general | solution.py:29
  108.2 2.1 %copy.17 = bf16[2,112,1792]{1,0,2:T(2,128)(2,1)} copy(bf16[2,112,1792]{2,1,0:T(8,128)(2,1)S(1)} %fusion.15) | data formatting | bytes 1605632 | tf_op jit(solution)/shard_map/convert_element_type | solution.py:29
  110.3 8.8 %all-to-all-start.1 = ((bf16[2,112,1792]{1,0,2:T(2,128)(2,1)}), bf16[2,112,1792]{1,0,2:T(2,128)(2,1)S(1)}, u32[]{:S(2)}, u32[]{:S(2)}) async-start(bf16[2,112,1792]{1,0,2:T(2,128)(2,1)} %copy.17), calls=%async_computation.1 | async-start | bytes 1835008 | tf_op jit(solution)/shard_map/all_to_all | solution.py:13
  119.8 24.6 %all-to-all-done.1 = bf16[2,112,1792]{1,0,2:T(2,128)(2,1)S(1)} async-done(((bf16[2,112,1792]{1,0,2:T(2,128)(2,1)}), bf16[2,112,1792]{1,0,2:T(2,128)(2,1)S(1)}, u32[]{:S(2)}, u32[]{:S(2)}) %all-to-all-start.1) | async-done | bytes 802848 | tf_op jit(solution)/shard_map/all_to_all | solution.py:13
  144.4 0.4 copy.24
  144.7 1.1 all_to_all.42
  145.8 4.6 %fusion.12 = f32[2,1792,112]{1,2,0:T(8,128)S(1)} fusion(bf16[2,1792,112]{1,2,0:T(8,128)(2,1)S(1)} %all_to_all.42, bf16[2,1792,1792]{2,1,0:T(8,128)(2,1)} %all-gather.2.cloned.1.call-done), kind=kOutput, calls=%fused_computation.12 | convolution fusion | flops 1438646272 | bytes 8830976 | tf_op jit(solution)/shard_map/ki,nkc->nic/dot_general | solution.py:31
  150.5 1.8 copy-done.5
  152.3 2.0 %fusion.24 = bf16[1,1792,112]{1,2,0:T(8,128)(2,1)S(1)} fusion(bf16[2,1792,1792]{2,1,0:T(8,128)(2,1)S(1)} %copy-done.5, bf16[1792,112]{0,1:T(8,128)(2,1)S(1)} %all_to_all.38, f32[2,1792,112]{1,2,0:T(8,128)S(1)} %fusion.12, f32[]{:T(128)} %bitcast.17, f32[]{:T(128)} %bitcast.15), kind=kOutput, calls=%fused_computation.16 | convolution fusion | flops 721530880 | bytes 8830984 | tf_op jit(solution)/shard_map/dot_general | solution.py:38
  154.4 1.2 copy.19
  155.6 28.9 %all_to_all.50 = bf16[2,1792,112]{2,0,1:T(2,128)(2,1)S(1)} all-to-all(bf16[2,1792,112]{2,0,1:T(2,128)(2,1)S(1)} %copy.19), channel_id=1, replica_groups=mesh['dp'=16,'shard'=16] {'shard'}, dimensions={1} | all-to-all | bytes 1605632 | tf_op jit(solution)/shard_map/all_to_all | solution.py:17
  184.5 0.4 copy.23
  185.0 0.4 reshape.45
  185.4 1.0 fusion.36
  186.5 0.5 unstack.44
  186.9 5.7 %fusion.27 = bf16[1,112,1792]{2,1,0:T(8,128)(2,1)} fusion(bf16[112,1792]{1,0:T(8,128)(2,1)S(1)} %unstack.44, bf16[2,1792,1792]{2,1,0:T(8,128)(2,1)} %all-gather.2.cloned.1.call-done), kind=kOutput, calls=%fused_computation.17 | convolution fusion | flops 719523840 | bytes 7225344 | tf_op jit(solution)/shard_map/rc,kc->rk/dot_general | solution.py:43
  (19 shorter events, 0.7 us)
Async XLA Ops:
  8.0 1.0 copy-start.1
  8.0 1.1 copy-start.2
  8.0 2.1 %copy-start = (f32[1,112,1792]{2,1,0:T(8,128)S(1)}, f32[1,112,1792]{2,1,0:T(8,128)}, u32[]{:S(2)}) copy-start(f32[1,112,1792]{2,1,0:T(8,128)} %param.8) | copy-start | bytes 2408452
  8.0 94.3 %reduce-scatter.4.cloned.1.call-start = ((), (), s32[]{:S(2)}) async-start(), calls=%async_computation.5 | async-start | bytes 6823936
  8.1 94.2 %copy-start.3 = (bf16[1,112,1792]{2,1,0:T(8,128)(2,1)S(1)}, bf16[1,112,1792]{2,1,0:T(8,128)(2,1)}, u32[]{:S(2)}) copy-start(bf16[1,112,1792]{2,1,0:T(8,128)(2,1)} %param.7) | copy-start | bytes 1204228
  8.8 94.7 %all-gather.2.cloned.1.call-start = ((), (), s32[]{:S(2)}) async-start(), calls=%async_computation.4 | async-start | bytes 13647872 | tf_op jit(solution)/shard_map/all_gather | solution.py:23
  103.5 4.7 %copy-start.4 = (bf16[1,112,1792]{2,1,0:T(8,128)(2,1)}, bf16[1,112,1792]{2,1,0:T(8,128)(2,1)S(1)}, u32[]{:S(2)}) copy-start(bf16[1,112,1792]{2,1,0:T(8,128)(2,1)S(1)} %fusion.43) | copy-start | bytes 1204228
  110.3 34.1 %all-to-all-start.1 = ((bf16[2,112,1792]{1,0,2:T(2,128)(2,1)}), bf16[2,112,1792]{1,0,2:T(2,128)(2,1)S(1)}, u32[]{:S(2)}, u32[]{:S(2)}) async-start(bf16[2,112,1792]{1,0,2:T(2,128)(2,1)} %copy.17), calls=%async_computation.1 | async-start | bytes 1835008 | tf_op jit(solution)/shard_map/all_to_all | solution.py:13
  145.8 6.5 %copy-start.5 = (bf16[2,1792,1792]{2,1,0:T(8,128)(2,1)S(1)}, bf16[2,1792,1792]{2,1,0:T(8,128)(2,1)}, u32[]{:S(2)}) copy-start(bf16[2,1792,1792]{2,1,0:T(8,128)(2,1)} %all-gather.2.cloned.1.call-done) | copy-start | bytes 38535172
Sparse Core Ops, SparseCore 0:
  12.6 89.6 reduce-scatter.3
Sparse Core Ops, SparseCore 1:
  11.8 84.3 all-gather.1

commit v4 on v3

--- a/solution.py
+++ b/solution.py
@@ -19,16 +19,19 @@
 
 def local(grad_parts, moment, second, left_basis, right_basis, block_steps):
     gradient = lax.psum_scatter(grad_parts[0], "dp", scatter_dimension=0, tiled=True)[0]
-    bases = jnp.concatenate([right_basis, left_basis], axis=0)
-    right_full, left_full = lax.all_gather(bases, "shard", axis=1, tiled=True)
+    right_full = lax.all_gather(right_basis[0], "shard", axis=0, tiled=True)
+    left_full = lax.all_gather(left_basis[0], "shard", axis=0, tiled=True)
     second_cols = to_cols(second[0].astype(bf16))
-    gradient, second_cols = lax.optimization_barrier((gradient, second_cols))
+    mom_right = jnp.dot(moment[0], right_full, preferred_element_type=f32).astype(bf16)
+    mom_cols = to_cols(mom_right)
+    gradient, second_cols, mom_cols = lax.optimization_barrier((gradient, second_cols, mom_cols))
 
     moment_new = (beta_one * moment[0].astype(f32) + (1.0 - beta_one) * gradient.astype(f32)).astype(bf16)
-    pair = jnp.stack([gradient, moment_new])
-    pair_right = jnp.einsum("nrk,kc->nrc", pair, right_full, preferred_element_type=f32).astype(bf16)
-    pair_cols = to_cols(pair_right)
-    rot_grad, rot_mom = jnp.einsum("ki,nkc->nic", left_full, pair_cols, preferred_element_type=f32)
+    grad_right = jnp.dot(gradient, right_full, preferred_element_type=f32).astype(bf16)
+    grad_cols = to_cols(grad_right)
+    pair_cols = jnp.stack([grad_cols, mom_cols])
+    rot_grad, rot_mom_old = jnp.einsum("ki,nkc->nic", left_full, pair_cols, preferred_element_type=f32)
+    rot_mom = beta_one * rot_mom_old + (1.0 - beta_one) * rot_grad
 
     second_new_cols = beta_two * second_cols.astype(f32) + (1.0 - beta_two) * rot_grad * rot_grad
     steps_float = block_steps[0].astype(f32)

time: 200 us -> 188 us (0.940)
  blocking collectives: 56.2 us -> 0 us
  waiting for transfers between devices: 89.3 us -> 111 us
  starting transfers between devices: 8.89 us -> 27.8 us
  matrix products: 17 us -> 20.6 us
    unnamed x3 -> x4, waiting for transfers between devices: 64.7 us -> 5.67 us
    all_to_all x2 -> x0, blocking collectives: 56.2 us -> none  [the longest x1 28.9 us: to_rows(): lax.all_to_all(cols, 'shard', split_axis=cols.ndim - 2, concat_axis=cols....]
    all_gather x1 -> x2, waiting for transfers between devices: 0.03 us -> 45.8 us  [the longest x1 45.8 us: local(): right_full = lax.all_gather(right_basis[0], 'shard', axis=0, tiled=True)]
    all_to_all x0 -> x1, waiting for transfers between devices: none -> 24.4 us  [to_rows(): lax.all_to_all(cols, 'shard', split_axis=cols.ndim - 2, concat_axis=cols....]
    all_to_all x1 -> x3, starting transfers between devices: 8.81 us -> 23.9 us  [to_cols(): lax.all_to_all(rows, 'shard', split_axis=rows.ndim - 1, concat_axis=rows....]
    all_to_all x1 -> x3, waiting for transfers between devices: 24.6 us -> 35.4 us  [to_cols(): lax.all_to_all(rows, 'shard', split_axis=rows.ndim - 1, concat_axis=rows....]
    all_to_all x0 -> x1, starting transfers between devices: none -> 3.76 us  [to_rows(): lax.all_to_all(cols, 'shard', split_axis=cols.ndim - 2, concat_axis=cols....]
    dot_general x1 -> x2, matrix products: 4.69 us -> 8.18 us  [the longest x1 4.2 us: local(): jnp.dot(gradient, right_full, preferred_element_type=f32).astype(bf16)]
  transfers between devices with their start and end apart: 3 -> 7, of which waited for: 2 -> 5; matrix products, arithmetic and copies ran while one was open for 1% -> 7% of each run, Pallas kernels for 0% -> 0%
where the time goes in v4:
time: 188 us; the launch traced here: 187 us
  waiting for transfers between devices  111 us (59%)
  starting transfers between devices  27.8 us (15%)
  matrix products  20.6 us (11%)
  between operations  16.4 us (9%)
  local copies, waits for them, and re-layouts  8.79 us (5%)
  other arithmetic  2.16 us (1%)
    all_gather x1, waiting for transfers between devices, local(): right_full = lax.all_gather(right_basis[0], 'shard', axis=0, tiled=True)  45.8 us
    all_to_all x3, waiting for transfers between devices, to_cols(): lax.all_to_all(rows, 'shard', split_axis=rows.ndim - 1, concat_axis=rows....  35.4 us
    all_to_all x1, waiting for transfers between devices, to_rows(): lax.all_to_all(cols, 'shard', split_axis=cols.ndim - 2, concat_axis=cols....  24.4 us
    all_to_all x3, starting transfers between devices, to_cols(): lax.all_to_all(rows, 'shard', split_axis=rows.ndim - 1, concat_axis=rows....  23.9 us
    dot_general x1, matrix products, local(): jnp.einsum('rc,kc->rk', left_dir_rows, right_full, preferred_element_type...  5.68 us
    unnamed x4, waiting for transfers between devices  5.67 us
    dot_general x1, matrix products, local(): jnp.einsum('ki,nkc->nic', left_full, pair_cols, preferred_element_type=f32)  4.61 us
    all_to_all x7, local copies, waits for them, and re-layouts, to_cols(): lax.all_to_all(rows, 'shard', split_axis=rows.ndim - 1, concat_axis=rows....  4.24 us
  transfers between devices with their start and end apart: 7, of which 5 were waited for; matrix products, arithmetic and copies ran while one was open for 7% of the time, Pallas kernels for 0%

profile of v4, /device:TPU:1, one launch (start us, length us, event | category | flops | bytes accessed | tf_op | source)
XLA Modules:
  0.0 187.1 jit_solution(15645008896976917468)
XLA Ops:
  8.1 0.7 all-gather.5.cloned.1.call-update
  9.4 0.7 all-gather.7.cloned.1.call-update
  10.1 1.0 copy.17
  11.1 10.0 %all-to-all-start = ((bf16[112,16,112]{0,2,1:T(8,128)(2,1)}), bf16[112,16,112]{0,2,1:T(8,128)(2,1)S(1)}, u32[]{:S(2)}, u32[]{:S(2)}) async-start(bf16[112,16,112]{0,2,1:T(8,128)(2,1)} %bitcast.3), calls=%async_computation | async-start | bytes 917504 | tf_op jit(solution)/shard_map/all_to_all | solution.py:13
  21.1 45.8 %all-gather.5.cloned.1.call-done = bf16[1,1792,1792]{2,1,0:T(8,128)(2,1)} async-done(((bf16[1,112,1792]{2,1,0:T(8,128)(2,1)}), bf16[1,1792,1792]{2,1,0:T(8,128)(2,1)}) %all-gather.5.cloned.1.call-update) | async-done | bytes 6422544 | tf_op jit(solution)/shard_map/all_gather | solution.py:22
  66.9 4.0 %fusion.13 = bf16[112,1792]{1,0:T(8,128)(2,1)S(1)} fusion(bf16[1,1792,1792]{2,1,0:T(8,128)(2,1)} %all-gather.5.cloned.1.call-done, bf16[1,112,1792]{2,1,0:T(8,128)(2,1)S(1)} %copy-done.1), kind=kOutput, calls=%fused_computation.11 | convolution fusion | flops 719523840 | bytes 7225344 | tf_op jit(solution)/shard_map/dot_general | solution.py:25
  70.9 0.8 all_to_all.52
  71.7 0.9 copy.19
  72.6 5.1 %all-to-all-start.1 = ((bf16[112,16,112]{2,0,1:T(8,128)(2,1)}), bf16[112,16,112]{2,0,1:T(8,128)(2,1)S(1)}, u32[]{:S(2)}, u32[]{:S(2)}) async-start(bf16[112,16,112]{2,0,1:T(8,128)(2,1)} %copy.19), calls=%async_computation.1 | async-start | bytes 917504 | tf_op jit(solution)/shard_map/all_to_all | solution.py:13
  78.3 19.6 %all-to-all-done.1 = bf16[112,16,112]{2,0,1:T(8,128)(2,1)S(1)} async-done(((bf16[112,16,112]{2,0,1:T(8,128)(2,1)}), bf16[112,16,112]{2,0,1:T(8,128)(2,1)S(1)}, u32[]{:S(2)}, u32[]{:S(2)}) %all-to-all-start.1) | async-done | bytes 401440 | tf_op jit(solution)/shard_map/all_to_all | solution.py:13
  98.1 3.8 %reduce-scatter.4.cloned.1.call-done = bf16[1,112,1792]{2,1,0:T(8,128)(2,1)} async-done(((bf16[16,112,1792]{2,1,0:T(8,128)(2,1)}), bf16[1,112,1792]{2,1,0:T(8,128)(2,1)}) %reduce-scatter.4.cloned.1.call-update) | async-done | bytes 401424
  101.9 4.2 %fusion.16 = bf16[112,1792]{1,0:T(8,128)(2,1)S(1)} fusion(bf16[112,1792]{1,0:T(8,128)(2,1)} %bitcast.90, bf16[1,1792,1792]{2,1,0:T(8,128)(2,1)} %all-gather.5.cloned.1.call-done), kind=kOutput, calls=%fused_computation.12 | convolution fusion | flops 719523840 | bytes 7225344 | tf_op jit(solution)/shard_map/dot_general | solution.py:30
  106.1 0.8 all_to_all.56
  106.9 0.9 copy.21
  107.8 8.9 %all-to-all-start.2 = ((bf16[112,16,112]{2,0,1:T(8,128)(2,1)}), bf16[112,16,112]{2,0,1:T(8,128)(2,1)S(1)}, u32[]{:S(2)}, u32[]{:S(2)}) async-start(bf16[112,16,112]{2,0,1:T(8,128)(2,1)} %copy.21), calls=%async_computation.2 | async-start | bytes 917504 | tf_op jit(solution)/shard_map/all_to_all | solution.py:13
  117.5 15.8 %all-to-all-done.2 = bf16[112,16,112]{2,0,1:T(8,128)(2,1)S(1)} async-done(((bf16[112,16,112]{2,0,1:T(8,128)(2,1)}), bf16[112,16,112]{2,0,1:T(8,128)(2,1)S(1)}, u32[]{:S(2)}, u32[]{:S(2)}) %all-to-all-start.2) | async-done | bytes 401440 | tf_op jit(solution)/shard_map/all_to_all | solution.py:13
  133.5 4.6 %fusion.10 = f32[2,1792,112]{1,2,0:T(8,128)S(1)} fusion(bf16[1,1792,1792]{2,1,0:T(8,128)(2,1)} %all-gather.7.cloned.1.call-done, bf16[1,1792,112]{1,2,0:T(8,128)(2,1)S(1)} %bitcast.92, bf16[1,1792,112]{1,2,0:T(8,128)(2,1)S(1)} %copy.26), kind=kOutput, calls=%fused_computation.10 | convolution fusion | flops 1439047680 | bytes 8830976 | tf_op jit(solution)/shard_map/ki,nkc->nic/dot_general | solution.py:33
  138.2 2.1 %fusion.25 = bf16[1,1792,112]{1,2,0:T(8,128)(2,1)S(1)} fusion(bf16[1,1792,1792]{2,1,0:T(8,128)(2,1)S(1)} %copy-done.3, bf16[1792,112]{0,1:T(8,128)(2,1)S(1)} %all_to_all.51, f32[2,1792,112]{1,2,0:T(8,128)S(1)} %fusion.10, f32[]{:T(128)} %bitcast.18, f32[]{:T(128)} %bitcast.17), kind=kOutput, calls=%fused_computation.15 | convolution fusion | flops 722132992 | bytes 8830984 | tf_op jit(solution)/shard_map/dot_general | solution.py:41
  140.4 2.0 %copy.23 = bf16[2,1792,112]{2,0,1:T(2,128)(2,1)} copy(bf16[2,1792,112]{1,2,0:T(8,128)(2,1)S(1)} %pad_maximum_fusion) | data formatting | bytes 1605632 | tf_op jit(solution)/shard_map/stack | solution.py:43
  142.4 3.8 %all-to-all-start.3 = ((bf16[2,1792,112]{2,0,1:T(2,128)(2,1)}), bf16[2,1792,112]{2,0,1:T(2,128)(2,1)S(1)}, u32[]{:S(2)}, u32[]{:S(2)}) async-start(bf16[2,1792,112]{2,0,1:T(2,128)(2,1)} %copy.23), calls=%async_computation.3 | async-start | bytes 1835008 | tf_op jit(solution)/shard_map/all_to_all | solution.py:17
  146.2 0.9 fusion.45
  147.1 24.4 %all-to-all-done.3 = bf16[2,1792,112]{2,0,1:T(2,128)(2,1)S(1)} async-done(((bf16[2,1792,112]{2,0,1:T(2,128)(2,1)}), bf16[2,1792,112]{2,0,1:T(2,128)(2,1)S(1)}, u32[]{:S(2)}, u32[]{:S(2)}) %all-to-all-start.3) | async-done | bytes 802848 | tf_op jit(solution)/shard_map/all_to_all | solution.py:17
  172.4 1.0 fusion.37
  174.0 5.7 %fusion.28 = bf16[1,112,1792]{2,1,0:T(8,128)(2,1)} fusion(bf16[112,1792]{1,0:T(8,128)(2,1)S(1)} %unstack.25, bf16[1,1792,1792]{2,1,0:T(8,128)(2,1)} %all-gather.5.cloned.1.call-done), kind=kOutput, calls=%fused_computation.16 | convolution fusion | flops 719523840 | bytes 7225344 | tf_op jit(solution)/shard_map/rc,kc->rk/dot_general | solution.py:46
  (25 shorter events, 3.3 us)
Async XLA Ops:
  8.0 2.1 %copy-start = (f32[1,112,1792]{2,1,0:T(8,128)S(1)}, f32[1,112,1792]{2,1,0:T(8,128)}, u32[]{:S(2)}) copy-start(f32[1,112,1792]{2,1,0:T(8,128)} %param.8) | copy-start | bytes 2408452
  8.0 58.9 %copy-start.1 = (bf16[1,112,1792]{2,1,0:T(8,128)(2,1)S(1)}, bf16[1,112,1792]{2,1,0:T(8,128)(2,1)}, u32[]{:S(2)}) copy-start(bf16[1,112,1792]{2,1,0:T(8,128)(2,1)} %param.7) | copy-start | bytes 1204228
  8.0 58.9 %all-gather.5.cloned.1.call-start = ((), (), s32[]{:S(2)}) async-start(), calls=%async_computation.5 | async-start | bytes 6823936 | tf_op jit(solution)/shard_map/all_gather | solution.py:22
  8.8 93.2 %reduce-scatter.4.cloned.1.call-start = ((), (), s32[]{:S(2)}) async-start(), calls=%async_computation.7 | async-start | bytes 6823936
  9.3 124.2 %all-gather.7.cloned.1.call-start = ((), (), s32[]{:S(2)}) async-start(), calls=%async_computation.6 | async-start | bytes 6823936 | tf_op jit(solution)/shard_map/all_gather | solution.py:23
  11.1 61.5 %all-to-all-start = ((bf16[112,16,112]{0,2,1:T(8,128)(2,1)}), bf16[112,16,112]{0,2,1:T(8,128)(2,1)S(1)}, u32[]{:S(2)}, u32[]{:S(2)}) async-start(bf16[112,16,112]{0,2,1:T(8,128)(2,1)} %bitcast.3), calls=%async_computation | async-start | bytes 917504 | tf_op jit(solution)/shard_map/all_to_all | solution.py:13
  72.6 25.3 %all-to-all-start.1 = ((bf16[112,16,112]{2,0,1:T(8,128)(2,1)}), bf16[112,16,112]{2,0,1:T(8,128)(2,1)S(1)}, u32[]{:S(2)}, u32[]{:S(2)}) async-start(bf16[112,16,112]{2,0,1:T(8,128)(2,1)} %copy.19), calls=%async_computation.1 | async-start | bytes 917504 | tf_op jit(solution)/shard_map/all_to_all | solution.py:13
  107.8 25.4 %all-to-all-start.2 = ((bf16[112,16,112]{2,0,1:T(8,128)(2,1)}), bf16[112,16,112]{2,0,1:T(8,128)(2,1)S(1)}, u32[]{:S(2)}, u32[]{:S(2)}) async-start(bf16[112,16,112]{2,0,1:T(8,128)(2,1)} %copy.21), calls=%async_computation.2 | async-start | bytes 917504 | tf_op jit(solution)/shard_map/all_to_all | solution.py:13
  133.5 4.7 %copy-start.3 = (bf16[1,1792,1792]{2,1,0:T(8,128)(2,1)S(1)}, bf16[1,1792,1792]{2,1,0:T(8,128)(2,1)}, u32[]{:S(2)}) copy-start(bf16[1,1792,1792]{2,1,0:T(8,128)(2,1)} %all-gather.7.cloned.1.call-done) | copy-start | bytes 19267588
  138.2 8.0 %copy-start.2 = (bf16[1,112,1792]{2,1,0:T(8,128)(2,1)S(1)}, bf16[1,112,1792]{2,1,0:T(8,128)(2,1)}, u32[]{:S(2)}) copy-start(bf16[1,112,1792]{2,1,0:T(8,128)(2,1)} %reduce-scatter.4.cloned.1.call-done) | copy-start | bytes 1204228
  142.4 29.1 %all-to-all-start.3 = ((bf16[2,1792,112]{2,0,1:T(2,128)(2,1)}), bf16[2,1792,112]{2,0,1:T(2,128)(2,1)S(1)}, u32[]{:S(2)}, u32[]{:S(2)}) async-start(bf16[2,1792,112]{2,0,1:T(2,128)(2,1)} %copy.23), calls=%async_computation.3 | async-start | bytes 1835008 | tf_op jit(solution)/shard_map/all_to_all | solution.py:17
Sparse Core Ops, SparseCore 0:
  10.8 56.0 all-gather.4
  68.9 57.6 all-gather.6
Sparse Core Ops, SparseCore 1:
  12.9 88.9 reduce-scatter.3

commit v5 on v4

v5 whole, which is shorter than its diff:
```python
import jax
import jax.numpy as jnp
from jax import lax
from jax.experimental import pallas as pl
from jax.experimental.pallas import tpu as pltpu
from jax.sharding import PartitionSpec as P

beta_one = 0.8
beta_two = 0.95
epsilon = 1e-08
f32, bf16 = jnp.float32, jnp.bfloat16
GROUP = 16
TILE = 256
VMEM_LIMIT = 48 * 2**20
by_rows = (((1,), (1,)), ((), ()))


def whole():
    return pl.BlockSpec(memory_space=pltpu.VMEM)


def spread(x_ref, out_ref, *lead):
    width = out_ref.shape[-1]
    for s in range(GROUP):
        out_ref[(s, *lead)] = x_ref[:, s * width : (s + 1) * width].astype(out_ref.dtype)


def cut_kernel(x_ref, out_ref):
    spread(x_ref, out_ref)


def right_kernel(a_ref, right_ref, out_ref, x_ref):
    @pl.loop(0, x_ref.shape[1] // TILE)
    def _(t):
        tile = pl.ds(pl.multiple_of(t * TILE, TILE), TILE)
        x_ref[:, tile] = jnp.dot(a_ref[...], right_ref[:, tile], preferred_element_type=f32)

    spread(x_ref, out_ref)


def middle_kernel(fix_ref, grad_ref, mom_ref, second_ref, left_ref, out_ref, pair_ref, second_t, rot_ref, dir_ref, back_ref):
    width = grad_ref.shape[1]
    pair_ref[:width] = grad_ref[...].astype(f32).T.astype(bf16)
    pair_ref[width:] = mom_ref[...].astype(f32).T.astype(bf16)
    second_t[...] = second_ref[...].astype(f32).T

    @pl.loop(0, rot_ref.shape[1] // TILE)
    def _(t):
        tile = pl.ds(pl.multiple_of(t * TILE, TILE), TILE)
        both = jnp.dot(pair_ref[...], left_ref[:, tile], preferred_element_type=f32)
        rot_grad = both[:width]
        rot_mom = beta_one * both[width:] + (1.0 - beta_one) * rot_grad
        rot_ref[:, tile] = rot_grad
        second_new = beta_two * second_t[:, tile] + (1.0 - beta_two) * rot_grad * rot_grad
        direction = rot_mom / fix_ref[0] / (jnp.sqrt(second_new / fix_ref[1]) + epsilon)
        dir_ref[:, tile] = direction.astype(bf16)

    @pl.loop(0, rot_ref.shape[1] // TILE)
    def _(t):
        tile = pl.ds(pl.multiple_of(t * TILE, TILE), TILE)
        back_ref[:, tile] = lax.dot_general(dir_ref[...], left_ref[tile, :], by_rows, preferred_element_type=f32)

    spread(rot_ref, out_ref, 0)
    spread(back_ref, out_ref, 1)


def last_kernel(in_ref, second_ref, right_ref, second_out, update_out, rows_ref):
    columns = second_ref.shape[1]
    width = in_ref.shape[-1]
    rot_grad = in_ref[:, 0].reshape(columns, width).astype(f32).T
    second_out[...] = beta_two * second_ref[...] + (1.0 - beta_two) * rot_grad * rot_grad
    rows_ref[...] = in_ref[:, 1].reshape(columns, width).astype(f32).T.astype(bf16)

    @pl.loop(0, columns // TILE)
    def _(t):
        tile = pl.ds(pl.multiple_of(t * TILE, TILE), TILE)
        update_out[:, tile] = lax.dot_general(rows_ref[...], right_ref[tile, :], by_rows, preferred_element_type=f32).astype(bf16)


def call(kernel, out_shape, in_specs, scratch, flops, moved):
    return pl.pallas_call(
        kernel,
        out_shape=out_shape,
        in_specs=in_specs,
        out_specs=jax.tree.map(lambda _: whole(), out_shape),
        scratch_shapes=scratch,
        compiler_params=pltpu.CompilerParams(vmem_limit_bytes=VMEM_LIMIT),
        cost_estimate=pl.CostEstimate(flops=flops, bytes_accessed=moved, transcendentals=0),
    )


def swap(pieces):
    return lax.all_to_all(pieces, "shard", split_axis=0, concat_axis=0, tiled=True)


def local(grad_parts, moment, second, left_basis, right_basis, block_steps):
    rows, columns = moment.shape[1:]
    product = 2 * rows * columns * columns
    basis_bytes = 2 * columns * columns
    pieces = jax.ShapeDtypeStruct((GROUP, rows, rows), bf16)
    times_right = call(right_kernel, pieces, [whole()] * 2, [pltpu.VMEM((rows, columns), f32)], product, basis_bytes)

    gradient = lax.psum_scatter(grad_parts[0], "dp", scatter_dimension=0, tiled=True)[0]
    right_full = lax.all_gather(right_basis[0], "shard", axis=0, tiled=True)
    left_full = lax.all_gather(left_basis[0], "shard", axis=0, tiled=True)
    second_cols = swap(call(cut_kernel, pieces, [whole()], [], 0, 6 * rows * columns)(second[0]))
    mom_cols = swap(times_right(moment[0], right_full))
    gradient, second_cols, mom_cols = lax.optimization_barrier((gradient, second_cols, mom_cols))

    moment_new = (beta_one * moment[0].astype(f32) + (1.0 - beta_one) * gradient.astype(f32)).astype(bf16)
    grad_cols = swap(times_right(gradient, right_full))

    steps_float = block_steps[0].astype(f32)
    fixes = jnp.stack([1.0 - jnp.power(f32(beta_one), steps_float), 1.0 - jnp.power(f32(beta_two), steps_float)])
    flat = [cols.reshape(columns, rows) for cols in (grad_cols, mom_cols, second_cols)]
    scratch = [
        pltpu.VMEM((2 * rows, columns), bf16),
        pltpu.VMEM((rows, columns), f32),
        pltpu.VMEM((rows, columns), f32),
        pltpu.VMEM((rows, columns), bf16),
        pltpu.VMEM((rows, columns), f32),
    ]
    both = jax.ShapeDtypeStruct((GROUP, 2, rows, rows), bf16)
    specs = [pl.BlockSpec(memory_space=pltpu.SMEM)] + [whole()] * 4
    sent = call(middle_kernel, both, specs, scratch, 3 * product, basis_bytes)(fixes, *flat, left_full)

    got = swap(sent)
    outs = (jax.ShapeDtypeStruct((rows, columns), f32), jax.ShapeDtypeStruct((rows, columns), bf16))
    scratch = [pltpu.VMEM((rows, columns), bf16)]
    second_new, update = call(last_kernel, outs, [whole()] * 3, scratch, product, basis_bytes)(got, second[0], right_full)
    return (moment_new[None], second_new[None], update[None])


def solution(mesh):
    return jax.shard_map(
        local,
        mesh=mesh,
        in_specs=(
            P("dp", None, "shard", None),
            P("dp", "shard", None),
            P("dp", "shard", None),
            P("dp", "shard", None),
            P("dp", "shard", None),
            P("dp"),
        ),
        out_specs=(P("dp", "shard", None), P("dp", "shard", None), P("dp", "shard", None)),
        check_vma=False,
    )
```

time: 188 us -> 188 us (level)
  Pallas kernels: 0 us -> 30.3 us
  blocking collectives: 0 us -> 24.9 us
  matrix products: 20.6 us -> 0 us
  waiting for transfers between devices: 111 us -> 91.4 us
  local copies, waits for them, and re-layouts: 8.79 us -> 1.05 us
  starting transfers between devices: 27.8 us -> 22.5 us
    pallas_call x0 -> x5, Pallas kernels: none -> 30.3 us  [the longest x1 10.9 us: local(): call(middle_kernel, both, specs, scratch, 3 * product, basis_bytes)]
    all_to_all x4 -> x3, waiting for transfers between devices: 59.9 us -> 34.8 us  [swap(): lax.all_to_all(pieces, 'shard', split_axis=0, concat_axis=0, tiled=True)]
    all_to_all x0 -> x1, blocking collectives: none -> 24.9 us  [swap(): lax.all_to_all(pieces, 'shard', split_axis=0, concat_axis=0, tiled=True)]
    dot_general x5 -> x0, matrix products: 20.6 us -> none  [the longest x1 5.68 us: local(): jnp.einsum('rc,kc->rk', left_dir_rows, right_full, preferred_element_type...]
    all_to_all x4 -> x3, starting transfers between devices: 27.7 us -> 22.4 us  [swap(): lax.all_to_all(pieces, 'shard', split_axis=0, concat_axis=0, tiled=True)]
    all_to_all x8 -> x0, local copies, waits for them, and re-layouts: 4.6 us -> none  [the longest x7 4.24 us: to_cols(): lax.all_to_all(rows, 'shard', split_axis=rows.ndim - 1, concat_axis=rows....]
    all_gather x1, waiting for transfers between devices: 0.02 us -> 4.05 us  [local(): left_full = lax.all_gather(left_basis[0], 'shard', axis=0, tiled=True)]
    another operation x4 -> x0, local copies, waits for them, and re-layouts: 2.77 us -> none  [the longest x1 2.03 us: local(): jnp.stack([rot_grad.astype(bf16), left_dir])]
  transfers between devices with their start and end apart: 7 -> 6, of which waited for: 5 -> 5; matrix products, arithmetic and copies ran while one was open for 7% -> 1% of each run, Pallas kernels for 0% -> 7%
where the time goes in v5:
time: 188 us; the launch traced here: 187 us
  waiting for transfers between devices  91.4 us (49%)
  Pallas kernels  30.3 us (16%)
  blocking collectives  24.9 us (13%)
  starting transfers between devices  22.5 us (12%)
  between operations  16.3 us (9%)
    all_gather x1, waiting for transfers between devices, local(): right_full = lax.all_gather(right_basis[0], 'shard', axis=0, tiled=True)  45.8 us
    all_to_all x3, waiting for transfers between devices, swap(): lax.all_to_all(pieces, 'shard', split_axis=0, concat_axis=0, tiled=True)  34.8 us
    all_to_all x1, blocking collectives, swap(): lax.all_to_all(pieces, 'shard', split_axis=0, concat_axis=0, tiled=True)  24.9 us
    all_to_all x3, starting transfers between devices, swap(): lax.all_to_all(pieces, 'shard', split_axis=0, concat_axis=0, tiled=True)  22.4 us
    pallas_call x1, Pallas kernels, local(): call(middle_kernel, both, specs, scratch, 3 * product, basis_bytes)  10.9 us
    pallas_call x1, Pallas kernels, local(): call(last_kernel, outs, [whole()] * 3, scratch, product, basis_bytes)  7.02 us
    unnamed x4, waiting for transfers between devices  6.74 us
    pallas_call x1, Pallas kernels, local(): grad_cols = swap(times_right(gradient, right_full))  6.09 us
  transfers between devices with their start and end apart: 6, of which 5 were waited for; matrix products, arithmetic and copies ran while one was open for 1% of the time, Pallas kernels for 7%

profile of v5, /device:TPU:1, one launch (start us, length us, event | category | flops | bytes accessed | tf_op | source)
XLA Modules:
  0.0 187.5 jit_solution(14902138464159311184)
XLA Ops:
  8.0 0.0 all-gather.5.cloned.1.call-start
  8.1 0.7 all-gather.5.cloned.1.call-update
  8.8 0.0 reduce-scatter.4.cloned.1.call-start
  8.8 0.5 reduce-scatter.4.cloned.1.call-update
  9.3 0.0 all-gather.7.cloned.1.call-start
  9.4 0.7 all-gather.7.cloned.1.call-update
  10.1 1.0 shard_map.85
  11.1 10.0 %all-to-all-start = ((bf16[16,112,112]{2,1,0:T(8,128)(2,1)}), bf16[16,112,112]{2,1,0:T(8,128)(2,1)S(1)}, u32[]{:S(2)}, u32[]{:S(2)}) async-start(bf16[16,112,112]{2,1,0:T(8,128)(2,1)} %shard_map.85), calls=%async_computation | async-start | bytes 917504 | tf_op jit(solution)/shard_map/all_to_all | solution.py:93
  21.1 45.8 %all-gather.5.cloned.1.call-done = bf16[1,1792,1792]{2,1,0:T(8,128)(2,1)} async-done(((bf16[1,112,1792]{2,1,0:T(8,128)(2,1)}), bf16[1,1792,1792]{2,1,0:T(8,128)(2,1)}) %all-gather.5.cloned.1.call-update) | async-done | bytes 6422544 | tf_op jit(solution)/shard_map/all_gather | solution.py:104
  66.9 5.3 %shard_map.86 = bf16[16,112,112]{2,1,0:T(8,128)(2,1)S(1)} custom-call(bf16[112,1792]{1,0:T(8,128)(2,1)S(1)} %bitcast.20, bf16[1792,1792]{1,0:T(8,128)(2,1)} %bitcast.23), custom_call_target="tpu_custom_call" | custom-call | flops 719323136 | bytes 6422528 | tf_op jit(solution)/shard_map/pallas_call | solution.py:107
  72.2 0.0 all-to-all-done
  72.2 24.9 %all_to_all.20 = bf16[16,112,112]{2,1,0:T(8,128)(2,1)S(1)} all-to-all(bf16[16,112,112]{2,1,0:T(8,128)(2,1)S(1)} %shard_map.86), channel_id=1, replica_groups=mesh['dp'=16,'shard'=16] {'shard'}, dimensions={0} | all-to-all | bytes 802816 | tf_op jit(solution)/shard_map/all_to_all | solution.py:93
  97.1 4.8 %reduce-scatter.4.cloned.1.call-done = bf16[1,112,1792]{2,1,0:T(8,128)(2,1)} async-done(((bf16[16,112,1792]{2,1,0:T(8,128)(2,1)}), bf16[1,112,1792]{2,1,0:T(8,128)(2,1)}) %reduce-scatter.4.cloned.1.call-update) | async-done | bytes 401424
  101.9 1.0 copy-done.2
  103.0 6.1 %shard_map.87 = bf16[16,112,112]{2,1,0:T(8,128)(2,1)} custom-call(bf16[112,1792]{1,0:T(8,128)(2,1)S(1)} %bitcast.21, bf16[1792,1792]{1,0:T(8,128)(2,1)} %bitcast.24), custom_call_target="tpu_custom_call" | custom-call | flops 719323136 | bytes 6422528 | tf_op jit(solution)/shard_map/pallas_call | solution.py:111
  109.1 8.9 %all-to-all-start.2 = ((bf16[16,112,112]{2,1,0:T(8,128)(2,1)}), bf16[16,112,112]{2,1,0:T(8,128)(2,1)S(1)}, u32[]{:S(2)}, u32[]{:S(2)}) async-start(bf16[16,112,112]{2,1,0:T(8,128)(2,1)} %shard_map.87), calls=%async_computation.2 | async-start | bytes 917504 | tf_op jit(solution)/shard_map/all_to_all | solution.py:93
  118.7 0.1 pad_maximum_fusion.fix_ref
  118.8 4.1 %all-gather.7.cloned.1.call-done = bf16[1,1792,1792]{2,1,0:T(8,128)(2,1)} async-done(((bf16[1,112,1792]{2,1,0:T(8,128)(2,1)}), bf16[1,1792,1792]{2,1,0:T(8,128)(2,1)}) %all-gather.7.cloned.1.call-update) | async-done | bytes 6422544 | tf_op jit(solution)/shard_map/all_gather | solution.py:105
  122.8 11.0 %all-to-all-done.2 = bf16[16,112,112]{2,1,0:T(8,128)(2,1)S(1)} async-done(((bf16[16,112,112]{2,1,0:T(8,128)(2,1)}), bf16[16,112,112]{2,1,0:T(8,128)(2,1)S(1)}, u32[]{:S(2)}, u32[]{:S(2)}) %all-to-all-start.2) | async-done | bytes 401440 | tf_op jit(solution)/shard_map/all_to_all | solution.py:93
  133.9 10.9 %shard_map.88 = bf16[16,2,112,112]{3,2,1,0:T(8,128)(2,1)} custom-call(f32[2]{0:T(128)S(1)} %pad_maximum_fusion.fix_ref, bf16[1792,112]{1,0:T(8,128)(2,1)S(1)} %bitcast.19, bf16[1792,112]{1,0:T(8,128)(2,1)S(1)} %bitcast.18, bf16[1792,112]{1,0:T(8,128)(2,1)S(1)} %bitcast.17, bf16[1792,1792]{1,0:T(8,128)(2,1)} %bitcast.27), custom_call_target="tpu_custom_call" | custom-call | flops 2157969408 | bytes 6422528 | tf_op jit(solution)/shard_map/pallas_call | solution.py:125
  144.8 3.5 %all-to-all-start.3 = ((bf16[16,2,112,112]{3,2,1,0:T(8,128)(2,1)}), bf16[16,2,112,112]{3,2,1,0:T(8,128)(2,1)S(1)}, u32[]{:S(2)}, u32[]{:S(2)}) async-start(bf16[16,2,112,112]{3,2,1,0:T(8,128)(2,1)} %shard_map.88), calls=%async_computation.3 | async-start | bytes 1835008 | tf_op jit(solution)/shard_map/all_to_all | solution.py:93
  148.4 0.9 fusion
  149.3 23.8 %all-to-all-done.3.in_ref = bf16[16,2,112,112]{3,2,1,0:T(8,128)(2,1)S(1)} async-done(((bf16[16,2,112,112]{3,2,1,0:T(8,128)(2,1)}), bf16[16,2,112,112]{3,2,1,0:T(8,128)(2,1)S(1)}, u32[]{:S(2)}, u32[]{:S(2)}) %all-to-all-start.3) | async-done | bytes 802848 | tf_op jit(solution)/shard_map/all_to_all | solution.py:93
  173.0 7.0 %shard_map.89 = (f32[112,1792]{1,0:T(8,128)}, bf16[112,1792]{1,0:T(8,128)(2,1)}) custom-call(bf16[16,2,112,112]{3,2,1,0:T(8,128)(2,1)S(1)} %all-to-all-done.3.in_ref, f32[112,1792]{1,0:T(8,128)S(1)} %bitcast.16, bf16[1792,1792]{1,0:T(8,128)(2,1)} %bitcast.25), custom_call_target="tpu_custom_call" | custom-call | flops 719323136 | bytes 6422528 | tf_op jit(solution)/shard_map/pallas_call | solution.py:130
  (7 shorter events, 0.0 us)
Async XLA Ops:
  8.0 2.1 %copy-start = (f32[1,112,1792]{2,1,0:T(8,128)S(1)}, f32[1,112,1792]{2,1,0:T(8,128)}, u32[]{:S(2)}) copy-start(f32[1,112,1792]{2,1,0:T(8,128)} %param.8) | copy-start | bytes 2408452
  8.0 58.9 %copy-start.1 = (bf16[1,112,1792]{2,1,0:T(8,128)(2,1)S(1)}, bf16[1,112,1792]{2,1,0:T(8,128)(2,1)}, u32[]{:S(2)}) copy-start(bf16[1,112,1792]{2,1,0:T(8,128)(2,1)} %param.7) | copy-start | bytes 1204228
  8.0 58.9 %all-gather.5.cloned.1.call-start = ((), (), s32[]{:S(2)}) async-start(), calls=%async_computation.5 | async-start | bytes 6823936 | tf_op jit(solution)/shard_map/all_gather | solution.py:104
  8.8 93.2 %reduce-scatter.4.cloned.1.call-start = ((), (), s32[]{:S(2)}) async-start(), calls=%async_computation.7 | async-start | bytes 6823936
  9.3 113.5 %all-gather.7.cloned.1.call-start = ((), (), s32[]{:S(2)}) async-start(), calls=%async_computation.6 | async-start | bytes 6823936 | tf_op jit(solution)/shard_map/all_gather | solution.py:105
  11.1 61.1 %all-to-all-start = ((bf16[16,112,112]{2,1,0:T(8,128)(2,1)}), bf16[16,112,112]{2,1,0:T(8,128)(2,1)S(1)}, u32[]{:S(2)}, u32[]{:S(2)}) async-start(bf16[16,112,112]{2,1,0:T(8,128)(2,1)} %shard_map.85), calls=%async_computation | async-start | bytes 917504 | tf_op jit(solution)/shard_map/all_to_all | solution.py:93
  101.9 1.0 copy-start.2
  109.1 39.3 %copy-start.3 = (bf16[1,112,1792]{2,1,0:T(8,128)(2,1)S(1)}, bf16[1,112,1792]{2,1,0:T(8,128)(2,1)}, u32[]{:S(2)}) copy-start(bf16[1,112,1792]{2,1,0:T(8,128)(2,1)} %reduce-scatter.4.cloned.1.call-done) | copy-start | bytes 1204228
  109.1 24.8 %all-to-all-start.2 = ((bf16[16,112,112]{2,1,0:T(8,128)(2,1)}), bf16[16,112,112]{2,1,0:T(8,128)(2,1)S(1)}, u32[]{:S(2)}, u32[]{:S(2)}) async-start(bf16[16,112,112]{2,1,0:T(8,128)(2,1)} %shard_map.87), calls=%async_computation.2 | async-start | bytes 917504 | tf_op jit(solution)/shard_map/all_to_all | solution.py:93
  144.8 28.2 %all-to-all-start.3 = ((bf16[16,2,112,112]{3,2,1,0:T(8,128)(2,1)}), bf16[16,2,112,112]{3,2,1,0:T(8,128)(2,1)S(1)}, u32[]{:S(2)}, u32[]{:S(2)}) async-start(bf16[16,2,112,112]{3,2,1,0:T(8,128)(2,1)} %shard_map.88), calls=%async_computation.3 | async-start | bytes 1835008 | tf_op jit(solution)/shard_map/all_to_all | solution.py:93
Sparse Core Ops, SparseCore 0:
  10.8 56.0 all-gather.4
  68.9 53.9 all-gather.6
Sparse Core Ops, SparseCore 1:
  12.9 88.9 reduce-scatter.3

commit v6 on v5

v6 whole, which is shorter than its diff:
```python
import jax
import jax.numpy as jnp
from jax import lax
from jax.experimental import pallas as pl
from jax.experimental.pallas import tpu as pltpu
from jax.sharding import PartitionSpec as P

beta_one = 0.8
beta_two = 0.95
epsilon = 1e-08
f32, bf16 = jnp.float32, jnp.bfloat16
GROUP = 16
TILE = 256
VMEM_LIMIT = 48 * 2**20
by_rows = (((1,), (1,)), ((), ()))


def whole():
    return pl.BlockSpec(memory_space=pltpu.VMEM)


def spread(x_ref, out_ref, *lead):
    width = out_ref.shape[-1]
    for s in range(GROUP):
        out_ref[(s, *lead)] = x_ref[:, s * width : (s + 1) * width].astype(out_ref.dtype)


def fetch(basis_ref, held, sems, by_column):
    copies = []
    for t in range(basis_ref.shape[0] // TILE):
        tile = pl.ds(t * TILE, TILE)
        spot = (slice(None), tile) if by_column else (tile, slice(None))
        copies.append(pltpu.make_async_copy(basis_ref.at[spot], held.at[spot], sems.at[t]))
        copies[-1].start()
    return copies


def cut_kernel(x_ref, out_ref):
    spread(x_ref, out_ref)


def turn_kernel(x_ref, out_ref):
    out_ref[...] = x_ref[...].astype(f32).T.astype(bf16)


def right_kernel(a_ref, right_ref, out_ref, x_ref, held, sems):
    for t, copy in enumerate(fetch(right_ref, held, sems, True)):
        copy.wait()
        tile = slice(t * TILE, (t + 1) * TILE)
        x_ref[:, tile] = jnp.dot(a_ref[...], held[:, tile], preferred_element_type=f32)
    spread(x_ref, out_ref)


def moment_kernel(cols_ref, left_ref, out_ref, held, sems):
    copies = fetch(left_ref, held, sems, True)
    x = cols_ref[...].astype(f32).T.astype(bf16)
    for t, copy in enumerate(copies):
        copy.wait()
        tile = slice(t * TILE, (t + 1) * TILE)
        out_ref[:, tile] = jnp.dot(x, held[:, tile], preferred_element_type=f32)


def middle_kernel(fix_ref, cols_ref, mom_ref, second_ref, left_ref, out_ref, rot_ref, dir_ref, back_ref, held, sems):
    copies = fetch(left_ref, held, sems, True)
    x = cols_ref[...].astype(f32).T.astype(bf16)
    for t, copy in enumerate(copies):
        copy.wait()
        tile = slice(t * TILE, (t + 1) * TILE)
        rot_grad = jnp.dot(x, held[:, tile], preferred_element_type=f32)
        rot_ref[:, tile] = rot_grad
        rot_mom = beta_one * mom_ref[:, tile] + (1.0 - beta_one) * rot_grad
        second_new = beta_two * second_ref[:, tile].astype(f32) + (1.0 - beta_two) * rot_grad * rot_grad
        direction = rot_mom * fix_ref[0] / (jnp.sqrt(second_new * fix_ref[1]) + epsilon)
        dir_ref[:, tile] = direction.astype(bf16)
    spread(rot_ref, out_ref, 0)
    for t in range(len(copies)):
        tile = slice(t * TILE, (t + 1) * TILE)
        back_ref[:, tile] = lax.dot_general(dir_ref[...], held[tile, :], by_rows, preferred_element_type=f32)
    spread(back_ref, out_ref, 1)


def last_kernel(in_ref, second_ref, right_ref, second_out, update_out, held, sems):
    copies = fetch(right_ref, held, sems, False)
    columns = second_ref.shape[1]
    width = in_ref.shape[-1]
    rows = in_ref[:, 1].reshape(columns, width).astype(f32).T.astype(bf16)
    for t, copy in enumerate(copies):
        copy.wait()
        tile = slice(t * TILE, (t + 1) * TILE)
        update_out[:, tile] = lax.dot_general(rows, held[tile, :], by_rows, preferred_element_type=f32).astype(bf16)
    rot_grad = in_ref[:, 0].reshape(columns, width).astype(f32).T
    second_out[...] = beta_two * second_ref[...] + (1.0 - beta_two) * rot_grad * rot_grad


def call(kernel, out_shape, in_specs, scratch, flops, moved):
    return pl.pallas_call(
        kernel,
        out_shape=out_shape,
        in_specs=in_specs,
        out_specs=jax.tree.map(lambda _: whole(), out_shape),
        scratch_shapes=scratch,
        compiler_params=pltpu.CompilerParams(vmem_limit_bytes=VMEM_LIMIT),
        cost_estimate=pl.CostEstimate(flops=flops, bytes_accessed=moved, transcendentals=0),
    )


def swap(pieces):
    return lax.all_to_all(pieces, "shard", split_axis=0, concat_axis=0, tiled=True)


def local(grad_parts, moment, second, left_basis, right_basis, block_steps):
    rows, columns = moment.shape[1:]
    product = 2 * rows * columns * columns
    basis_bytes = 2 * columns * columns
    apart = pl.BlockSpec(memory_space=pl.ANY)
    narrow = pltpu.VMEM((rows, columns), bf16)
    wide = pltpu.VMEM((rows, columns), f32)
    basis = [pltpu.VMEM((columns, columns), bf16), pltpu.SemaphoreType.DMA((columns // TILE,))]
    pieces = jax.ShapeDtypeStruct((GROUP, rows, rows), bf16)
    turned = jax.ShapeDtypeStruct((rows, columns), bf16)
    summed = jax.ShapeDtypeStruct((rows, columns), f32)
    times_right = call(right_kernel, pieces, [whole(), apart], [wide, *basis], product, basis_bytes)

    gradient = lax.psum_scatter(grad_parts[0], "dp", scatter_dimension=0, tiled=True)[0]
    right_full = lax.all_gather(right_basis[0], "shard", axis=0, tiled=True)
    left_full = lax.all_gather(left_basis[0], "shard", axis=0, tiled=True)
    second_cols = swap(call(cut_kernel, pieces, [whole()], [], 0, 6 * rows * columns)(second[0]))
    second_turned = call(turn_kernel, turned, [whole()], [], 0, 4 * rows * columns)(second_cols.reshape(columns, rows))
    mom_cols = swap(times_right(moment[0], right_full))
    gradient, second_turned, mom_cols = lax.optimization_barrier((gradient, second_turned, mom_cols))

    moment_new = (beta_one * moment[0].astype(f32) + (1.0 - beta_one) * gradient.astype(f32)).astype(bf16)
    grad_cols = swap(times_right(gradient, right_full))
    times_left = call(moment_kernel, summed, [whole(), apart], basis, product, basis_bytes)
    rot_mom_old = times_left(mom_cols.reshape(columns, rows), left_full)

    steps_float = block_steps[0].astype(f32)
    fixes = 1.0 / jnp.stack([1.0 - jnp.power(f32(beta_one), steps_float), 1.0 - jnp.power(f32(beta_two), steps_float)])
    both = jax.ShapeDtypeStruct((GROUP, 2, rows, rows), bf16)
    specs = [pl.BlockSpec(memory_space=pltpu.SMEM), whole(), whole(), whole(), apart]
    middle = call(middle_kernel, both, specs, [wide, narrow, wide, *basis], 2 * product, basis_bytes)
    sent = middle(fixes, grad_cols.reshape(columns, rows), rot_mom_old, second_turned, left_full)

    got = swap(sent)
    last = call(last_kernel, (summed, turned), [whole(), whole(), apart], basis, product, basis_bytes)
    second_new, update = last(got, second[0], right_full)
    return (moment_new[None], second_new[None], update[None])


def solution(mesh):
    return jax.shard_map(
        local,
        mesh=mesh,
        in_specs=(
            P("dp", None, "shard", None),
            P("dp", "shard", None),
            P("dp", "shard", None),
            P("dp", "shard", None),
            P("dp", "shard", None),
            P("dp"),
        ),
        out_specs=(P("dp", "shard", None), P("dp", "shard", None), P("dp", "shard", None)),
        check_vma=False,
    )
```

time: 188 us -> 186 us (0.989); the launches traced: 187 us -> 182 us
  blocking collectives: 24.9 us -> 0 us
  waiting for transfers between devices: 91.4 us -> 108 us
  starting transfers between devices: 22.5 us -> 27.4 us
  Pallas kernels: 30.3 us -> 28.4 us
    all_to_all x1 -> x0, blocking collectives: 24.9 us -> none  [swap(): lax.all_to_all(pieces, 'shard', split_axis=0, concat_axis=0, tiled=True)]
    all_to_all x3 -> x4, waiting for transfers between devices: 34.8 us -> 47.4 us  [swap(): lax.all_to_all(pieces, 'shard', split_axis=0, concat_axis=0, tiled=True)]
    all_to_all x3 -> x4, starting transfers between devices: 22.4 us -> 27.3 us  [swap(): lax.all_to_all(pieces, 'shard', split_axis=0, concat_axis=0, tiled=True)]
    all_gather x1, waiting for transfers between devices: 4.05 us -> 6.99 us  [local(): left_full = lax.all_gather(left_basis[0], 'shard', axis=0, tiled=True)]
    pallas_call x2 -> x4, Pallas kernels: 17.9 us -> 17.9 us  [the longest x1 7.43 us: local(): middle(fixes, grad_cols.reshape(columns, rows), rot_mom_old, second_turne...]
  transfers between devices with their start and end apart: 6 -> 7, of which waited for: 5 -> 6; matrix products, arithmetic and copies ran while one was open for 1% -> 1% of each run, Pallas kernels for 7% -> 8%
where the time goes in v6:
time: 186 us; the launch traced here: 182 us
  waiting for transfers between devices  108 us (58%)
  Pallas kernels  28.4 us (15%)
  starting transfers between devices  27.4 us (15%)
  between operations  16.3 us (9%)
    all_to_all x4, waiting for transfers between devices, swap(): lax.all_to_all(pieces, 'shard', split_axis=0, concat_axis=0, tiled=True)  47.4 us
    all_gather x1, waiting for transfers between devices, local(): right_full = lax.all_gather(right_basis[0], 'shard', axis=0, tiled=True)  45.8 us
    all_to_all x4, starting transfers between devices, swap(): lax.all_to_all(pieces, 'shard', split_axis=0, concat_axis=0, tiled=True)  27.3 us
    unnamed x4, waiting for transfers between devices  7.7 us
    pallas_call x1, Pallas kernels, local(): middle(fixes, grad_cols.reshape(columns, rows), rot_mom_old, second_turne...  7.43 us
    all_gather x1, waiting for transfers between devices, local(): left_full = lax.all_gather(left_basis[0], 'shard', axis=0, tiled=True)  6.99 us
    pallas_call x1, Pallas kernels, local(): second_new, update = last(got, second[0], right_full)  6.48 us
    pallas_call x1, Pallas kernels, local(): mom_cols = swap(times_right(moment[0], right_full))  4.71 us
  transfers between devices with their start and end apart: 7, of which 6 were waited for; matrix products, arithmetic and copies ran while one was open for 1% of the time, Pallas kernels for 8%

profile of v6, /device:TPU:1, one launch (start us, length us, event | category | flops | bytes accessed | tf_op | source)
XLA Modules:
  0.0 182.1 jit_solution(12646147926270810519)
XLA Ops:
  8.1 0.7 all-gather.5.cloned.1.call-update
  8.8 0.0 reduce-scatter.4.cloned.1.call-start
  8.8 0.5 reduce-scatter.4.cloned.1.call-update
  9.4 0.7 all-gather.7.cloned.1.call-update
  10.1 1.1 shard_map.85
  11.2 10.0 %all-to-all-start = ((bf16[16,112,112]{2,1,0:T(8,128)(2,1)}), bf16[16,112,112]{2,1,0:T(8,128)(2,1)S(1)}, u32[]{:S(2)}, u32[]{:S(2)}) async-start(bf16[16,112,112]{2,1,0:T(8,128)(2,1)} %shard_map.85), calls=%async_computation | async-start | bytes 917504 | tf_op jit(solution)/shard_map/all_to_all | solution.py:108
  21.2 45.8 %all-gather.5.cloned.1.call-done = bf16[1,1792,1792]{2,1,0:T(8,128)(2,1)} async-done(((bf16[1,112,1792]{2,1,0:T(8,128)(2,1)}), bf16[1,1792,1792]{2,1,0:T(8,128)(2,1)}) %all-gather.5.cloned.1.call-update) | async-done | bytes 6422544 | tf_op jit(solution)/shard_map/all_gather | solution.py:125
  67.0 4.7 %shard_map.87 = bf16[16,112,112]{2,1,0:T(8,128)(2,1)} custom-call(bf16[112,1792]{1,0:T(8,128)(2,1)S(1)} %bitcast.20, bf16[1792,1792]{1,0:T(8,128)(2,1)} %bitcast.23), custom_call_target="tpu_custom_call" | custom-call | flops 719323136 | bytes 6422528 | tf_op jit(solution)/shard_map/pallas_call | solution.py:129
  71.7 4.9 %all-to-all-start.1 = ((bf16[16,112,112]{2,1,0:T(8,128)(2,1)}), bf16[16,112,112]{2,1,0:T(8,128)(2,1)S(1)}, u32[]{:S(2)}, u32[]{:S(2)}) async-start(bf16[16,112,112]{2,1,0:T(8,128)(2,1)} %shard_map.87), calls=%async_computation.1 | async-start | bytes 917504 | tf_op jit(solution)/shard_map/all_to_all | solution.py:108
  76.6 0.2 shard_map.86.second_ref
  76.8 19.3 %all-to-all-done.1 = bf16[16,112,112]{2,1,0:T(8,128)(2,1)S(1)} async-done(((bf16[16,112,112]{2,1,0:T(8,128)(2,1)}), bf16[16,112,112]{2,1,0:T(8,128)(2,1)S(1)}, u32[]{:S(2)}, u32[]{:S(2)}) %all-to-all-start.1) | async-done | bytes 401440 | tf_op jit(solution)/shard_map/all_to_all | solution.py:108
  96.1 5.8 %reduce-scatter.4.cloned.1.call-done = bf16[1,112,1792]{2,1,0:T(8,128)(2,1)} async-done(((bf16[16,112,1792]{2,1,0:T(8,128)(2,1)}), bf16[1,112,1792]{2,1,0:T(8,128)(2,1)}) %reduce-scatter.4.cloned.1.call-update) | async-done | bytes 401424
  101.9 1.0 copy-done.2
  102.9 4.7 %shard_map.88 = bf16[16,112,112]{2,1,0:T(8,128)(2,1)} custom-call(bf16[112,1792]{1,0:T(8,128)(2,1)S(1)} %bitcast.21, bf16[1792,1792]{1,0:T(8,128)(2,1)} %bitcast.24), custom_call_target="tpu_custom_call" | custom-call | flops 719323136 | bytes 6422528 | tf_op jit(solution)/shard_map/pallas_call | solution.py:133
  107.6 8.9 %all-to-all-start.2 = ((bf16[16,112,112]{2,1,0:T(8,128)(2,1)}), bf16[16,112,112]{2,1,0:T(8,128)(2,1)S(1)}, u32[]{:S(2)}, u32[]{:S(2)}) async-start(bf16[16,112,112]{2,1,0:T(8,128)(2,1)} %shard_map.88), calls=%async_computation.2 | async-start | bytes 917504 | tf_op jit(solution)/shard_map/all_to_all | solution.py:108
  117.3 0.1 maximum_divide_fusion.fix_ref
  117.3 7.0 %all-gather.7.cloned.1.call-done = bf16[1,1792,1792]{2,1,0:T(8,128)(2,1)} async-done(((bf16[1,112,1792]{2,1,0:T(8,128)(2,1)}), bf16[1,1792,1792]{2,1,0:T(8,128)(2,1)}) %all-gather.7.cloned.1.call-update) | async-done | bytes 6422544 | tf_op jit(solution)/shard_map/all_gather | solution.py:126
  124.3 3.8 %shard_map.89.mom_ref = f32[112,1792]{1,0:T(8,128)S(1)} custom-call(bf16[1792,112]{1,0:T(8,128)(2,1)S(1)} %bitcast.18, bf16[1792,1792]{1,0:T(8,128)(2,1)} %bitcast.26), custom_call_target="tpu_custom_call" | custom-call | flops 719323136 | bytes 6422528 | tf_op jit(solution)/shard_map/pallas_call | solution.py:135
  128.2 4.3 %all-to-all-done.2 = bf16[16,112,112]{2,1,0:T(8,128)(2,1)S(1)} async-done(((bf16[16,112,112]{2,1,0:T(8,128)(2,1)}), bf16[16,112,112]{2,1,0:T(8,128)(2,1)S(1)}, u32[]{:S(2)}, u32[]{:S(2)}) %all-to-all-start.2) | async-done | bytes 401440 | tf_op jit(solution)/shard_map/all_to_all | solution.py:108
  132.5 7.4 %shard_map.90 = bf16[16,2,112,112]{3,2,1,0:T(8,128)(2,1)} custom-call(f32[2]{0:T(128)S(1)} %maximum_divide_fusion.fix_ref, bf16[1792,112]{1,0:T(8,128)(2,1)S(1)} %bitcast.19, f32[112,1792]{1,0:T(8,128)S(1)} %shard_map.89.mom_ref, bf16[112,1792]{1,0:T(8,128)(2,1)S(1)} %shard_map.86.second_ref, bf16[1792,1792]{1,0:T(8,128)(2,1)} %bitcast.27), custom_call_target="tpu_custom_call" | custom-call | flops 1438646272 | bytes 6422528 | tf_op jit(solution)/shard_map/pallas_call | solution.py:142
  139.9 3.5 %all-to-all-start.3 = ((bf16[16,2,112,112]{3,2,1,0:T(8,128)(2,1)}), bf16[16,2,112,112]{3,2,1,0:T(8,128)(2,1)S(1)}, u32[]{:S(2)}, u32[]{:S(2)}) async-start(bf16[16,2,112,112]{3,2,1,0:T(8,128)(2,1)} %shard_map.90), calls=%async_computation.3 | async-start | bytes 1835008 | tf_op jit(solution)/shard_map/all_to_all | solution.py:108
  143.4 0.9 fusion
  144.3 23.8 %all-to-all-done.3.in_ref = bf16[16,2,112,112]{3,2,1,0:T(8,128)(2,1)S(1)} async-done(((bf16[16,2,112,112]{3,2,1,0:T(8,128)(2,1)}), bf16[16,2,112,112]{3,2,1,0:T(8,128)(2,1)S(1)}, u32[]{:S(2)}, u32[]{:S(2)}) %all-to-all-start.3) | async-done | bytes 802848 | tf_op jit(solution)/shard_map/all_to_all | solution.py:108
  168.2 6.5 %shard_map.91 = (f32[112,1792]{1,0:T(8,128)}, bf16[112,1792]{1,0:T(8,128)(2,1)}) custom-call(bf16[16,2,112,112]{3,2,1,0:T(8,128)(2,1)S(1)} %all-to-all-done.3.in_ref, f32[112,1792]{1,0:T(8,128)S(1)} %bitcast.16, bf16[1792,1792]{1,0:T(8,128)(2,1)} %bitcast.25), custom_call_target="tpu_custom_call" | custom-call | flops 719323136 | bytes 6422528 | tf_op jit(solution)/shard_map/pallas_call | solution.py:146
  (10 shorter events, 0.1 us)
Async XLA Ops:
  8.0 2.1 %copy-start = (f32[1,112,1792]{2,1,0:T(8,128)S(1)}, f32[1,112,1792]{2,1,0:T(8,128)}, u32[]{:S(2)}) copy-start(f32[1,112,1792]{2,1,0:T(8,128)} %param.8) | copy-start | bytes 2408452
  8.0 59.0 %copy-start.1 = (bf16[1,112,1792]{2,1,0:T(8,128)(2,1)S(1)}, bf16[1,112,1792]{2,1,0:T(8,128)(2,1)}, u32[]{:S(2)}) copy-start(bf16[1,112,1792]{2,1,0:T(8,128)(2,1)} %param.7) | copy-start | bytes 1204228
  8.0 58.9 %all-gather.5.cloned.1.call-start = ((), (), s32[]{:S(2)}) async-start(), calls=%async_computation.5 | async-start | bytes 6823936 | tf_op jit(solution)/shard_map/all_gather | solution.py:125
  8.8 93.2 %reduce-scatter.4.cloned.1.call-start = ((), (), s32[]{:S(2)}) async-start(), calls=%async_computation.7 | async-start | bytes 6823936
  9.3 115.0 %all-gather.7.cloned.1.call-start = ((), (), s32[]{:S(2)}) async-start(), calls=%async_computation.6 | async-start | bytes 6823936 | tf_op jit(solution)/shard_map/all_gather | solution.py:126
  11.2 60.5 %all-to-all-start = ((bf16[16,112,112]{2,1,0:T(8,128)(2,1)}), bf16[16,112,112]{2,1,0:T(8,128)(2,1)S(1)}, u32[]{:S(2)}, u32[]{:S(2)}) async-start(bf16[16,112,112]{2,1,0:T(8,128)(2,1)} %shard_map.85), calls=%async_computation | async-start | bytes 917504 | tf_op jit(solution)/shard_map/all_to_all | solution.py:108
  71.7 24.4 %all-to-all-start.1 = ((bf16[16,112,112]{2,1,0:T(8,128)(2,1)}), bf16[16,112,112]{2,1,0:T(8,128)(2,1)S(1)}, u32[]{:S(2)}, u32[]{:S(2)}) async-start(bf16[16,112,112]{2,1,0:T(8,128)(2,1)} %shard_map.87), calls=%async_computation.1 | async-start | bytes 917504 | tf_op jit(solution)/shard_map/all_to_all | solution.py:108
  101.9 1.0 copy-start.2
  107.6 24.8 %all-to-all-start.2 = ((bf16[16,112,112]{2,1,0:T(8,128)(2,1)}), bf16[16,112,112]{2,1,0:T(8,128)(2,1)S(1)}, u32[]{:S(2)}, u32[]{:S(2)}) async-start(bf16[16,112,112]{2,1,0:T(8,128)(2,1)} %shard_map.88), calls=%async_computation.2 | async-start | bytes 917504 | tf_op jit(solution)/shard_map/all_to_all | solution.py:108
  128.2 15.3 %copy-start.3 = (bf16[1,112,1792]{2,1,0:T(8,128)(2,1)S(1)}, bf16[1,112,1792]{2,1,0:T(8,128)(2,1)}, u32[]{:S(2)}) copy-start(bf16[1,112,1792]{2,1,0:T(8,128)(2,1)} %reduce-scatter.4.cloned.1.call-done) | copy-start | bytes 1204228
  139.9 28.3 %all-to-all-start.3 = ((bf16[16,2,112,112]{3,2,1,0:T(8,128)(2,1)}), bf16[16,2,112,112]{3,2,1,0:T(8,128)(2,1)S(1)}, u32[]{:S(2)}, u32[]{:S(2)}) async-start(bf16[16,2,112,112]{3,2,1,0:T(8,128)(2,1)} %shard_map.90), calls=%async_computation.3 | async-start | bytes 1835008 | tf_op jit(solution)/shard_map/all_to_all | solution.py:108
Sparse Core Ops, SparseCore 0:
  10.8 56.0 all-gather.4
  68.9 55.3 all-gather.6
Sparse Core Ops, SparseCore 1:
  12.9 88.9 reduce-scatter.3

commit v7 on v6

v7 whole, which is shorter than its diff:
```python
import jax
import jax.numpy as jnp
from jax import lax
from jax.experimental import pallas as pl
from jax.experimental.pallas import tpu as pltpu
from jax.sharding import PartitionSpec as P

beta_one = 0.8
beta_two = 0.95
epsilon = 1e-08
f32, bf16 = jnp.float32, jnp.bfloat16
GROUP = 16
TILE = 256
VMEM_LIMIT = 14 * 2**20
by_rows = (((1,), (1,)), ((), ()))


def whole():
    return pl.BlockSpec(memory_space=pltpu.VMEM)


def spread(x_ref, out_ref, *lead):
    width = out_ref.shape[-1]
    for s in range(GROUP):
        out_ref[(s, *lead)] = x_ref[:, s * width : (s + 1) * width].astype(out_ref.dtype)


def tiles(basis_ref):
    return [slice(start, start + TILE) for start in range(0, basis_ref.shape[0], TILE)]


def cut_kernel(x_ref, out_ref):
    spread(x_ref, out_ref)


def turn_kernel(x_ref, out_ref):
    out_ref[...] = x_ref[...].astype(f32).T.astype(bf16)


def right_kernel(a_ref, right_ref, out_ref, x_ref):
    for tile in tiles(right_ref):
        x_ref[:, tile] = jnp.dot(a_ref[...], right_ref[:, tile], preferred_element_type=f32)
    spread(x_ref, out_ref)


def moment_kernel(cols_ref, left_ref, out_ref):
    x = cols_ref[...].astype(f32).T.astype(bf16)
    for tile in tiles(left_ref):
        out_ref[:, tile] = jnp.dot(x, left_ref[:, tile], preferred_element_type=f32)


def middle_kernel(fix_ref, cols_ref, mom_ref, second_ref, left_ref, out_ref, rot_ref, dir_ref, back_ref):
    x = cols_ref[...].astype(f32).T.astype(bf16)
    for tile in tiles(left_ref):
        rot_grad = jnp.dot(x, left_ref[:, tile], preferred_element_type=f32)
        rot_ref[:, tile] = rot_grad
        rot_mom = beta_one * mom_ref[:, tile] + (1.0 - beta_one) * rot_grad
        second_new = beta_two * second_ref[:, tile].astype(f32) + (1.0 - beta_two) * rot_grad * rot_grad
        direction = rot_mom * fix_ref[0] / (jnp.sqrt(second_new * fix_ref[1]) + epsilon)
        dir_ref[:, tile] = direction.astype(bf16)
    spread(rot_ref, out_ref, 0)
    for tile in tiles(left_ref):
        back_ref[:, tile] = lax.dot_general(dir_ref[...], left_ref[tile, :], by_rows, preferred_element_type=f32)
    spread(back_ref, out_ref, 1)


def last_kernel(in_ref, second_ref, right_ref, second_out, update_out):
    columns = second_ref.shape[1]
    width = in_ref.shape[-1]
    rows = in_ref[:, 1].reshape(columns, width).astype(f32).T.astype(bf16)
    for tile in tiles(right_ref):
        update_out[:, tile] = lax.dot_general(rows, right_ref[tile, :], by_rows, preferred_element_type=f32).astype(bf16)
    rot_grad = in_ref[:, 0].reshape(columns, width).astype(f32).T
    second_out[...] = beta_two * second_ref[...] + (1.0 - beta_two) * rot_grad * rot_grad


def call(kernel, out_shape, in_specs, scratch, flops, moved):
    return pl.pallas_call(
        kernel,
        out_shape=out_shape,
        in_specs=in_specs,
        out_specs=jax.tree.map(lambda _: whole(), out_shape),
        scratch_shapes=scratch,
        compiler_params=pltpu.CompilerParams(vmem_limit_bytes=VMEM_LIMIT),
        cost_estimate=pl.CostEstimate(flops=flops, bytes_accessed=moved, transcendentals=0),
    )


def swap(pieces):
    return lax.all_to_all(pieces, "shard", split_axis=0, concat_axis=0, tiled=True)


def local(grad_parts, moment, second, left_basis, right_basis, block_steps):
    rows, columns = moment.shape[1:]
    product = 2 * rows * columns * columns
    basis_bytes = 2 * columns * columns
    narrow = pltpu.VMEM((rows, columns), bf16)
    wide = pltpu.VMEM((rows, columns), f32)
    pieces = jax.ShapeDtypeStruct((GROUP, rows, rows), bf16)
    turned = jax.ShapeDtypeStruct((rows, columns), bf16)
    summed = jax.ShapeDtypeStruct((rows, columns), f32)
    times_right = call(right_kernel, pieces, [whole(), whole()], [wide], product, basis_bytes)

    gradient = lax.psum_scatter(grad_parts[0], "dp", scatter_dimension=0, tiled=True)[0]
    right_full = lax.all_gather(right_basis[0], "shard", axis=0, tiled=True)
    left_full = lax.all_gather(left_basis[0], "shard", axis=0, tiled=True)
    second_cols = swap(call(cut_kernel, pieces, [whole()], [], 0, 6 * rows * columns)(second[0]))
    second_turned = call(turn_kernel, turned, [whole()], [], 0, 4 * rows * columns)(second_cols.reshape(columns, rows))
    mom_cols = swap(times_right(moment[0], right_full))
    gradient, second_turned, mom_cols = lax.optimization_barrier((gradient, second_turned, mom_cols))

    moment_new = (beta_one * moment[0].astype(f32) + (1.0 - beta_one) * gradient.astype(f32)).astype(bf16)
    grad_cols = swap(times_right(gradient, right_full))
    times_left = call(moment_kernel, summed, [whole()] * 2, [], product, basis_bytes)
    rot_mom_old = times_left(mom_cols.reshape(columns, rows), left_full)

    steps_float = block_steps[0].astype(f32)
    fixes = 1.0 / jnp.stack([1.0 - jnp.power(f32(beta_one), steps_float), 1.0 - jnp.power(f32(beta_two), steps_float)])
    both = jax.ShapeDtypeStruct((GROUP, 2, rows, rows), bf16)
    specs = [pl.BlockSpec(memory_space=pltpu.SMEM)] + [whole()] * 4
    middle = call(middle_kernel, both, specs, [wide, narrow, wide], 2 * product, basis_bytes)
    sent = middle(fixes, grad_cols.reshape(columns, rows), rot_mom_old, second_turned, left_full)

    got = swap(sent)
    last = call(last_kernel, (summed, turned), [whole()] * 3, [], product, basis_bytes)
    second_new, update = last(got, second[0], right_full)
    return (moment_new[None], second_new[None], update[None])


def solution(mesh):
    return jax.shard_map(
        local,
        mesh=mesh,
        in_specs=(
            P("dp", None, "shard", None),
            P("dp", "shard", None),
            P("dp", "shard", None),
            P("dp", "shard", None),
            P("dp", "shard", None),
            P("dp"),
        ),
        out_specs=(P("dp", "shard", None), P("dp", "shard", None), P("dp", "shard", None)),
        check_vma=False,
    )
```

time: 186 us -> 187 us (level)
  local copies, waits for them, and re-layouts: 1.02 us -> 16.3 us
  Pallas kernels: 28.4 us -> 14 us
    unnamed x8 -> x22, local copies, waits for them, and re-layouts: 1.02 us -> 16.3 us
    pallas_call x1, Pallas kernels: 6.48 us -> 3.15 us  [local(): second_new, update = last(got, second[0], right_full)]
    pallas_call x1, Pallas kernels: 4.71 us -> 1.88 us  [local(): mom_cols = swap(times_right(moment[0], right_full))]
    pallas_call x1, Pallas kernels: 3.84 us -> 1.03 us  [local(): rot_mom_old = times_left(mom_cols.reshape(columns, rows), left_full)]
    pallas_call x1, Pallas kernels: 4.69 us -> 1.96 us  [local(): grad_cols = swap(times_right(gradient, right_full))]
    pallas_call x1, Pallas kernels: 7.43 us -> 4.75 us  [local(): middle(fixes, grad_cols.reshape(columns, rows), rot_mom_old, second_turne...]
  transfers between devices with their start and end apart: 7 -> 7, of which waited for: 6 -> 6; matrix products, arithmetic and copies ran while one was open for 1% -> 1% of each run, Pallas kernels for 8% -> 3%
where the time goes in v7:
time: 187 us; the launch traced here: 183 us
  waiting for transfers between devices  108 us (58%)
  starting transfers between devices  27.6 us (15%)
  local copies, waits for them, and re-layouts  16.3 us (9%)
  between operations  16.3 us (9%)
  Pallas kernels  14 us (7%)
    all_to_all x4, waiting for transfers between devices, swap(): lax.all_to_all(pieces, 'shard', split_axis=0, concat_axis=0, tiled=True)  46.9 us
    all_gather x1, waiting for transfers between devices, local(): right_full = lax.all_gather(right_basis[0], 'shard', axis=0, tiled=True)  45.8 us
    all_to_all x4, starting transfers between devices, swap(): lax.all_to_all(pieces, 'shard', split_axis=0, concat_axis=0, tiled=True)  27.5 us
    unnamed x22, local copies, waits for them, and re-layouts  16.3 us
    all_gather x1, waiting for transfers between devices, local(): left_full = lax.all_gather(left_basis[0], 'shard', axis=0, tiled=True)  7.83 us
    unnamed x4, waiting for transfers between devices  7.23 us
    pallas_call x1, Pallas kernels, local(): middle(fixes, grad_cols.reshape(columns, rows), rot_mom_old, second_turne...  4.75 us
  transfers between devices with their start and end apart: 7, of which 6 were waited for; matrix products, arithmetic and copies ran while one was open for 1% of the time, Pallas kernels for 3%

profile of v7, /device:TPU:1, one launch (start us, length us, event | category | flops | bytes accessed | tf_op | source)
XLA Modules:
  0.0 183.0 jit_solution(17284187201746207711)
XLA Ops:
  10.1 1.1 shard_map.85
  11.2 10.0 %all-to-all-start = ((bf16[16,112,112]{2,1,0:T(8,128)(2,1)}), bf16[16,112,112]{2,1,0:T(8,128)(2,1)S(1)}, u32[]{:S(2)}, u32[]{:S(2)}) async-start(bf16[16,112,112]{2,1,0:T(8,128)(2,1)} %shard_map.85), calls=%async_computation | async-start | bytes 917504 | tf_op jit(solution)/shard_map/all_to_all | solution.py:90
  21.1 45.8 %all-gather.5.cloned.1.call-done = bf16[1,1792,1792]{2,1,0:T(8,128)(2,1)} async-done(((bf16[1,112,1792]{2,1,0:T(8,128)(2,1)}), bf16[1,1792,1792]{2,1,0:T(8,128)(2,1)}) %all-gather.5.cloned.1.call-update) | async-done | bytes 6422544 | tf_op jit(solution)/shard_map/all_gather | solution.py:105
  67.0 2.9 %copy-done = bf16[1,1792,1792]{2,1,0:T(8,128)(2,1)S(1)} copy-done((bf16[1,1792,1792]{2,1,0:T(8,128)(2,1)S(1)}, bf16[1,1792,1792]{2,1,0:T(8,128)(2,1)}, u32[]{:S(2)}) %copy-start) | copy-done | bytes 6422552
  69.9 1.9 %shard_map.87 = bf16[16,112,112]{2,1,0:T(8,128)(2,1)} custom-call(bf16[112,1792]{1,0:T(8,128)(2,1)S(1)} %bitcast.25, bf16[1792,1792]{1,0:T(8,128)(2,1)S(1)} %bitcast.15), custom_call_target="tpu_custom_call" | custom-call | flops 719323136 | bytes 6422528 | tf_op jit(solution)/shard_map/pallas_call | solution.py:109
  71.7 5.1 %all-to-all-start.1 = ((bf16[16,112,112]{2,1,0:T(8,128)(2,1)}), bf16[16,112,112]{2,1,0:T(8,128)(2,1)S(1)}, u32[]{:S(2)}, u32[]{:S(2)}) async-start(bf16[16,112,112]{2,1,0:T(8,128)(2,1)} %shard_map.87), calls=%async_computation.1 | async-start | bytes 917504 | tf_op jit(solution)/shard_map/all_to_all | solution.py:90
  77.0 19.6 %all-to-all-done.1 = bf16[16,112,112]{2,1,0:T(8,128)(2,1)S(1)} async-done(((bf16[16,112,112]{2,1,0:T(8,128)(2,1)}), bf16[16,112,112]{2,1,0:T(8,128)(2,1)S(1)}, u32[]{:S(2)}, u32[]{:S(2)}) %all-to-all-start.1) | async-done | bytes 401440 | tf_op jit(solution)/shard_map/all_to_all | solution.py:90
  96.6 5.3 %reduce-scatter.4.cloned.1.call-done = bf16[1,112,1792]{2,1,0:T(8,128)(2,1)} async-done(((bf16[16,112,1792]{2,1,0:T(8,128)(2,1)}), bf16[1,112,1792]{2,1,0:T(8,128)(2,1)}) %reduce-scatter.4.cloned.1.call-update) | async-done | bytes 401424
  101.9 2.9 %copy-done.1 = bf16[1,1792,1792]{2,1,0:T(8,128)(2,1)S(1)} copy-done((bf16[1,1792,1792]{2,1,0:T(8,128)(2,1)S(1)}, bf16[1,1792,1792]{2,1,0:T(8,128)(2,1)}, u32[]{:S(2)}) %copy-start.1) | copy-done | bytes 6422552
  104.9 1.0 copy-done.7
  105.9 2.0 %shard_map.88 = bf16[16,112,112]{2,1,0:T(8,128)(2,1)} custom-call(bf16[112,1792]{1,0:T(8,128)(2,1)S(1)} %bitcast.26, bf16[1792,1792]{1,0:T(8,128)(2,1)S(1)} %bitcast.16), custom_call_target="tpu_custom_call" | custom-call | flops 719323136 | bytes 6422528 | tf_op jit(solution)/shard_map/pallas_call | solution.py:113
  107.9 8.9 %all-to-all-start.2 = ((bf16[16,112,112]{2,1,0:T(8,128)(2,1)}), bf16[16,112,112]{2,1,0:T(8,128)(2,1)S(1)}, u32[]{:S(2)}, u32[]{:S(2)}) async-start(bf16[16,112,112]{2,1,0:T(8,128)(2,1)} %shard_map.88), calls=%async_computation.2 | async-start | bytes 917504 | tf_op jit(solution)/shard_map/all_to_all | solution.py:90
  117.5 7.8 %all-gather.7.cloned.1.call-done = bf16[1,1792,1792]{2,1,0:T(8,128)(2,1)} async-done(((bf16[1,112,1792]{2,1,0:T(8,128)(2,1)}), bf16[1,1792,1792]{2,1,0:T(8,128)(2,1)}) %all-gather.7.cloned.1.call-update) | async-done | bytes 6422544 | tf_op jit(solution)/shard_map/all_gather | solution.py:106
  125.4 2.8 %copy-done.3 = bf16[1,1792,1792]{2,1,0:T(8,128)(2,1)S(1)} copy-done((bf16[1,1792,1792]{2,1,0:T(8,128)(2,1)S(1)}, bf16[1,1792,1792]{2,1,0:T(8,128)(2,1)}, u32[]{:S(2)}) %copy-start.3) | copy-done | bytes 6422552
  128.2 1.0 shard_map.89.mom_ref
  129.2 3.5 %all-to-all-done.2 = bf16[16,112,112]{2,1,0:T(8,128)(2,1)S(1)} async-done(((bf16[16,112,112]{2,1,0:T(8,128)(2,1)}), bf16[16,112,112]{2,1,0:T(8,128)(2,1)S(1)}, u32[]{:S(2)}, u32[]{:S(2)}) %all-to-all-start.2) | async-done | bytes 401440 | tf_op jit(solution)/shard_map/all_to_all | solution.py:90
  132.7 2.8 %copy-done.4 = bf16[1,1792,1792]{2,1,0:T(8,128)(2,1)S(1)} copy-done((bf16[1,1792,1792]{2,1,0:T(8,128)(2,1)S(1)}, bf16[1,1792,1792]{2,1,0:T(8,128)(2,1)}, u32[]{:S(2)}) %copy-start.4) | copy-done | bytes 6422552
  135.5 1.0 copy-done.10
  136.5 4.7 %shard_map.90 = bf16[16,2,112,112]{3,2,1,0:T(8,128)(2,1)} custom-call(f32[2]{0:T(128)S(1)} %maximum_divide_fusion.fix_ref, bf16[1792,112]{1,0:T(8,128)(2,1)S(1)} %bitcast.24, f32[112,1792]{1,0:T(8,128)S(1)} %shard_map.89.mom_ref, bf16[112,1792]{1,0:T(8,128)(2,1)S(1)} %copy-done.10, bf16[1792,1792]{1,0:T(8,128)(2,1)S(1)} %bitcast.19), custom_call_target="tpu_custom_call" | custom-call | flops 1438646272 | bytes 6422528 | tf_op jit(solution)/shard_map/pallas_call | solution.py:122
  141.3 3.5 %all-to-all-start.3 = ((bf16[16,2,112,112]{3,2,1,0:T(8,128)(2,1)}), bf16[16,2,112,112]{3,2,1,0:T(8,128)(2,1)S(1)}, u32[]{:S(2)}, u32[]{:S(2)}) async-start(bf16[16,2,112,112]{3,2,1,0:T(8,128)(2,1)} %shard_map.90), calls=%async_computation.3 | async-start | bytes 1835008 | tf_op jit(solution)/shard_map/all_to_all | solution.py:90
  144.8 0.9 fusion
  145.7 23.9 %all-to-all-done.3.in_ref = bf16[16,2,112,112]{3,2,1,0:T(8,128)(2,1)S(1)} async-done(((bf16[16,2,112,112]{3,2,1,0:T(8,128)(2,1)}), bf16[16,2,112,112]{3,2,1,0:T(8,128)(2,1)S(1)}, u32[]{:S(2)}, u32[]{:S(2)}) %all-to-all-start.3) | async-done | bytes 802848 | tf_op jit(solution)/shard_map/all_to_all | solution.py:90
  169.6 2.8 %copy-done.2 = bf16[1,1792,1792]{2,1,0:T(8,128)(2,1)S(1)} copy-done((bf16[1,1792,1792]{2,1,0:T(8,128)(2,1)S(1)}, bf16[1,1792,1792]{2,1,0:T(8,128)(2,1)}, u32[]{:S(2)}) %copy-start.2) | copy-done | bytes 6422552
  172.4 3.2 %shard_map.91 = (f32[112,1792]{1,0:T(8,128)}, bf16[112,1792]{1,0:T(8,128)(2,1)}) custom-call(bf16[16,2,112,112]{3,2,1,0:T(8,128)(2,1)S(1)} %all-to-all-done.3.in_ref, f32[112,1792]{1,0:T(8,128)S(1)} %bitcast.21, bf16[1792,1792]{1,0:T(8,128)(2,1)S(1)} %bitcast.17), custom_call_target="tpu_custom_call" | custom-call | flops 719323136 | bytes 6422528 | tf_op jit(solution)/shard_map/pallas_call | solution.py:126
  (24 shorter events, 2.3 us)
Async XLA Ops:
  8.0 2.1 %copy-start.5 = (f32[1,112,1792]{2,1,0:T(8,128)S(1)}, f32[1,112,1792]{2,1,0:T(8,128)}, u32[]{:S(2)}) copy-start(f32[1,112,1792]{2,1,0:T(8,128)} %param.8) | copy-start | bytes 2408452
  8.0 58.9 %copy-start.6 = (bf16[1,112,1792]{2,1,0:T(8,128)(2,1)S(1)}, bf16[1,112,1792]{2,1,0:T(8,128)(2,1)}, u32[]{:S(2)}) copy-start(bf16[1,112,1792]{2,1,0:T(8,128)(2,1)} %param.7) | copy-start | bytes 1204228
  8.0 58.9 %all-gather.5.cloned.1.call-start = ((), (), s32[]{:S(2)}) async-start(), calls=%async_computation.5 | async-start | bytes 6823936 | tf_op jit(solution)/shard_map/all_gather | solution.py:105
  8.8 93.2 %reduce-scatter.4.cloned.1.call-start = ((), (), s32[]{:S(2)}) async-start(), calls=%async_computation.7 | async-start | bytes 6823936
  9.3 116.0 %all-gather.7.cloned.1.call-start = ((), (), s32[]{:S(2)}) async-start(), calls=%async_computation.6 | async-start | bytes 6823936 | tf_op jit(solution)/shard_map/all_gather | solution.py:106
  11.2 60.6 %all-to-all-start = ((bf16[16,112,112]{2,1,0:T(8,128)(2,1)}), bf16[16,112,112]{2,1,0:T(8,128)(2,1)S(1)}, u32[]{:S(2)}, u32[]{:S(2)}) async-start(bf16[16,112,112]{2,1,0:T(8,128)(2,1)} %shard_map.85), calls=%async_computation | async-start | bytes 917504 | tf_op jit(solution)/shard_map/all_to_all | solution.py:90
  66.9 2.9 %copy-start = (bf16[1,1792,1792]{2,1,0:T(8,128)(2,1)S(1)}, bf16[1,1792,1792]{2,1,0:T(8,128)(2,1)}, u32[]{:S(2)}) copy-start(bf16[1,1792,1792]{2,1,0:T(8,128)(2,1)} %all-gather.5.cloned.1.call-done) | copy-start | bytes 19267588
  71.7 24.9 %all-to-all-start.1 = ((bf16[16,112,112]{2,1,0:T(8,128)(2,1)}), bf16[16,112,112]{2,1,0:T(8,128)(2,1)S(1)}, u32[]{:S(2)}, u32[]{:S(2)}) async-start(bf16[16,112,112]{2,1,0:T(8,128)(2,1)} %shard_map.87), calls=%async_computation.1 | async-start | bytes 917504 | tf_op jit(solution)/shard_map/all_to_all | solution.py:90
  77.0 48.3 %copy-start.9 = (bf16[112,1792]{1,0:T(8,128)(2,1)}, bf16[112,1792]{1,0:T(8,128)(2,1)S(1)}, u32[]{:S(2)}) copy-start(bf16[112,1792]{1,0:T(8,128)(2,1)S(1)} %shard_map.86.second_ref) | copy-start | bytes 1204228
  101.9 2.9 %copy-start.1 = (bf16[1,1792,1792]{2,1,0:T(8,128)(2,1)S(1)}, bf16[1,1792,1792]{2,1,0:T(8,128)(2,1)}, u32[]{:S(2)}) copy-start(bf16[1,1792,1792]{2,1,0:T(8,128)(2,1)} %all-gather.5.cloned.1.call-done) | copy-start | bytes 19267588
  104.9 1.0 copy-start.7
  107.9 24.9 %all-to-all-start.2 = ((bf16[16,112,112]{2,1,0:T(8,128)(2,1)}), bf16[16,112,112]{2,1,0:T(8,128)(2,1)S(1)}, u32[]{:S(2)}, u32[]{:S(2)}) async-start(bf16[16,112,112]{2,1,0:T(8,128)(2,1)} %shard_map.88), calls=%async_computation.2 | async-start | bytes 917504 | tf_op jit(solution)/shard_map/all_to_all | solution.py:90
  125.4 2.8 %copy-start.3 = (bf16[1,1792,1792]{2,1,0:T(8,128)(2,1)S(1)}, bf16[1,1792,1792]{2,1,0:T(8,128)(2,1)}, u32[]{:S(2)}) copy-start(bf16[1,1792,1792]{2,1,0:T(8,128)(2,1)} %all-gather.7.cloned.1.call-done) | copy-start | bytes 19267588
  128.2 16.6 %copy-start.8 = (bf16[1,112,1792]{2,1,0:T(8,128)(2,1)S(1)}, bf16[1,112,1792]{2,1,0:T(8,128)(2,1)}, u32[]{:S(2)}) copy-start(bf16[1,112,1792]{2,1,0:T(8,128)(2,1)} %reduce-scatter.4.cloned.1.call-done) | copy-start | bytes 1204228
  132.7 2.8 %copy-start.4 = (bf16[1,1792,1792]{2,1,0:T(8,128)(2,1)S(1)}, bf16[1,1792,1792]{2,1,0:T(8,128)(2,1)}, u32[]{:S(2)}) copy-start(bf16[1,1792,1792]{2,1,0:T(8,128)(2,1)} %all-gather.7.cloned.1.call-done) | copy-start | bytes 19267588
  135.5 1.0 copy-start.10
  141.3 28.3 %all-to-all-start.3 = ((bf16[16,2,112,112]{3,2,1,0:T(8,128)(2,1)}), bf16[16,2,112,112]{3,2,1,0:T(8,128)(2,1)S(1)}, u32[]{:S(2)}, u32[]{:S(2)}) async-start(bf16[16,2,112,112]{3,2,1,0:T(8,128)(2,1)} %shard_map.90), calls=%async_computation.3 | async-start | bytes 1835008 | tf_op jit(solution)/shard_map/all_to_all | solution.py:90
  169.6 2.8 %copy-start.2 = (bf16[1,1792,1792]{2,1,0:T(8,128)(2,1)S(1)}, bf16[1,1792,1792]{2,1,0:T(8,128)(2,1)}, u32[]{:S(2)}) copy-start(bf16[1,1792,1792]{2,1,0:T(8,128)(2,1)} %all-gather.5.cloned.1.call-done) | copy-start | bytes 19267588
Sparse Core Ops, SparseCore 0:
  10.8 56.0 all-gather.4
  68.9 56.3 all-gather.6
Sparse Core Ops, SparseCore 1:
  12.9 88.9 reduce-scatter.3

commit v8 on v6

--- a/solution.py
+++ b/solution.py
@@ -19,10 +19,13 @@
     return pl.BlockSpec(memory_space=pltpu.VMEM)
 
 
-def spread(x_ref, out_ref, *lead):
+def piece(x_ref, out_ref, s, lead=()):
     width = out_ref.shape[-1]
-    for s in range(GROUP):
-        out_ref[(s, *lead)] = x_ref[:, s * width : (s + 1) * width].astype(out_ref.dtype)
+    out_ref[(s, *lead)] = x_ref[:, s * width : (s + 1) * width].astype(out_ref.dtype)
+
+
+def ready(t, width):
+    return range(t * TILE // width, (t + 1) * TILE // width)
 
 
 def fetch(basis_ref, held, sems, by_column):
@@ -36,19 +39,34 @@
 
 
 def cut_kernel(x_ref, out_ref):
-    spread(x_ref, out_ref)
+    for s in range(GROUP):
+        piece(x_ref, out_ref, s)
 
 
 def turn_kernel(x_ref, out_ref):
     out_ref[...] = x_ref[...].astype(f32).T.astype(bf16)
 
 
-def right_kernel(a_ref, right_ref, out_ref, x_ref, held, sems):
-    for t, copy in enumerate(fetch(right_ref, held, sems, True)):
+def right_kernel(a_ref, right_ref, out_ref, x_ref, a_held, held, a_sem, sems, mix=lambda gradient: None):
+    rows = pltpu.make_async_copy(a_ref, a_held, a_sem)
+    rows.start()
+    copies = fetch(right_ref, held, sems, True)
+    rows.wait()
+    mix(a_held)
+    for t, copy in enumerate(copies):
         copy.wait()
         tile = slice(t * TILE, (t + 1) * TILE)
-        x_ref[:, tile] = jnp.dot(a_ref[...], held[:, tile], preferred_element_type=f32)
-    spread(x_ref, out_ref)
+        x_ref[:, tile] = jnp.dot(a_held[...], held[:, tile], preferred_element_type=f32)
+        for s in ready(t, out_ref.shape[-1]):
+            piece(x_ref, out_ref, s)
+
+
+def gradient_kernel(a_ref, right_ref, moment_ref, out_ref, moment_out, *scratch):
+    def mix(gradient):
+        new = beta_one * moment_ref[...].astype(f32) + (1.0 - beta_one) * gradient[...].astype(f32)
+        moment_out[...] = new.astype(bf16)
+
+    right_kernel(a_ref, right_ref, out_ref, *scratch, mix=mix)
 
 
 def moment_kernel(cols_ref, left_ref, out_ref, held, sems):
@@ -72,11 +90,13 @@
         second_new = beta_two * second_ref[:, tile].astype(f32) + (1.0 - beta_two) * rot_grad * rot_grad
         direction = rot_mom * fix_ref[0] / (jnp.sqrt(second_new * fix_ref[1]) + epsilon)
         dir_ref[:, tile] = direction.astype(bf16)
-    spread(rot_ref, out_ref, 0)
+        for s in ready(t, out_ref.shape[-1]):
+            piece(rot_ref, out_ref, s, (0,))
     for t in range(len(copies)):
         tile = slice(t * TILE, (t + 1) * TILE)
         back_ref[:, tile] = lax.dot_general(dir_ref[...], held[tile, :], by_rows, preferred_element_type=f32)
-    spread(back_ref, out_ref, 1)
+        for s in ready(t, out_ref.shape[-1]):
+            piece(back_ref, out_ref, s, (1,))
 
 
 def last_kernel(in_ref, second_ref, right_ref, second_out, update_out, held, sems):
@@ -84,12 +104,12 @@
     columns = second_ref.shape[1]
     width = in_ref.shape[-1]
     rows = in_ref[:, 1].reshape(columns, width).astype(f32).T.astype(bf16)
+    rot_grad = in_ref[:, 0].reshape(columns, width).astype(f32).T
+    second_out[...] = beta_two * second_ref[...] + (1.0 - beta_two) * rot_grad * rot_grad
     for t, copy in enumerate(copies):
         copy.wait()
         tile = slice(t * TILE, (t + 1) * TILE)
         update_out[:, tile] = lax.dot_general(rows, held[tile, :], by_rows, preferred_element_type=f32).astype(bf16)
-    rot_grad = in_ref[:, 0].reshape(columns, width).astype(f32).T
-    second_out[...] = beta_two * second_ref[...] + (1.0 - beta_two) * rot_grad * rot_grad
 
 
 def call(kernel, out_shape, in_specs, scratch, flops, moved):
@@ -112,25 +132,27 @@
     rows, columns = moment.shape[1:]
     product = 2 * rows * columns * columns
     basis_bytes = 2 * columns * columns
-    apart = pl.BlockSpec(memory_space=pl.ANY)
+    apart = pl.BlockSpec(memory_space=pltpu.HBM)
     narrow = pltpu.VMEM((rows, columns), bf16)
     wide = pltpu.VMEM((rows, columns), f32)
     basis = [pltpu.VMEM((columns, columns), bf16), pltpu.SemaphoreType.DMA((columns // TILE,))]
     pieces = jax.ShapeDtypeStruct((GROUP, rows, rows), bf16)
     turned = jax.ShapeDtypeStruct((rows, columns), bf16)
     summed = jax.ShapeDtypeStruct((rows, columns), f32)
-    times_right = call(right_kernel, pieces, [whole(), apart], [wide, *basis], product, basis_bytes)
+    right_scratch = [wide, narrow, basis[0], pltpu.SemaphoreType.DMA, basis[1]]
 
     gradient = lax.psum_scatter(grad_parts[0], "dp", scatter_dimension=0, tiled=True)[0]
     right_full = lax.all_gather(right_basis[0], "shard", axis=0, tiled=True)
     left_full = lax.all_gather(left_basis[0], "shard", axis=0, tiled=True)
     second_cols = swap(call(cut_kernel, pieces, [whole()], [], 0, 6 * rows * columns)(second[0]))
     second_turned = call(turn_kernel, turned, [whole()], [], 0, 4 * rows * columns)(second_cols.reshape(columns, rows))
+    times_right = call(right_kernel, pieces, [apart, apart], right_scratch, product, basis_bytes)
     mom_cols = swap(times_right(moment[0], right_full))
     gradient, second_turned, mom_cols = lax.optimization_barrier((gradient, second_turned, mom_cols))
 
-    moment_new = (beta_one * moment[0].astype(f32) + (1.0 - beta_one) * gradient.astype(f32)).astype(bf16)
-    grad_cols = swap(times_right(gradient, right_full))
+    times_right = call(gradient_kernel, (pieces, turned), [apart, apart, whole()], right_scratch, product, basis_bytes)
+    grad_right, moment_new = times_right(gradient, right_full, moment[0])
+    grad_cols = swap(grad_right)
     times_left = call(moment_kernel, summed, [whole(), apart], basis, product, basis_bytes)
     rot_mom_old = times_left(mom_cols.reshape(columns, rows), left_full)
 

time: 186 us -> 185 us (level)
  blocking collectives: 0 us -> 28.5 us
  waiting for transfers between devices: 108 us -> 83.7 us
  starting transfers between devices: 27.4 us -> 23.8 us
    all_to_all x0 -> x1, blocking collectives: none -> 28.5 us  [swap(): lax.all_to_all(pieces, 'shard', split_axis=0, concat_axis=0, tiled=True)]
    all_to_all x4 -> x3, waiting for transfers between devices: 47.4 us -> 23.5 us  [swap(): lax.all_to_all(pieces, 'shard', split_axis=0, concat_axis=0, tiled=True)]
    all_to_all x4 -> x3, starting transfers between devices: 27.3 us -> 23.7 us  [swap(): lax.all_to_all(pieces, 'shard', split_axis=0, concat_axis=0, tiled=True)]
  transfers between devices with their start and end apart: 7 -> 6, of which waited for: 6 -> 5; matrix products, arithmetic and copies ran while one was open for 1% -> 0% of each run, Pallas kernels for 8% -> 9%
where the time goes in v8:
time: 185 us; the launch traced here: 182 us
  waiting for transfers between devices  83.7 us (45%)
  Pallas kernels  28.8 us (16%)
  blocking collectives  28.5 us (15%)
  starting transfers between devices  23.8 us (13%)
  between operations  16.3 us (9%)
    all_gather x1, waiting for transfers between devices, local(): right_full = lax.all_gather(right_basis[0], 'shard', axis=0, tiled=True)  45.8 us
    all_to_all x1, blocking collectives, swap(): lax.all_to_all(pieces, 'shard', split_axis=0, concat_axis=0, tiled=True)  28.5 us
    all_to_all x3, starting transfers between devices, swap(): lax.all_to_all(pieces, 'shard', split_axis=0, concat_axis=0, tiled=True)  23.7 us
    all_to_all x3, waiting for transfers between devices, swap(): lax.all_to_all(pieces, 'shard', split_axis=0, concat_axis=0, tiled=True)  23.5 us
    all_gather x1, waiting for transfers between devices, local(): left_full = lax.all_gather(left_basis[0], 'shard', axis=0, tiled=True)  7.68 us
    pallas_call x1, Pallas kernels, local(): middle(fixes, grad_cols.reshape(columns, rows), rot_mom_old, second_turne...  6.78 us
    unnamed x4, waiting for transfers between devices  6.7 us
    pallas_call x1, Pallas kernels, local(): second_new, update = last(got, second[0], right_full)  6.23 us
  transfers between devices with their start and end apart: 6, of which 5 were waited for; matrix products, arithmetic and copies ran while one was open for 0% of the time, Pallas kernels for 9%

profile of v8, /device:TPU:1, one launch (start us, length us, event | category | flops | bytes accessed | tf_op | source)
XLA Modules:
  0.0 182.2 jit_solution(15749413059586753332)
XLA Ops:
  8.0 0.0 all-gather.5.cloned.1.call-start
  8.1 0.7 all-gather.5.cloned.1.call-update
  8.8 0.0 reduce-scatter.4.cloned.1.call-start
  8.8 0.5 reduce-scatter.4.cloned.1.call-update
  9.3 0.0 all-gather.7.cloned.1.call-start
  9.4 0.7 all-gather.7.cloned.1.call-update
  10.1 1.1 shard_map.85
  11.2 10.0 %all-to-all-start = ((bf16[16,112,112]{2,1,0:T(8,128)(2,1)}), bf16[16,112,112]{2,1,0:T(8,128)(2,1)S(1)}, u32[]{:S(2)}, u32[]{:S(2)}) async-start(bf16[16,112,112]{2,1,0:T(8,128)(2,1)} %shard_map.85), calls=%async_computation | async-start | bytes 917504 | tf_op jit(solution)/shard_map/all_to_all | solution.py:128
  21.2 45.8 %all-gather.5.cloned.1.call-done = bf16[1,1792,1792]{2,1,0:T(8,128)(2,1)} async-done(((bf16[1,112,1792]{2,1,0:T(8,128)(2,1)}), bf16[1,1792,1792]{2,1,0:T(8,128)(2,1)}) %all-gather.5.cloned.1.call-update) | async-done | bytes 6422544 | tf_op jit(solution)/shard_map/all_gather | solution.py:145
  67.0 5.3 %shard_map.87 = bf16[16,112,112]{2,1,0:T(8,128)(2,1)} custom-call(bf16[112,1792]{1,0:T(8,128)(2,1)S(1)} %bitcast.18, bf16[1792,1792]{1,0:T(8,128)(2,1)} %bitcast.21), custom_call_target="tpu_custom_call" | custom-call | flops 719323136 | bytes 6422528 | tf_op jit(solution)/shard_map/pallas_call | solution.py:150
  72.3 4.9 %all-to-all-start.1 = ((bf16[16,112,112]{2,1,0:T(8,128)(2,1)}), bf16[16,112,112]{2,1,0:T(8,128)(2,1)S(1)}, u32[]{:S(2)}, u32[]{:S(2)}) async-start(bf16[16,112,112]{2,1,0:T(8,128)(2,1)} %shard_map.87), calls=%async_computation.1 | async-start | bytes 917504 | tf_op jit(solution)/shard_map/all_to_all | solution.py:128
  77.2 0.2 shard_map.86.second_ref
  77.4 19.9 %all-to-all-done.1 = bf16[16,112,112]{2,1,0:T(8,128)(2,1)S(1)} async-done(((bf16[16,112,112]{2,1,0:T(8,128)(2,1)}), bf16[16,112,112]{2,1,0:T(8,128)(2,1)S(1)}, u32[]{:S(2)}, u32[]{:S(2)}) %all-to-all-start.1) | async-done | bytes 401440 | tf_op jit(solution)/shard_map/all_to_all | solution.py:128
  97.3 4.8 %reduce-scatter.4.cloned.1.call-done = bf16[1,112,1792]{2,1,0:T(8,128)(2,1)} async-done(((bf16[16,112,1792]{2,1,0:T(8,128)(2,1)}), bf16[1,112,1792]{2,1,0:T(8,128)(2,1)}) %reduce-scatter.4.cloned.1.call-update) | async-done | bytes 401424
  102.1 1.0 copy-done.2
  103.2 5.3 %shard_map.88 = (bf16[16,112,112]{2,1,0:T(8,128)(2,1)}, bf16[112,1792]{1,0:T(8,128)(2,1)}) custom-call(bf16[112,1792]{1,0:T(8,128)(2,1)S(1)} %bitcast.20, bf16[1792,1792]{1,0:T(8,128)(2,1)} %bitcast.22, bf16[112,1792]{1,0:T(8,128)(2,1)S(1)} %bitcast.19), custom_call_target="tpu_custom_call" | custom-call | flops 719323136 | bytes 6422528 | tf_op jit(solution)/shard_map/pallas_call | solution.py:154
  108.5 8.8 %all-to-all-start.2 = ((bf16[16,112,112]{2,1,0:T(8,128)(2,1)}), bf16[16,112,112]{2,1,0:T(8,128)(2,1)S(1)}, u32[]{:S(2)}, u32[]{:S(2)}) async-start(bf16[16,112,112]{2,1,0:T(8,128)(2,1)} %get-tuple-element.12), calls=%async_computation.2 | async-start | bytes 917504 | tf_op jit(solution)/shard_map/all_to_all | solution.py:128
  118.0 0.1 maximum_divide_fusion.fix_ref
  118.1 7.7 %all-gather.7.cloned.1.call-done = bf16[1,1792,1792]{2,1,0:T(8,128)(2,1)} async-done(((bf16[1,112,1792]{2,1,0:T(8,128)(2,1)}), bf16[1,1792,1792]{2,1,0:T(8,128)(2,1)}) %all-gather.7.cloned.1.call-update) | async-done | bytes 6422544 | tf_op jit(solution)/shard_map/all_gather | solution.py:146
  125.8 3.8 %shard_map.89.mom_ref = f32[112,1792]{1,0:T(8,128)S(1)} custom-call(bf16[1792,112]{1,0:T(8,128)(2,1)S(1)} %bitcast.16, bf16[1792,1792]{1,0:T(8,128)(2,1)} %bitcast.24), custom_call_target="tpu_custom_call" | custom-call | flops 719323136 | bytes 6422528 | tf_op jit(solution)/shard_map/pallas_call | solution.py:157
  129.7 3.6 %all-to-all-done.2 = bf16[16,112,112]{2,1,0:T(8,128)(2,1)S(1)} async-done(((bf16[16,112,112]{2,1,0:T(8,128)(2,1)}), bf16[16,112,112]{2,1,0:T(8,128)(2,1)S(1)}, u32[]{:S(2)}, u32[]{:S(2)}) %all-to-all-start.2) | async-done | bytes 401440 | tf_op jit(solution)/shard_map/all_to_all | solution.py:128
  133.2 6.8 %shard_map.90 = bf16[16,2,112,112]{3,2,1,0:T(8,128)(2,1)S(1)} custom-call(f32[2]{0:T(128)S(1)} %maximum_divide_fusion.fix_ref, bf16[1792,112]{1,0:T(8,128)(2,1)S(1)} %bitcast.17, f32[112,1792]{1,0:T(8,128)S(1)} %shard_map.89.mom_ref, bf16[112,1792]{1,0:T(8,128)(2,1)S(1)} %shard_map.86.second_ref, bf16[1792,1792]{1,0:T(8,128)(2,1)} %bitcast.25), custom_call_target="tpu_custom_call" | custom-call | flops 1438646272 | bytes 6422528 | tf_op jit(solution)/shard_map/pallas_call | solution.py:164
  140.0 28.5 %all_to_all.20.in_ref = bf16[16,2,112,112]{3,2,1,0:T(8,128)(2,1)S(1)} all-to-all(bf16[16,2,112,112]{3,2,1,0:T(8,128)(2,1)S(1)} %shard_map.90), channel_id=1, replica_groups=mesh['dp'=16,'shard'=16] {'shard'}, dimensions={0} | all-to-all | bytes 1605632 | tf_op jit(solution)/shard_map/all_to_all | solution.py:128
  168.5 6.2 %shard_map.91 = (f32[112,1792]{1,0:T(8,128)}, bf16[112,1792]{1,0:T(8,128)(2,1)}) custom-call(bf16[16,2,112,112]{3,2,1,0:T(8,128)(2,1)S(1)} %all_to_all.20.in_ref, f32[112,1792]{1,0:T(8,128)S(1)} %bitcast.14, bf16[1792,1792]{1,0:T(8,128)(2,1)} %bitcast.23), custom_call_target="tpu_custom_call" | custom-call | flops 719323136 | bytes 6422528 | tf_op jit(solution)/shard_map/pallas_call | solution.py:168
  (6 shorter events, 0.0 us)
Async XLA Ops:
  8.0 2.1 %copy-start = (f32[1,112,1792]{2,1,0:T(8,128)S(1)}, f32[1,112,1792]{2,1,0:T(8,128)}, u32[]{:S(2)}) copy-start(f32[1,112,1792]{2,1,0:T(8,128)} %param.8) | copy-start | bytes 2408452
  8.0 59.0 %copy-start.1 = (bf16[1,112,1792]{2,1,0:T(8,128)(2,1)S(1)}, bf16[1,112,1792]{2,1,0:T(8,128)(2,1)}, u32[]{:S(2)}) copy-start(bf16[1,112,1792]{2,1,0:T(8,128)(2,1)} %param.7) | copy-start | bytes 1204228
  8.0 58.9 %all-gather.5.cloned.1.call-start = ((), (), s32[]{:S(2)}) async-start(), calls=%async_computation.5 | async-start | bytes 6823936 | tf_op jit(solution)/shard_map/all_gather | solution.py:145
  8.8 93.4 %reduce-scatter.4.cloned.1.call-start = ((), (), s32[]{:S(2)}) async-start(), calls=%async_computation.7 | async-start | bytes 6823936
  9.3 116.5 %all-gather.7.cloned.1.call-start = ((), (), s32[]{:S(2)}) async-start(), calls=%async_computation.6 | async-start | bytes 6823936 | tf_op jit(solution)/shard_map/all_gather | solution.py:146
  11.2 61.1 %all-to-all-start = ((bf16[16,112,112]{2,1,0:T(8,128)(2,1)}), bf16[16,112,112]{2,1,0:T(8,128)(2,1)S(1)}, u32[]{:S(2)}, u32[]{:S(2)}) async-start(bf16[16,112,112]{2,1,0:T(8,128)(2,1)} %shard_map.85), calls=%async_computation | async-start | bytes 917504 | tf_op jit(solution)/shard_map/all_to_all | solution.py:128
  72.3 25.0 %all-to-all-start.1 = ((bf16[16,112,112]{2,1,0:T(8,128)(2,1)}), bf16[16,112,112]{2,1,0:T(8,128)(2,1)S(1)}, u32[]{:S(2)}, u32[]{:S(2)}) async-start(bf16[16,112,112]{2,1,0:T(8,128)(2,1)} %shard_map.87), calls=%async_computation.1 | async-start | bytes 917504 | tf_op jit(solution)/shard_map/all_to_all | solution.py:128
  102.1 1.0 copy-start.2
  108.5 24.7 %all-to-all-start.2 = ((bf16[16,112,112]{2,1,0:T(8,128)(2,1)}), bf16[16,112,112]{2,1,0:T(8,128)(2,1)S(1)}, u32[]{:S(2)}, u32[]{:S(2)}) async-start(bf16[16,112,112]{2,1,0:T(8,128)(2,1)} %get-tuple-element.12), calls=%async_computation.2 | async-start | bytes 917504 | tf_op jit(solution)/shard_map/all_to_all | solution.py:128
Sparse Core Ops, SparseCore 0:
  10.8 56.0 all-gather.4
  68.9 56.8 all-gather.6
Sparse Core Ops, SparseCore 1:
  12.9 89.1 reduce-scatter.3

commit v9 on v8

--- a/solution.py
+++ b/solution.py
@@ -24,18 +24,21 @@
     out_ref[(s, *lead)] = x_ref[:, s * width : (s + 1) * width].astype(out_ref.dtype)
 
 
-def ready(t, width):
-    return range(t * TILE // width, (t + 1) * TILE // width)
-
-
-def fetch(basis_ref, held, sems, by_column):
+def fetch(basis_ref, held, sems):
     copies = []
     for t in range(basis_ref.shape[0] // TILE):
         tile = pl.ds(t * TILE, TILE)
-        spot = (slice(None), tile) if by_column else (tile, slice(None))
-        copies.append(pltpu.make_async_copy(basis_ref.at[spot], held.at[spot], sems.at[t]))
+        copies.append(pltpu.make_async_copy(basis_ref.at[tile, :], held.at[tile, :], sems.at[t]))
         copies[-1].start()
     return copies
+
+
+def product_into(out_ref, x_ref, copies, held):
+    for t, copy in enumerate(copies):
+        copy.wait()
+        tile = slice(t * TILE, (t + 1) * TILE)
+        part = jnp.dot(x_ref[:, tile], held[tile, :], preferred_element_type=f32)
+        out_ref[...] = part if t == 0 else out_ref[...] + part
 
 
 def cut_kernel(x_ref, out_ref):
@@ -50,15 +53,12 @@
 def right_kernel(a_ref, right_ref, out_ref, x_ref, a_held, held, a_sem, sems, mix=lambda gradient: None):
     rows = pltpu.make_async_copy(a_ref, a_held, a_sem)
     rows.start()
-    copies = fetch(right_ref, held, sems, True)
+    copies = fetch(right_ref, held, sems)
     rows.wait()
     mix(a_held)
-    for t, copy in enumerate(copies):
-        copy.wait()
-        tile = slice(t * TILE, (t + 1) * TILE)
-        x_ref[:, tile] = jnp.dot(a_held[...], held[:, tile], preferred_element_type=f32)
-        for s in ready(t, out_ref.shape[-1]):
-            piece(x_ref, out_ref, s)
+    product_into(x_ref, a_held, copies, held)
+    for s in range(GROUP):
+        piece(x_ref, out_ref, s)
 
 
 def gradient_kernel(a_ref, right_ref, moment_ref, out_ref, moment_out, *scratch):
@@ -69,38 +69,31 @@
     right_kernel(a_ref, right_ref, out_ref, *scratch, mix=mix)
 
 
-def moment_kernel(cols_ref, left_ref, out_ref, held, sems):
-    copies = fetch(left_ref, held, sems, True)
-    x = cols_ref[...].astype(f32).T.astype(bf16)
-    for t, copy in enumerate(copies):
-        copy.wait()
-        tile = slice(t * TILE, (t + 1) * TILE)
-        out_ref[:, tile] = jnp.dot(x, held[:, tile], preferred_element_type=f32)
+def moment_kernel(cols_ref, left_ref, out_ref, x_ref, held, sems):
+    copies = fetch(left_ref, held, sems)
+    x_ref[...] = cols_ref[...].astype(f32).T.astype(bf16)
+    product_into(out_ref, x_ref, copies, held)
 
 
-def middle_kernel(fix_ref, cols_ref, mom_ref, second_ref, left_ref, out_ref, rot_ref, dir_ref, back_ref, held, sems):
-    copies = fetch(left_ref, held, sems, True)
-    x = cols_ref[...].astype(f32).T.astype(bf16)
-    for t, copy in enumerate(copies):
-        copy.wait()
-        tile = slice(t * TILE, (t + 1) * TILE)
-        rot_grad = jnp.dot(x, held[:, tile], preferred_element_type=f32)
-        rot_ref[:, tile] = rot_grad
-        rot_mom = beta_one * mom_ref[:, tile] + (1.0 - beta_one) * rot_grad
-        second_new = beta_two * second_ref[:, tile].astype(f32) + (1.0 - beta_two) * rot_grad * rot_grad
-        direction = rot_mom * fix_ref[0] / (jnp.sqrt(second_new * fix_ref[1]) + epsilon)
-        dir_ref[:, tile] = direction.astype(bf16)
-        for s in ready(t, out_ref.shape[-1]):
-            piece(rot_ref, out_ref, s, (0,))
+def middle_kernel(fix_ref, cols_ref, mom_ref, second_ref, left_ref, out_ref, rot_ref, x_ref, back_ref, held, sems):
+    copies = fetch(left_ref, held, sems)
+    x_ref[...] = cols_ref[...].astype(f32).T.astype(bf16)
+    product_into(rot_ref, x_ref, copies, held)
+    rot_grad = rot_ref[...]
+    rot_mom = beta_one * mom_ref[...] + (1.0 - beta_one) * rot_grad
+    second_new = beta_two * second_ref[...].astype(f32) + (1.0 - beta_two) * rot_grad * rot_grad
+    direction = rot_mom * fix_ref[0] / (jnp.sqrt(second_new * fix_ref[1]) + epsilon)
+    x_ref[...] = direction.astype(bf16)
     for t in range(len(copies)):
         tile = slice(t * TILE, (t + 1) * TILE)
-        back_ref[:, tile] = lax.dot_general(dir_ref[...], held[tile, :], by_rows, preferred_element_type=f32)
-        for s in ready(t, out_ref.shape[-1]):
-            piece(back_ref, out_ref, s, (1,))
+        back_ref[:, tile] = lax.dot_general(x_ref[...], held[tile, :], by_rows, preferred_element_type=f32)
+    for s in range(GROUP):
+        piece(rot_ref, out_ref, s, (0,))
+        piece(back_ref, out_ref, s, (1,))
 
 
 def last_kernel(in_ref, second_ref, right_ref, second_out, update_out, held, sems):
-    copies = fetch(right_ref, held, sems, False)
+    copies = fetch(right_ref, held, sems)
     columns = second_ref.shape[1]
     width = in_ref.shape[-1]
     rows = in_ref[:, 1].reshape(columns, width).astype(f32).T.astype(bf16)
@@ -153,7 +146,7 @@
     times_right = call(gradient_kernel, (pieces, turned), [apart, apart, whole()], right_scratch, product, basis_bytes)
     grad_right, moment_new = times_right(gradient, right_full, moment[0])
     grad_cols = swap(grad_right)
-    times_left = call(moment_kernel, summed, [whole(), apart], basis, product, basis_bytes)
+    times_left = call(moment_kernel, summed, [whole(), apart], [narrow, *basis], product, basis_bytes)
     rot_mom_old = times_left(mom_cols.reshape(columns, rows), left_full)
 
     steps_float = block_steps[0].astype(f32)

time: 185 us -> 183 us (0.989)
  Pallas kernels: 28.8 us -> 25.6 us
  transfers between devices with their start and end apart: 6 -> 6, of which waited for: 5 -> 5; matrix products, arithmetic and copies ran while one was open for 0% -> 0% of each run, Pallas kernels for 9% -> 7%
where the time goes in v9:
time: 183 us; the launch traced here: 181 us
  waiting for transfers between devices  85 us (46%)
  blocking collectives  28.7 us (16%)
  Pallas kernels  25.6 us (14%)
  starting transfers between devices  24.1 us (13%)
  between operations  16.3 us (9%)
    all_gather x1, waiting for transfers between devices, local(): right_full = lax.all_gather(right_basis[0], 'shard', axis=0, tiled=True)  45.8 us
    all_to_all x1, blocking collectives, swap(): lax.all_to_all(pieces, 'shard', split_axis=0, concat_axis=0, tiled=True)  28.7 us
    all_to_all x3, starting transfers between devices, swap(): lax.all_to_all(pieces, 'shard', split_axis=0, concat_axis=0, tiled=True)  24 us
    all_to_all x3, waiting for transfers between devices, swap(): lax.all_to_all(pieces, 'shard', split_axis=0, concat_axis=0, tiled=True)  23.7 us
    unnamed x4, waiting for transfers between devices  7.88 us
    all_gather x1, waiting for transfers between devices, local(): left_full = lax.all_gather(left_basis[0], 'shard', axis=0, tiled=True)  7.58 us
    pallas_call x1, Pallas kernels, local(): second_new, update = last(got, second[0], right_full)  6.23 us
    pallas_call x1, Pallas kernels, local(): middle(fixes, grad_cols.reshape(columns, rows), rot_mom_old, second_turne...  6.05 us
  transfers between devices with their start and end apart: 6, of which 5 were waited for; matrix products, arithmetic and copies ran while one was open for 0% of the time, Pallas kernels for 7%

profile of v9, /device:TPU:1, one launch (start us, length us, event | category | flops | bytes accessed | tf_op | source)
XLA Modules:
  0.0 180.8 jit_solution(14143664212930076207)
XLA Ops:
  8.0 0.0 all-gather.5.cloned.1.call-start
  8.1 0.7 all-gather.5.cloned.1.call-update
  8.8 0.0 reduce-scatter.4.cloned.1.call-start
  8.8 0.5 reduce-scatter.4.cloned.1.call-update
  9.3 0.0 all-gather.7.cloned.1.call-start
  9.4 0.7 all-gather.7.cloned.1.call-update
  10.1 1.1 shard_map.85
  11.2 10.0 %all-to-all-start = ((bf16[16,112,112]{2,1,0:T(8,128)(2,1)}), bf16[16,112,112]{2,1,0:T(8,128)(2,1)S(1)}, u32[]{:S(2)}, u32[]{:S(2)}) async-start(bf16[16,112,112]{2,1,0:T(8,128)(2,1)} %shard_map.85), calls=%async_computation | async-start | bytes 917504 | tf_op jit(solution)/shard_map/all_to_all | solution.py:121
  21.2 45.8 %all-gather.5.cloned.1.call-done = bf16[1,1792,1792]{2,1,0:T(8,128)(2,1)} async-done(((bf16[1,112,1792]{2,1,0:T(8,128)(2,1)}), bf16[1,1792,1792]{2,1,0:T(8,128)(2,1)}) %all-gather.5.cloned.1.call-update) | async-done | bytes 6422544 | tf_op jit(solution)/shard_map/all_gather | solution.py:138
  67.0 4.4 %shard_map.87 = bf16[16,112,112]{2,1,0:T(8,128)(2,1)} custom-call(bf16[112,1792]{1,0:T(8,128)(2,1)S(1)} %bitcast.18, bf16[1792,1792]{1,0:T(8,128)(2,1)} %bitcast.21), custom_call_target="tpu_custom_call" | custom-call | flops 719323136 | bytes 6422528 | tf_op jit(solution)/shard_map/pallas_call | solution.py:143
  71.4 5.1 %all-to-all-start.1 = ((bf16[16,112,112]{2,1,0:T(8,128)(2,1)}), bf16[16,112,112]{2,1,0:T(8,128)(2,1)S(1)}, u32[]{:S(2)}, u32[]{:S(2)}) async-start(bf16[16,112,112]{2,1,0:T(8,128)(2,1)} %shard_map.87), calls=%async_computation.1 | async-start | bytes 917504 | tf_op jit(solution)/shard_map/all_to_all | solution.py:121
  76.5 0.2 shard_map.86.second_ref
  76.7 19.3 %all-to-all-done.1 = bf16[16,112,112]{2,1,0:T(8,128)(2,1)S(1)} async-done(((bf16[16,112,112]{2,1,0:T(8,128)(2,1)}), bf16[16,112,112]{2,1,0:T(8,128)(2,1)S(1)}, u32[]{:S(2)}, u32[]{:S(2)}) %all-to-all-start.1) | async-done | bytes 401440 | tf_op jit(solution)/shard_map/all_to_all | solution.py:121
  96.0 6.0 %reduce-scatter.4.cloned.1.call-done = bf16[1,112,1792]{2,1,0:T(8,128)(2,1)} async-done(((bf16[16,112,1792]{2,1,0:T(8,128)(2,1)}), bf16[1,112,1792]{2,1,0:T(8,128)(2,1)}) %reduce-scatter.4.cloned.1.call-update) | async-done | bytes 401424
  101.9 1.0 copy-done.2
  102.9 4.5 %shard_map.88 = (bf16[16,112,112]{2,1,0:T(8,128)(2,1)}, bf16[112,1792]{1,0:T(8,128)(2,1)}) custom-call(bf16[112,1792]{1,0:T(8,128)(2,1)S(1)} %bitcast.20, bf16[1792,1792]{1,0:T(8,128)(2,1)} %bitcast.22, bf16[112,1792]{1,0:T(8,128)(2,1)S(1)} %bitcast.19), custom_call_target="tpu_custom_call" | custom-call | flops 719323136 | bytes 6422528 | tf_op jit(solution)/shard_map/pallas_call | solution.py:147
  107.4 8.9 %all-to-all-start.2 = ((bf16[16,112,112]{2,1,0:T(8,128)(2,1)}), bf16[16,112,112]{2,1,0:T(8,128)(2,1)S(1)}, u32[]{:S(2)}, u32[]{:S(2)}) async-start(bf16[16,112,112]{2,1,0:T(8,128)(2,1)} %get-tuple-element.12), calls=%async_computation.2 | async-start | bytes 917504 | tf_op jit(solution)/shard_map/all_to_all | solution.py:121
  117.0 0.1 maximum_divide_fusion.fix_ref
  117.1 7.6 %all-gather.7.cloned.1.call-done = bf16[1,1792,1792]{2,1,0:T(8,128)(2,1)} async-done(((bf16[1,112,1792]{2,1,0:T(8,128)(2,1)}), bf16[1,1792,1792]{2,1,0:T(8,128)(2,1)}) %all-gather.7.cloned.1.call-update) | async-done | bytes 6422544 | tf_op jit(solution)/shard_map/all_gather | solution.py:139
  124.7 3.2 %shard_map.89.mom_ref = f32[112,1792]{1,0:T(8,128)S(1)} custom-call(bf16[1792,112]{1,0:T(8,128)(2,1)S(1)} %bitcast.16, bf16[1792,1792]{1,0:T(8,128)(2,1)} %bitcast.24), custom_call_target="tpu_custom_call" | custom-call | flops 719323136 | bytes 6422528 | tf_op jit(solution)/shard_map/pallas_call | solution.py:150
  127.9 4.4 %all-to-all-done.2 = bf16[16,112,112]{2,1,0:T(8,128)(2,1)S(1)} async-done(((bf16[16,112,112]{2,1,0:T(8,128)(2,1)}), bf16[16,112,112]{2,1,0:T(8,128)(2,1)S(1)}, u32[]{:S(2)}, u32[]{:S(2)}) %all-to-all-start.2) | async-done | bytes 401440 | tf_op jit(solution)/shard_map/all_to_all | solution.py:121
  132.3 6.0 %shard_map.90 = bf16[16,2,112,112]{3,2,1,0:T(8,128)(2,1)S(1)} custom-call(f32[2]{0:T(128)S(1)} %maximum_divide_fusion.fix_ref, bf16[1792,112]{1,0:T(8,128)(2,1)S(1)} %bitcast.17, f32[112,1792]{1,0:T(8,128)S(1)} %shard_map.89.mom_ref, bf16[112,1792]{1,0:T(8,128)(2,1)S(1)} %shard_map.86.second_ref, bf16[1792,1792]{1,0:T(8,128)(2,1)} %bitcast.25), custom_call_target="tpu_custom_call" | custom-call | flops 1438646272 | bytes 6422528 | tf_op jit(solution)/shard_map/pallas_call | solution.py:157
  138.4 28.7 %all_to_all.20.in_ref = bf16[16,2,112,112]{3,2,1,0:T(8,128)(2,1)S(1)} all-to-all(bf16[16,2,112,112]{3,2,1,0:T(8,128)(2,1)S(1)} %shard_map.90), channel_id=1, replica_groups=mesh['dp'=16,'shard'=16] {'shard'}, dimensions={0} | all-to-all | bytes 1605632 | tf_op jit(solution)/shard_map/all_to_all | solution.py:121
  167.1 6.2 %shard_map.91 = (f32[112,1792]{1,0:T(8,128)}, bf16[112,1792]{1,0:T(8,128)(2,1)}) custom-call(bf16[16,2,112,112]{3,2,1,0:T(8,128)(2,1)S(1)} %all_to_all.20.in_ref, f32[112,1792]{1,0:T(8,128)S(1)} %bitcast.14, bf16[1792,1792]{1,0:T(8,128)(2,1)} %bitcast.23), custom_call_target="tpu_custom_call" | custom-call | flops 719323136 | bytes 6422528 | tf_op jit(solution)/shard_map/pallas_call | solution.py:161
  (6 shorter events, 0.0 us)
Async XLA Ops:
  8.0 2.1 %copy-start = (f32[1,112,1792]{2,1,0:T(8,128)S(1)}, f32[1,112,1792]{2,1,0:T(8,128)}, u32[]{:S(2)}) copy-start(f32[1,112,1792]{2,1,0:T(8,128)} %param.8) | copy-start | bytes 2408452
  8.0 59.0 %copy-start.1 = (bf16[1,112,1792]{2,1,0:T(8,128)(2,1)S(1)}, bf16[1,112,1792]{2,1,0:T(8,128)(2,1)}, u32[]{:S(2)}) copy-start(bf16[1,112,1792]{2,1,0:T(8,128)(2,1)} %param.7) | copy-start | bytes 1204228
  8.0 58.9 %all-gather.5.cloned.1.call-start = ((), (), s32[]{:S(2)}) async-start(), calls=%async_computation.5 | async-start | bytes 6823936 | tf_op jit(solution)/shard_map/all_gather | solution.py:138
  8.8 93.2 %reduce-scatter.4.cloned.1.call-start = ((), (), s32[]{:S(2)}) async-start(), calls=%async_computation.7 | async-start | bytes 6823936
  9.3 115.4 %all-gather.7.cloned.1.call-start = ((), (), s32[]{:S(2)}) async-start(), calls=%async_computation.6 | async-start | bytes 6823936 | tf_op jit(solution)/shard_map/all_gather | solution.py:139
  11.2 60.2 %all-to-all-start = ((bf16[16,112,112]{2,1,0:T(8,128)(2,1)}), bf16[16,112,112]{2,1,0:T(8,128)(2,1)S(1)}, u32[]{:S(2)}, u32[]{:S(2)}) async-start(bf16[16,112,112]{2,1,0:T(8,128)(2,1)} %shard_map.85), calls=%async_computation | async-start | bytes 917504 | tf_op jit(solution)/shard_map/all_to_all | solution.py:121
  71.4 24.6 %all-to-all-start.1 = ((bf16[16,112,112]{2,1,0:T(8,128)(2,1)}), bf16[16,112,112]{2,1,0:T(8,128)(2,1)S(1)}, u32[]{:S(2)}, u32[]{:S(2)}) async-start(bf16[16,112,112]{2,1,0:T(8,128)(2,1)} %shard_map.87), calls=%async_computation.1 | async-start | bytes 917504 | tf_op jit(solution)/shard_map/all_to_all | solution.py:121
  101.9 1.0 copy-start.2
  107.4 24.9 %all-to-all-start.2 = ((bf16[16,112,112]{2,1,0:T(8,128)(2,1)}), bf16[16,112,112]{2,1,0:T(8,128)(2,1)S(1)}, u32[]{:S(2)}, u32[]{:S(2)}) async-start(bf16[16,112,112]{2,1,0:T(8,128)(2,1)} %get-tuple-element.12), calls=%async_computation.2 | async-start | bytes 917504 | tf_op jit(solution)/shard_map/all_to_all | solution.py:121
Sparse Core Ops, SparseCore 0:
  10.8 56.0 all-gather.4
  68.9 55.7 all-gather.6
Sparse Core Ops, SparseCore 1:
  12.9 88.9 reduce-scatter.3

commit v10 on v9

--- a/solution.py
+++ b/solution.py
@@ -47,7 +47,7 @@
 
 
 def turn_kernel(x_ref, out_ref):
-    out_ref[...] = x_ref[...].astype(f32).T.astype(bf16)
+    out_ref[...] = x_ref[...].T
 
 
 def right_kernel(a_ref, right_ref, out_ref, x_ref, a_held, held, a_sem, sems, mix=lambda gradient: None):
@@ -71,13 +71,13 @@
 
 def moment_kernel(cols_ref, left_ref, out_ref, x_ref, held, sems):
     copies = fetch(left_ref, held, sems)
-    x_ref[...] = cols_ref[...].astype(f32).T.astype(bf16)
+    x_ref[...] = cols_ref[...].T
     product_into(out_ref, x_ref, copies, held)
 
 
 def middle_kernel(fix_ref, cols_ref, mom_ref, second_ref, left_ref, out_ref, rot_ref, x_ref, back_ref, held, sems):
     copies = fetch(left_ref, held, sems)
-    x_ref[...] = cols_ref[...].astype(f32).T.astype(bf16)
+    x_ref[...] = cols_ref[...].T
     product_into(rot_ref, x_ref, copies, held)
     rot_grad = rot_ref[...]
     rot_mom = beta_one * mom_ref[...] + (1.0 - beta_one) * rot_grad
@@ -96,8 +96,8 @@
     copies = fetch(right_ref, held, sems)
     columns = second_ref.shape[1]
     width = in_ref.shape[-1]
-    rows = in_ref[:, 1].reshape(columns, width).astype(f32).T.astype(bf16)
-    rot_grad = in_ref[:, 0].reshape(columns, width).astype(f32).T
+    rows = in_ref[:, 1].reshape(columns, width).T
+    rot_grad = in_ref[:, 0].reshape(columns, width).T.astype(f32)
     second_out[...] = beta_two * second_ref[...] + (1.0 - beta_two) * rot_grad * rot_grad
     for t, copy in enumerate(copies):
         copy.wait()

time: 183 us -> 183 us (level)
  no operation moved by 1% of the time
where the time goes in v10:
time: 183 us; the launch traced here: 181 us
  waiting for transfers between devices  85 us (46%)
  blocking collectives  28.7 us (16%)
  Pallas kernels  25.7 us (14%)
  starting transfers between devices  24.1 us (13%)
  between operations  16.3 us (9%)
    all_gather x1, waiting for transfers between devices, local(): right_full = lax.all_gather(right_basis[0], 'shard', axis=0, tiled=True)  45.8 us
    all_to_all x1, blocking collectives, swap(): lax.all_to_all(pieces, 'shard', split_axis=0, concat_axis=0, tiled=True)  28.7 us
    all_to_all x3, starting transfers between devices, swap(): lax.all_to_all(pieces, 'shard', split_axis=0, concat_axis=0, tiled=True)  24 us
    all_to_all x3, waiting for transfers between devices, swap(): lax.all_to_all(pieces, 'shard', split_axis=0, concat_axis=0, tiled=True)  23.7 us
    unnamed x4, waiting for transfers between devices  7.88 us
    all_gather x1, waiting for transfers between devices, local(): left_full = lax.all_gather(left_basis[0], 'shard', axis=0, tiled=True)  7.58 us
    pallas_call x1, Pallas kernels, local(): second_new, update = last(got, second[0], right_full)  6.33 us
    pallas_call x1, Pallas kernels, local(): middle(fixes, grad_cols.reshape(columns, rows), rot_mom_old, second_turne...  6.02 us
  transfers between devices with their start and end apart: 6, of which 5 were waited for; matrix products, arithmetic and copies ran while one was open for 0% of the time, Pallas kernels for 7%

profile of v10, /device:TPU:1, one launch (start us, length us, event | category | flops | bytes accessed | tf_op | source)
XLA Modules:
  0.0 180.9 jit_solution(13869777639046938284)
XLA Ops:
  8.0 0.0 all-gather.5.cloned.1.call-start
  8.1 0.7 all-gather.5.cloned.1.call-update
  8.8 0.0 reduce-scatter.4.cloned.1.call-start
  8.8 0.5 reduce-scatter.4.cloned.1.call-update
  9.3 0.0 all-gather.7.cloned.1.call-start
  9.4 0.7 all-gather.7.cloned.1.call-update
  10.1 1.1 shard_map.85
  11.2 10.0 %all-to-all-start = ((bf16[16,112,112]{2,1,0:T(8,128)(2,1)}), bf16[16,112,112]{2,1,0:T(8,128)(2,1)S(1)}, u32[]{:S(2)}, u32[]{:S(2)}) async-start(bf16[16,112,112]{2,1,0:T(8,128)(2,1)} %shard_map.85), calls=%async_computation | async-start | bytes 917504 | tf_op jit(solution)/shard_map/all_to_all | solution.py:121
  21.2 45.8 %all-gather.5.cloned.1.call-done = bf16[1,1792,1792]{2,1,0:T(8,128)(2,1)} async-done(((bf16[1,112,1792]{2,1,0:T(8,128)(2,1)}), bf16[1,1792,1792]{2,1,0:T(8,128)(2,1)}) %all-gather.5.cloned.1.call-update) | async-done | bytes 6422544 | tf_op jit(solution)/shard_map/all_gather | solution.py:138
  67.0 4.4 %shard_map.87 = bf16[16,112,112]{2,1,0:T(8,128)(2,1)} custom-call(bf16[112,1792]{1,0:T(8,128)(2,1)S(1)} %bitcast.18, bf16[1792,1792]{1,0:T(8,128)(2,1)} %bitcast.21), custom_call_target="tpu_custom_call" | custom-call | flops 719323136 | bytes 6422528 | tf_op jit(solution)/shard_map/pallas_call | solution.py:143
  71.4 5.1 %all-to-all-start.1 = ((bf16[16,112,112]{2,1,0:T(8,128)(2,1)}), bf16[16,112,112]{2,1,0:T(8,128)(2,1)S(1)}, u32[]{:S(2)}, u32[]{:S(2)}) async-start(bf16[16,112,112]{2,1,0:T(8,128)(2,1)} %shard_map.87), calls=%async_computation.1 | async-start | bytes 917504 | tf_op jit(solution)/shard_map/all_to_all | solution.py:121
  76.5 0.2 shard_map.86.second_ref
  76.7 19.3 %all-to-all-done.1 = bf16[16,112,112]{2,1,0:T(8,128)(2,1)S(1)} async-done(((bf16[16,112,112]{2,1,0:T(8,128)(2,1)}), bf16[16,112,112]{2,1,0:T(8,128)(2,1)S(1)}, u32[]{:S(2)}, u32[]{:S(2)}) %all-to-all-start.1) | async-done | bytes 401440 | tf_op jit(solution)/shard_map/all_to_all | solution.py:121
  96.0 6.0 %reduce-scatter.4.cloned.1.call-done = bf16[1,112,1792]{2,1,0:T(8,128)(2,1)} async-done(((bf16[16,112,1792]{2,1,0:T(8,128)(2,1)}), bf16[1,112,1792]{2,1,0:T(8,128)(2,1)}) %reduce-scatter.4.cloned.1.call-update) | async-done | bytes 401424
  101.9 1.0 copy-done.2
  102.9 4.5 %shard_map.88 = (bf16[16,112,112]{2,1,0:T(8,128)(2,1)}, bf16[112,1792]{1,0:T(8,128)(2,1)}) custom-call(bf16[112,1792]{1,0:T(8,128)(2,1)S(1)} %bitcast.20, bf16[1792,1792]{1,0:T(8,128)(2,1)} %bitcast.22, bf16[112,1792]{1,0:T(8,128)(2,1)S(1)} %bitcast.19), custom_call_target="tpu_custom_call" | custom-call | flops 719323136 | bytes 6422528 | tf_op jit(solution)/shard_map/pallas_call | solution.py:147
  107.4 8.9 %all-to-all-start.2 = ((bf16[16,112,112]{2,1,0:T(8,128)(2,1)}), bf16[16,112,112]{2,1,0:T(8,128)(2,1)S(1)}, u32[]{:S(2)}, u32[]{:S(2)}) async-start(bf16[16,112,112]{2,1,0:T(8,128)(2,1)} %get-tuple-element.12), calls=%async_computation.2 | async-start | bytes 917504 | tf_op jit(solution)/shard_map/all_to_all | solution.py:121
  117.0 0.1 maximum_divide_fusion.fix_ref
  117.1 7.6 %all-gather.7.cloned.1.call-done = bf16[1,1792,1792]{2,1,0:T(8,128)(2,1)} async-done(((bf16[1,112,1792]{2,1,0:T(8,128)(2,1)}), bf16[1,1792,1792]{2,1,0:T(8,128)(2,1)}) %all-gather.7.cloned.1.call-update) | async-done | bytes 6422544 | tf_op jit(solution)/shard_map/all_gather | solution.py:139
  124.7 3.2 %shard_map.89.mom_ref = f32[112,1792]{1,0:T(8,128)S(1)} custom-call(bf16[1792,112]{1,0:T(8,128)(2,1)S(1)} %bitcast.16, bf16[1792,1792]{1,0:T(8,128)(2,1)} %bitcast.24), custom_call_target="tpu_custom_call" | custom-call | flops 719323136 | bytes 6422528 | tf_op jit(solution)/shard_map/pallas_call | solution.py:150
  127.9 4.4 %all-to-all-done.2 = bf16[16,112,112]{2,1,0:T(8,128)(2,1)S(1)} async-done(((bf16[16,112,112]{2,1,0:T(8,128)(2,1)}), bf16[16,112,112]{2,1,0:T(8,128)(2,1)S(1)}, u32[]{:S(2)}, u32[]{:S(2)}) %all-to-all-start.2) | async-done | bytes 401440 | tf_op jit(solution)/shard_map/all_to_all | solution.py:121
  132.3 6.0 %shard_map.90 = bf16[16,2,112,112]{3,2,1,0:T(8,128)(2,1)S(1)} custom-call(f32[2]{0:T(128)S(1)} %maximum_divide_fusion.fix_ref, bf16[1792,112]{1,0:T(8,128)(2,1)S(1)} %bitcast.17, f32[112,1792]{1,0:T(8,128)S(1)} %shard_map.89.mom_ref, bf16[112,1792]{1,0:T(8,128)(2,1)S(1)} %shard_map.86.second_ref, bf16[1792,1792]{1,0:T(8,128)(2,1)} %bitcast.25), custom_call_target="tpu_custom_call" | custom-call | flops 1438646272 | bytes 6422528 | tf_op jit(solution)/shard_map/pallas_call | solution.py:157
  138.4 28.7 %all_to_all.20.in_ref = bf16[16,2,112,112]{3,2,1,0:T(8,128)(2,1)S(1)} all-to-all(bf16[16,2,112,112]{3,2,1,0:T(8,128)(2,1)S(1)} %shard_map.90), channel_id=1, replica_groups=mesh['dp'=16,'shard'=16] {'shard'}, dimensions={0} | all-to-all | bytes 1605632 | tf_op jit(solution)/shard_map/all_to_all | solution.py:121
  167.1 6.3 %shard_map.91 = (f32[112,1792]{1,0:T(8,128)}, bf16[112,1792]{1,0:T(8,128)(2,1)}) custom-call(bf16[16,2,112,112]{3,2,1,0:T(8,128)(2,1)S(1)} %all_to_all.20.in_ref, f32[112,1792]{1,0:T(8,128)S(1)} %bitcast.14, bf16[1792,1792]{1,0:T(8,128)(2,1)} %bitcast.23), custom_call_target="tpu_custom_call" | custom-call | flops 719323136 | bytes 6422528 | tf_op jit(solution)/shard_map/pallas_call | solution.py:161
  (6 shorter events, 0.0 us)
Async XLA Ops:
  8.0 2.1 %copy-start = (f32[1,112,1792]{2,1,0:T(8,128)S(1)}, f32[1,112,1792]{2,1,0:T(8,128)}, u32[]{:S(2)}) copy-start(f32[1,112,1792]{2,1,0:T(8,128)} %param.8) | copy-start | bytes 2408452
  8.0 59.0 %copy-start.1 = (bf16[1,112,1792]{2,1,0:T(8,128)(2,1)S(1)}, bf16[1,112,1792]{2,1,0:T(8,128)(2,1)}, u32[]{:S(2)}) copy-start(bf16[1,112,1792]{2,1,0:T(8,128)(2,1)} %param.7) | copy-start | bytes 1204228
  8.0 58.9 %all-gather.5.cloned.1.call-start = ((), (), s32[]{:S(2)}) async-start(), calls=%async_computation.5 | async-start | bytes 6823936 | tf_op jit(solution)/shard_map/all_gather | solution.py:138
  8.8 93.2 %reduce-scatter.4.cloned.1.call-start = ((), (), s32[]{:S(2)}) async-start(), calls=%async_computation.7 | async-start | bytes 6823936
  9.3 115.4 %all-gather.7.cloned.1.call-start = ((), (), s32[]{:S(2)}) async-start(), calls=%async_computation.6 | async-start | bytes 6823936 | tf_op jit(solution)/shard_map/all_gather | solution.py:139
  11.2 60.2 %all-to-all-start = ((bf16[16,112,112]{2,1,0:T(8,128)(2,1)}), bf16[16,112,112]{2,1,0:T(8,128)(2,1)S(1)}, u32[]{:S(2)}, u32[]{:S(2)}) async-start(bf16[16,112,112]{2,1,0:T(8,128)(2,1)} %shard_map.85), calls=%async_computation | async-start | bytes 917504 | tf_op jit(solution)/shard_map/all_to_all | solution.py:121
  71.4 24.6 %all-to-all-start.1 = ((bf16[16,112,112]{2,1,0:T(8,128)(2,1)}), bf16[16,112,112]{2,1,0:T(8,128)(2,1)S(1)}, u32[]{:S(2)}, u32[]{:S(2)}) async-start(bf16[16,112,112]{2,1,0:T(8,128)(2,1)} %shard_map.87), calls=%async_computation.1 | async-start | bytes 917504 | tf_op jit(solution)/shard_map/all_to_all | solution.py:121
  101.9 1.0 copy-start.2
  107.4 24.9 %all-to-all-start.2 = ((bf16[16,112,112]{2,1,0:T(8,128)(2,1)}), bf16[16,112,112]{2,1,0:T(8,128)(2,1)S(1)}, u32[]{:S(2)}, u32[]{:S(2)}) async-start(bf16[16,112,112]{2,1,0:T(8,128)(2,1)} %get-tuple-element.12), calls=%async_computation.2 | async-start | bytes 917504 | tf_op jit(solution)/shard_map/all_to_all | solution.py:121
Sparse Core Ops, SparseCore 0:
  10.8 56.0 all-gather.4
  68.9 55.7 all-gather.6
Sparse Core Ops, SparseCore 1:
  12.9 88.9 reduce-scatter.3
